TPU v7x, 128 devices: a whole 4x4x4 slice. The times are simulated.
128 devices in a mesh: blk: 32 (over x, z, core), layer: 4 (over y).
Axes of the slice: x: 4, y: 4, z: 4, core: 2. Of those that a mesh axis runs over, the one named last changes fastest.
Arguments:
- tile_values: bfloat16 [64, 4, 4, 128, 128], P('blk', 'layer'), may hold values from 0 to 10, as said below
- band_rows: int32 [64, 4, 4], P('blk', 'layer'), may hold values from 0 to 15, as said below
- kept_rows: int32 [64, 4, 4], P('blk', 'layer'), may hold values from 0 to 15, as said below
- prune_mask: int32 [64, 4, 128], P('blk'), may hold values 0 or 1
Outputs:
- kept: bfloat16 [64, 4, 4, 128, 128], P('blk', None, 'layer')
Inputs may be any that keep to these rules, and one draw needn't show every extreme that they name: `tile_values`: positive tile entries. `band_rows`: within each column panel and band the 4 block rows are distinct. `kept_rows`: within each column panel and band the 4 kept block rows are distinct.
All inputs are finite; a program needn't handle non-finite values. No bound on the sum of `prune_mask` on one device may be relied on, other than what follows from the above.
Results may differ from a plain program's by a relative error of at most 0.001.
Values may be sent and summed in bfloat16 or wider, within the bound.
No kernel may reach another device: no remote copies, remote signals or barrier semaphores. Data moves between devices by JAX's collectives and lax.ppermute only.
A program may use at most 192 MiB of HBM per device.

v0:
```python
import jax
import jax.numpy as jnp
from jax import lax
from jax.sharding import PartitionSpec as P


def densify(packed, positions, block_count):
    slot_ids = jnp.arange(block_count, dtype=jnp.int32)
    select = (positions[:, None, :] == slot_ids[None, :, None]).astype(jnp.bfloat16)
    dense = jnp.einsum("nrk,nkab->nrab", select, packed, preferred_element_type=jnp.float32)
    return dense.astype(jnp.bfloat16)


def per_device(tile_values, band_rows, kept_rows, prune_mask):
    panels = tile_values.shape[0]
    per_band = tile_values.shape[2]
    tile_size = tile_values.shape[3]
    band_count = lax.axis_size("layer")
    cycle_size = lax.axis_size("blk")
    panel_count = panels * cycle_size
    band_blocks = panel_count // band_count
    gathered, gathered_rows = (
        lax.all_gather(tile_values, "layer", axis=1, tiled=True),
        lax.all_gather(band_rows, "layer", axis=1, tiled=True),
    )
    right_dense = densify(
        gathered.reshape(panels * band_count, per_band, tile_size, tile_size),
        gathered_rows.reshape(panels * band_count, per_band),
        band_blocks,
    )
    right_side = (
        right_dense.reshape(panels, panel_count, tile_size, tile_size)
        .transpose(1, 2, 0, 3)
        .reshape(panel_count * tile_size, panels * tile_size)
    )
    own_tiles = tile_values[:, 0]
    own_rows = band_rows[:, 0]
    dense_own = densify(own_tiles, own_rows, band_blocks)
    dense_left = lax.all_gather(dense_own, "blk", axis=0, tiled=True)
    piece_count = dense_left.shape[0]
    operand = right_side
    operand = operand.reshape(piece_count, tile_size, panels * tile_size)
    left_blocks = dense_left.reshape(piece_count, band_blocks * tile_size, tile_size)
    expanded = lax.dot_general(
        left_blocks, operand, (((0, 2), (0, 1)), ((), ())), preferred_element_type=jnp.float32
    )
    squared = expanded * expanded
    partial_value = jnp.sum(squared, axis=0)
    totals = lax.psum(partial_value, "layer")
    row_count = panel_count * tile_size
    scaled = (squared * (row_count / totals)).astype(jnp.bfloat16)
    kept_count = kept_rows.shape[2]
    per_layer = kept_count // band_count
    gathered_rows_all, every_kept = (
        lax.all_gather(scaled, "layer", axis=0, tiled=True),
        lax.all_gather(kept_rows, "layer", axis=1, tiled=True),
    )
    blocked = gathered_rows_all.reshape(panel_count, tile_size, panels, tile_size)
    layer_index = lax.axis_index("layer")
    own_slots = lax.dynamic_slice_in_dim(every_kept, layer_index * per_layer, per_layer, 2)
    target = own_slots + (jnp.arange(band_count, dtype=jnp.int32) * band_blocks)[None, :, None]
    select = (
        target[..., None] == jnp.arange(panel_count, dtype=jnp.int32)[None, None, None, :]
    ).astype(jnp.bfloat16)
    picked = jnp.einsum(
        "jqmr,rajc->jqmac", select, blocked, preferred_element_type=jnp.float32
    ).astype(jnp.bfloat16)
    keep_mask = prune_mask[:, :, None, None, :].astype(jnp.bfloat16)
    return picked * keep_mask


def solution(mesh):
    return jax.shard_map(
        per_device,
        mesh=mesh,
        in_specs=(
            P("blk", "layer", None, None, None),
            P("blk", "layer", None),
            P("blk", "layer", None),
            P("blk", None, None),
        ),
        out_specs=P("blk", None, "layer", None, None),
        check_vma=False,
    )
```

profile of v0, /device:TPU:1, one launch (start us, length us, event | category | flops | bytes accessed | tf_op | source)
XLA Modules:
  0.0 246.9 jit_solution(17233081495594254588)
XLA Ops:
  6.5 0.0 copy-start.1
  6.5 0.0 all-gather.6.cloned.1.call-start
  6.5 0.7 all-gather.6.cloned.1.call-update
  7.3 0.0 all-gather.4.cloned.1.call-start
  7.3 1.6 convolution_convert_fusion.1
  8.9 1.2 copy.45
  10.2 0.0 all-gather.4.cloned.1.call-update
  10.2 0.0 all-gather.8.cloned.1.call-start
  10.2 0.0 copy-done.1
  10.3 8.8 %all_gather.17 = s32[2,4,4]{2,0,1:T(2,128)S(1)} all-gather(s32[2,1,4]{2,0,1:T(2,128)S(1)} %bitcast.43), channel_id=1, replica_groups=mesh['blk'=32,'layer'=4] {'layer'}, dimensions={1}, use_global_device_ids=true | all-gather | bytes 160 | tf_op jit(solution)/shard_map/all_gather | solution.py:24
  19.1 16.3 %all-gather.6.cloned.1.call-done = bf16[2,4,4,128,128]{4,3,2,1,0:T(8,128)(2,1)} async-done(((bf16[2,1,4,128,128]{4,3,2,1,0:T(8,128)(2,1)}), bf16[2,4,4,128,128]{4,3,2,1,0:T(8,128)(2,1)}) %all-gather.6.cloned.1.call-update) | async-done | bytes 1048592 | tf_op jit(solution)/shard_map/all_gather | solution.py:23
  35.3 2.0 copy.49
  37.4 2.2 convolution_convert_fusion
  39.6 3.1 %copy.50 = bf16[8,16,128,128]{3,2,1,0:T(8,128)(2,1)} copy(bf16[8,16,128,128]{3,1,2,0:T(8,128)(2,1)S(1)} %convolution_convert_fusion) | data formatting | bytes 8388608 | tf_op jit(solution)/shard_map/convert_element_type | solution.py:11
  42.7 6.4 %copy.51 = bf16[64,128,2,128]{1,3,2,0:T(8,128)(2,1)} copy(bf16[64,128,2,128]{3,1,0,2:T(8,128)(2,1)} %bitcast.37) | data formatting | bytes 8388608 | tf_op jit(solution)/shard_map/transpose | solution.py:33
  49.1 104.1 %all-gather.4.cloned.1.call-done = bf16[64,16,128,128]{3,2,1,0:T(8,128)(2,1)} async-done(((bf16[2,16,128,128]{3,2,1,0:T(8,128)(2,1)}), bf16[64,16,128,128]{3,2,1,0:T(8,128)(2,1)}) %all-gather.4.cloned.1.call-update) | async-done | bytes 33554448 | tf_op jit(solution)/shard_map/all_gather | solution.py:39
  153.2 16.0 %fusion.22 = (f32[256]{0:T(256)S(1)}, f32[2048,256]{1,0:T(8,128)S(1)}) fusion(bf16[64,2048,128]{2,1,0:T(8,128)(2,1)} %bitcast.45, bf16[64,128,256]{1,2,0:T(8,128)(2,1)} %bitcast.38), kind=kOutput, calls=%fused_computation.24 | convolution fusion | flops 8590983168 | bytes 39846912 | tf_op jit(solution)/shard_map/dot_general | solution.py:44
  169.2 0.0 copy-start.2
  169.3 0.0 copy-start
  169.3 8.5 %psum.7 = f32[256]{0:T(256)S(1)} all-reduce(f32[256]{0:T(256)S(1)} %get-tuple-element.5), channel_id=1, replica_groups=mesh['blk'=32,'layer'=4] {'layer'}, use_global_device_ids=true, to_apply=%region_1.0 | all-reduce | flops 256 | bytes 2048 | tf_op jit(solution)/shard_map/psum | solution.py:49
  177.7 1.1 multiply_convert_fusion
  178.9 0.0 all-gather.8.cloned.1.call-update
  178.9 0.0 copy-done.2
  178.9 5.2 %all_gather.15 = s32[2,4,4]{2,0,1:T(2,128)S(1)} all-gather(s32[2,1,4]{2,0,1:T(2,128)S(1)} %bitcast.44), channel_id=1, replica_groups=mesh['blk'=32,'layer'=4] {'layer'}, dimensions={1}, use_global_device_ids=true | all-gather | bytes 160 | tf_op jit(solution)/shard_map/all_gather | solution.py:56
  184.2 0.1 constant_dynamic-slice_fusion
  184.2 0.1 copy.61
  184.3 0.0 copy-done
  184.4 41.6 %all-gather.8.cloned.1.call-done = bf16[8192,256]{1,0:T(8,128)(2,1)} async-done(((bf16[2048,256]{1,0:T(8,128)(2,1)}), bf16[8192,256]{1,0:T(8,128)(2,1)}) %all-gather.8.cloned.1.call-update) | async-done | bytes 4194320 | tf_op jit(solution)/shard_map/all_gather | solution.py:55
  226.0 6.9 %reshape.36 = bf16[64,128,2,128]{3,2,1,0:T(2,128)(2,1)} reshape(bf16[8192,256]{1,0:T(8,128)(2,1)} %all-gather.8.cloned.1.call-done) | data formatting | bytes 8388608 | tf_op jit(solution)/shard_map/reshape | solution.py:58
  232.9 6.7 %fusion.9 = bf16[2,4,1,128,128]{4,1,3,0,2:T(4,128)(2,1)S(1)} fusion(bf16[64,128,2,128]{3,2,1,0:T(2,128)(2,1)} %reshape.36, bf16[2,4,128]{2,1,0:T(4,128)(2,1)S(1)} %convert_element_type.24, s32[2,4]{1,0:T(2,128)S(1)} %add_bitcast_fusion), kind=kOutput, calls=%fused_computation.9 | convolution fusion | flops 17039872 | bytes 4458528 | tf_op jit(solution)/shard_map/jqmr,rajc->jqmac/dot_general | solution.py:65
  239.7 0.7 copy.54
  (5 shorter events, 0.0 us)
Async XLA Ops:
  6.5 3.7 %copy-start.1 = (s32[2,1,4]{2,1,0:T(1,128)S(1)}, s32[2,1,4]{2,1,0:T(1,128)}, u32[]{:S(2)}) copy-start(s32[2,1,4]{2,1,0:T(1,128)} %param.5) | copy-start | bytes 100
  6.5 28.8 %all-gather.6.cloned.1.call-start = ((), (), s32[]{:S(2)}) async-start(), calls=%async_computation.1 | async-start | bytes 1310720 | tf_op jit(solution)/shard_map/all_gather | solution.py:23
  7.3 146.0 %all-gather.4.cloned.1.call-start = ((), (), s32[]{:S(2)}) async-start(), calls=%async_computation | async-start | bytes 34603008 | tf_op jit(solution)/shard_map/all_gather | solution.py:39
  10.2 215.8 %all-gather.8.cloned.1.call-start = ((), (), s32[]{:S(2)}) async-start(), calls=%async_computation.2 | async-start | bytes 5242880 | tf_op jit(solution)/shard_map/all_gather | solution.py:55
  169.2 9.7 %copy-start.2 = (s32[2,1,4]{2,1,0:T(1,128)S(1)}, s32[2,1,4]{2,1,0:T(1,128)}, u32[]{:S(2)}) copy-start(s32[2,1,4]{2,1,0:T(1,128)} %param.6) | copy-start | bytes 100
  169.3 15.1 %copy-start = (s32[2,4,128]{2,1,0:T(4,128)S(1)}, s32[2,4,128]{2,1,0:T(4,128)}, u32[]{:S(2)}) copy-start(s32[2,4,128]{2,1,0:T(4,128)} %param.7) | copy-start | bytes 12292
Sparse Core Ops, SparseCore 0:
  9.0 26.2 all-gather.5
  37.6 115.5 all-gather.3
  179.0 46.9 all-gather.7
where the time goes:
time: 247 us
  waiting for transfers between devices  163 us (66%)
  matrix products  26.5 us (11%)
  blocking collectives  22.5 us (9%)
  local copies, waits for them, and re-layouts  20.7 us (8%)
  between operations  13.2 us (5%)
    all_gather x1, waiting for transfers between devices, per_device(): dense_left = lax.all_gather(dense_own, 'blk', axis=0, tiled=True)  104 us
    all_gather x1, waiting for transfers between devices, per_device(): lax.all_gather(scaled, 'layer', axis=0, tiled=True)  41.6 us
    all_gather x1, waiting for transfers between devices, per_device(): lax.all_gather(tile_values, 'layer', axis=1, tiled=True)  16.3 us
    dot_general x1, matrix products, per_device(): lax.dot_general(left_blocks, operand, (((0, 2), (0, 1)), ((), ())), prefe...  16 us
    all_gather x1, blocking collectives, per_device(): lax.all_gather(band_rows, 'layer', axis=1, tiled=True)  8.8 us
    psum x1, blocking collectives, per_device(): totals = lax.psum(partial_value, 'layer')  8.46 us
    reshape x1, local copies, waits for them, and re-layouts, per_device(): gathered_rows_all.reshape(panel_count, tile_size, panels, tile_size)  6.95 us
    dot_general x1, matrix products, per_device(): jnp.einsum('jqmr,rajc->jqmac', select, blocked, preferred_element_type=jn...  6.72 us
  transfers between devices with their start and end apart: 3, of which 3 were waited for; matrix products, arithmetic and copies ran while one was open for 7% of the time, Pallas kernels for 0%

commit v1 on v0

v1 whole, which is shorter than its diff:
```python
import functools

import jax
import jax.numpy as jnp
from jax import lax
from jax.experimental import pallas as pl
from jax.experimental.pallas import tpu as pltpu
from jax.sharding import Mesh, PartitionSpec as P

TILE = 128
SLOTS = 4
PANELS = 2
BANDS = 4
BLOCKS = 16
COLUMNS = 64
BODY = PANELS * SLOTS * TILE
UNIT = BODY + 16
CHUNK = PANELS * TILE + 8
CELL = ("x", "z", "core")
VMEM = pl.BlockSpec(memory_space=pltpu.VMEM)
SMEM = pl.BlockSpec(memory_space=pltpu.SMEM)
LIMIT = pltpu.CompilerParams(vmem_limit_bytes=40 * 1024 * 1024)


def ring(shift):
    return [(i, (i + shift) % 4) for i in range(4)]


def cells(first, second):
    pairs = []
    for x in range(4):
        for z in range(4):
            for core, (dx, dz) in enumerate((first, second)):
                target = ((x + dx) % 4) * 4 + (z + dz) % 4
                pairs.append(((x * 4 + z) * 2 + core, target * 2 + core))
    return pairs


def pack_kernel(rows_ref, tiles_ref, unit_ref):
    band = lax.axis_index("layer")
    cell = (lax.axis_index("x") * 4 + lax.axis_index("z")) * 2 + lax.axis_index("core")
    unit_ref[:BODY] = tiles_ref[...].reshape(BODY, TILE)
    lane = lax.broadcasted_iota(jnp.int32, (16, TILE), 1)
    ids = jnp.zeros((16, TILE), jnp.int32)
    for j in range(PANELS):
        for k in range(SLOTS):
            ids = jnp.where(lane == 8 * j + k, rows_ref[j, 0, k] + BLOCKS * band, ids)
        ids = jnp.where(lane == 8 * j + 4, cell * PANELS + j, ids)
    unit_ref[BODY:] = ids.astype(jnp.float32).astype(jnp.bfloat16)


def expand_kernel(lefts, kept_ref, *refs):
    left_refs, right_refs = refs[:lefts], refs[lefts : lefts + BANDS]
    chunk_refs = refs[lefts + BANDS : lefts + 2 * BANDS]
    acc, right, wide, ids, where, sem = refs[lefts + 2 * BANDS :]
    band = lax.axis_index("layer")

    for a, ref in enumerate(left_refs):
        for u in range(4):
            row = ref[u * UNIT + BODY : (u + 1) * UNIT].astype(jnp.float32).astype(jnp.int32)
            wide[pl.ds(a * 4 + u, 1)] = row[:1]
    for b, ref in enumerate(right_refs):
        row = ref[BODY:].astype(jnp.float32).astype(jnp.int32)
        wide[pl.ds(lefts * 4 + b, 1)] = row[:1]
        for p in range(PANELS):
            right[p, pl.ds(b * SLOTS, SLOTS)] = ref[p * SLOTS * TILE : (p + 1) * SLOTS * TILE].reshape(SLOTS, TILE, TILE)
    copy = pltpu.make_async_copy(wide, ids, sem)
    copy.start()
    acc[...] = jnp.zeros_like(acc)
    copy.wait()

    for p in range(PANELS):
        for j in range(COLUMNS):
            where[p, j] = -1
    for p in range(PANELS):
        for b in range(BANDS):
            for k in range(SLOTS):
                where[p, ids[lefts * 4 + b, 8 * p + k]] = b * SLOTS + k

    for a, ref in enumerate(left_refs):

        def step(i, carry, a=a, ref=ref):
            unit = a * 4 + i // PANELS
            j = lax.rem(i, PANELS)
            column = ids[unit, 8 * j + 4]
            start = pl.multiple_of((i // PANELS) * UNIT + j * SLOTS * TILE, 16)
            for p in range(PANELS):
                slot = where[p, column]

                @pl.when(slot >= 0)
                def _():
                    product = jnp.dot(
                        ref[pl.ds(start, SLOTS * TILE)], right[p, slot], preferred_element_type=jnp.float32
                    )
                    for k in range(SLOTS):
                        block = ids[unit, 8 * j + k] - BLOCKS * band
                        acc[p, block] += product[k * TILE : (k + 1) * TILE]

            return carry

        lax.fori_loop(0, 4 * PANELS, step, 0)

    for p in range(PANELS):

        def add(r, total):
            value = acc[p, r]
            return total + jnp.sum((value * value).reshape(TILE // 8, 8, TILE), axis=0)

        total = lax.fori_loop(0, BLOCKS, add, jnp.zeros((8, TILE), jnp.float32))
        total = jnp.sum(total, axis=0, keepdims=True)
        for s in range(BANDS):
            slot = lax.rem(band + s, BANDS)
            value = acc[p, kept_ref[p, 0, slot]]
            chunk_refs[s][p * TILE : (p + 1) * TILE] = value * value
            chunk_refs[s][PANELS * TILE + 4 * p : PANELS * TILE + 4 * p + 4] = jnp.broadcast_to(total, (4, TILE))


def finish_kernel(mask_ref, *refs):
    chunk_refs, out_ref = refs[:BANDS], refs[BANDS]
    band = lax.axis_index("layer")
    for p in range(PANELS):
        row = PANELS * TILE + 4 * p
        total = sum(ref[row : row + 1] for ref in chunk_refs)
        scale = (COLUMNS * TILE) / total
        for s in range(BANDS):
            source = lax.rem(band - s + BANDS, BANDS)
            keep = mask_ref[p, pl.ds(source, 1)].astype(jnp.float32).astype(jnp.bfloat16)
            value = (chunk_refs[s][p * TILE : (p + 1) * TILE] * scale).astype(jnp.bfloat16)
            out_ref[p, source, 0] = value * keep


def per_device(tile_values, band_rows, kept_rows, prune_mask):
    unit = pl.pallas_call(
        pack_kernel,
        out_shape=jax.ShapeDtypeStruct((UNIT, TILE), jnp.bfloat16),
        in_specs=[SMEM, VMEM],
        out_specs=VMEM,
        compiler_params=LIMIT,
    )(band_rows, tile_values)

    lines = [lax.ppermute(unit, CELL, cells(a, b)) for a, b in (((1, 0), (0, 1)), ((3, 0), (0, 3)), ((2, 0), (0, 2)))]
    line = jnp.concatenate([unit, *lines], axis=0)
    rights = [unit] + [lax.ppermute(unit, "layer", ring(s)) for s in (1, 3, 2)]
    rest = [lax.ppermute(line, CELL, cells(a, b)) for a, b in (((0, 1), (1, 0)), ((0, 3), (3, 0)), ((0, 2), (2, 0)))]
    lefts = [line, *rest]
    lefts = lefts + [lax.ppermute(one, "core", [(0, 1), (1, 0)]) for one in lefts]

    count = len(lefts)
    ids = count * 4 + 8
    chunks = pl.pallas_call(
        functools.partial(expand_kernel, count),
        out_shape=[jax.ShapeDtypeStruct((CHUNK, TILE), jnp.float32)] * BANDS,
        in_specs=[SMEM] + [VMEM] * (count + BANDS),
        out_specs=[VMEM] * BANDS,
        scratch_shapes=[
            pltpu.VMEM((PANELS, BLOCKS, TILE, TILE), jnp.float32),
            pltpu.VMEM((PANELS, BANDS * SLOTS, TILE, TILE), jnp.bfloat16),
            pltpu.VMEM((ids, TILE), jnp.int32),
            pltpu.SMEM((ids, TILE), jnp.int32),
            pltpu.SMEM((PANELS, COLUMNS), jnp.int32),
            pltpu.SemaphoreType.DMA,
        ],
        compiler_params=LIMIT,
        cost_estimate=pl.CostEstimate(flops=2**29, bytes_accessed=10 * 2**20, transcendentals=0),
    )(kept_rows, *lefts, *rights)

    chunks = [chunks[0]] + [lax.ppermute(chunks[s], "layer", ring(s)) for s in (1, 2, 3)]
    return pl.pallas_call(
        finish_kernel,
        out_shape=jax.ShapeDtypeStruct((PANELS, BANDS, 1, TILE, TILE), jnp.bfloat16),
        in_specs=[VMEM] * (1 + BANDS),
        out_specs=VMEM,
        compiler_params=LIMIT,
    )(prune_mask, *chunks)


def solution(mesh):
    parts = Mesh(mesh.devices.reshape(4, 4, 2, 4), CELL + ("layer",))
    return jax.shard_map(
        per_device,
        mesh=parts,
        in_specs=(
            P(CELL, "layer", None, None, None),
            P(CELL, "layer", None),
            P(CELL, "layer", None),
            P(CELL, None, None),
        ),
        out_specs=P(CELL, None, "layer", None, None),
        check_vma=False,
    )
```

time: 247 us -> 90.5 us (0.37)
  the two profiles are of different devices: /device:TPU:1 before, /device:TPU:32 now
where the time goes in v1:
time: 90.5 us; the launch traced here: 90.4 us
  waiting for transfers between devices  56 us (62%)
  starting transfers between devices  20.9 us (23%)
  Pallas kernels  11.7 us (13%)
  local copies, waits for them, and re-layouts  1.64 us (2%)
    ppermute x3, waiting for transfers between devices, per_device(): lax.ppermute(line, CELL, cells(a, b))  23.4 us
    ppermute x3, waiting for transfers between devices, per_device(): rights = [unit] + [lax.ppermute(unit, 'layer', ring(s)) for s in (1, 3, 2)]  20.7 us
    pallas_call x1, Pallas kernels, per_device(): pl.pallas_call(functools.partial(expand_kernel, count), out_shape=[jax.Sh...  10.4 us
    ppermute x3, starting transfers between devices, per_device(): rights = [unit] + [lax.ppermute(unit, 'layer', ring(s)) for s in (1, 3, 2)]  7.25 us
    ppermute x3, waiting for transfers between devices, per_device(): lax.ppermute(unit, CELL, cells(a, b))  6.74 us
    ppermute x3, waiting for transfers between devices, per_device(): lax.ppermute(chunks[s], 'layer', ring(s))  5.21 us
    ppermute x3, starting transfers between devices, per_device(): lax.ppermute(unit, CELL, cells(a, b))  5.13 us
    ppermute x3, starting transfers between devices, per_device(): lax.ppermute(line, CELL, cells(a, b))  5.08 us
  transfers between devices with their start and end apart: 16, of which 11 were waited for; matrix products, arithmetic and copies ran while one was open for 0% of the time, Pallas kernels for 0%

profile of v1, /device:TPU:32, one launch (start us, length us, event | category | flops | bytes accessed | tf_op | source)
XLA Modules:
  0.0 90.4 jit_solution(12652388218429389736)
XLA Ops:
  0.0 0.0 copy-start
  0.0 0.9 %copy-done = bf16[2,1,4,128,128]{4,3,2,1,0:T(8,128)(2,1)S(1)} copy-done((bf16[2,1,4,128,128]{4,3,2,1,0:T(8,128)(2,1)S(1)}, bf16[2,1,4,128,128]{4,3,2,1,0:T(8,128)(2,1)}, u32[]{:S(2)}) %copy-start) | copy-done | bytes 262168
  1.0 0.0 copy-start.2
  1.0 0.7 copy-done.2
  1.6 0.6 shard_map.46.refs_8_
  2.2 0.0 copy-start.3
  2.2 3.1 %collective-permute-start.2 = (bf16[1040,128]{1,0:T(8,128)(2,1)S(1)}, bf16[1040,128]{1,0:T(8,128)(2,1)S(1)}, u32[]{:S(2)}, u32[]{:S(2)}) collective-permute-start(bf16[1040,128]{1,0:T(8,128)(2,1)S(1)} %shard_map.46.refs_8_), channel_id=1, source_target_pairs={{0,64},{4,20},{8,72},{12,28},{16,80},{20,4},{24,88},{28,12},{32,96... | collective-permute-start | bytes 798728 | tf_op jit(solution)/shard_map/ppermute | solution.py:141
  5.3 1.1 %collective-permute-start.1 = (bf16[1040,128]{1,0:T(8,128)(2,1)S(1)}, bf16[1040,128]{1,0:T(8,128)(2,1)S(1)}, u32[]{:S(2)}, u32[]{:S(2)}) collective-permute-start(bf16[1040,128]{1,0:T(8,128)(2,1)S(1)} %shard_map.46.refs_8_), channel_id=1, source_target_pairs={{0,96},{4,28},{8,104},{12,4},{16,112},{20,12},{24,120},{28,20},{32... | collective-permute-start | bytes 798728 | tf_op jit(solution)/shard_map/ppermute | solution.py:141
  6.5 0.9 collective-permute-start
  7.4 2.9 %collective-permute-done.2 = bf16[1040,128]{1,0:T(8,128)(2,1)S(1)} collective-permute-done((bf16[1040,128]{1,0:T(8,128)(2,1)S(1)}, bf16[1040,128]{1,0:T(8,128)(2,1)S(1)}, u32[]{:S(2)}, u32[]{:S(2)}) %collective-permute-start.2) | collective-permute-done | bytes 266272 | tf_op jit(solution)/shard_map/ppermute | solution.py:141
  10.2 3.0 %collective-permute-done.1 = bf16[1040,128]{1,0:T(8,128)(2,1)S(1)} collective-permute-done((bf16[1040,128]{1,0:T(8,128)(2,1)S(1)}, bf16[1040,128]{1,0:T(8,128)(2,1)S(1)}, u32[]{:S(2)}, u32[]{:S(2)}) %collective-permute-start.1) | collective-permute-done | bytes 266272 | tf_op jit(solution)/shard_map/ppermute | solution.py:141
  13.2 0.9 %collective-permute-done = bf16[1040,128]{1,0:T(8,128)(2,1)S(1)} collective-permute-done((bf16[1040,128]{1,0:T(8,128)(2,1)S(1)}, bf16[1040,128]{1,0:T(8,128)(2,1)S(1)}, u32[]{:S(2)}, u32[]{:S(2)}) %collective-permute-start) | collective-permute-done | bytes 266272 | tf_op jit(solution)/shard_map/ppermute | solution.py:141
  14.1 0.1 pad_maximum_fusion.refs_0_
  14.2 0.0 copy-start.1
  14.2 3.1 %collective-permute-start.5 = (bf16[4160,128]{1,0:T(8,128)(2,1)S(1)}, bf16[4160,128]{1,0:T(8,128)(2,1)S(1)}, u32[]{:S(2)}, u32[]{:S(2)}) collective-permute-start(bf16[4160,128]{1,0:T(8,128)(2,1)S(1)} %pad_maximum_fusion.refs_0_), channel_id=1, source_target_pairs={{0,16},{4,68},{8,24},{12,76},{16,0},{20,84},{24,8},{28,92},{32,48}... | collective-permute-start | bytes 3194888 | tf_op jit(solution)/shard_map/ppermute | solution.py:144
  17.2 1.0 %collective-permute-start.4 = (bf16[4160,128]{1,0:T(8,128)(2,1)S(1)}, bf16[4160,128]{1,0:T(8,128)(2,1)S(1)}, u32[]{:S(2)}, u32[]{:S(2)}) collective-permute-start(bf16[4160,128]{1,0:T(8,128)(2,1)S(1)} %pad_maximum_fusion.refs_0_), channel_id=1, source_target_pairs={{0,24},{4,100},{8,0},{12,108},{16,8},{20,116},{24,16},{28,124},{32... | collective-permute-start | bytes 3194888 | tf_op jit(solution)/shard_map/ppermute | solution.py:144
  18.2 1.0 %collective-permute-start.3 = (bf16[4160,128]{1,0:T(8,128)(2,1)S(1)}, bf16[4160,128]{1,0:T(8,128)(2,1)S(1)}, u32[]{:S(2)}, u32[]{:S(2)}) collective-permute-start(bf16[4160,128]{1,0:T(8,128)(2,1)S(1)} %pad_maximum_fusion.refs_0_), channel_id=1, source_target_pairs={{0,8},{4,36},{8,16},{12,44},{16,24},{20,52},{24,0},{28,60},{32,40}... | collective-permute-start | bytes 3194888 | tf_op jit(solution)/shard_map/ppermute | solution.py:144
  19.3 0.0 collective-permute-start.6
  19.3 11.6 %collective-permute-done.5.refs_3_ = bf16[4160,128]{1,0:T(8,128)(2,1)S(1)} collective-permute-done((bf16[4160,128]{1,0:T(8,128)(2,1)S(1)}, bf16[4160,128]{1,0:T(8,128)(2,1)S(1)}, u32[]{:S(2)}, u32[]{:S(2)}) %collective-permute-start.5) | collective-permute-done | bytes 1064992 | tf_op jit(solution)/shard_map/ppermute | solution.py:144
  30.8 0.0 collective-permute-start.9
  30.8 11.3 %collective-permute-done.4.refs_2_ = bf16[4160,128]{1,0:T(8,128)(2,1)S(1)} collective-permute-done((bf16[4160,128]{1,0:T(8,128)(2,1)S(1)}, bf16[4160,128]{1,0:T(8,128)(2,1)S(1)}, u32[]{:S(2)}, u32[]{:S(2)}) %collective-permute-start.4) | collective-permute-done | bytes 1064992 | tf_op jit(solution)/shard_map/ppermute | solution.py:144
  42.1 0.0 collective-permute-start.8
  42.2 0.5 collective-permute-done.3.refs_1_
  42.6 0.0 collective-permute-start.7
  42.7 3.2 %collective-permute-start.12 = (bf16[1040,128]{1,0:T(8,128)(2,1)S(1)}, bf16[1040,128]{1,0:T(8,128)(2,1)S(1)}, u32[]{:S(2)}, u32[]{:S(2)}) collective-permute-start(bf16[1040,128]{1,0:T(8,128)(2,1)S(1)} %shard_map.46.refs_8_), channel_id=1, source_target_pairs={{0,2},{1,3},{2,0},{3,1},{4,6},{5,7},{6,4},{7,5},{8,10},{9,11},{10,... | collective-permute-start | bytes 798728 | tf_op jit(solution)/shard_map/ppermute | solution.py:143
  45.9 7.1 %collective-permute-done.12.refs_11_ = bf16[1040,128]{1,0:T(8,128)(2,1)S(1)} collective-permute-done((bf16[1040,128]{1,0:T(8,128)(2,1)S(1)}, bf16[1040,128]{1,0:T(8,128)(2,1)S(1)}, u32[]{:S(2)}, u32[]{:S(2)}) %collective-permute-start.12) | collective-permute-done | bytes 266272 | tf_op jit(solution)/shard_map/ppermute | solution.py:143
  53.0 3.0 %collective-permute-start.11 = (bf16[1040,128]{1,0:T(8,128)(2,1)S(1)}, bf16[1040,128]{1,0:T(8,128)(2,1)S(1)}, u32[]{:S(2)}, u32[]{:S(2)}) collective-permute-start(bf16[1040,128]{1,0:T(8,128)(2,1)S(1)} %shard_map.46.refs_8_), channel_id=1, source_target_pairs={{0,3},{1,0},{2,1},{3,2},{4,7},{5,4},{6,5},{7,6},{8,11},{9,8},{10,9... | collective-permute-start | bytes 798728 | tf_op jit(solution)/shard_map/ppermute | solution.py:143
  56.0 5.5 %collective-permute-done.11.refs_10_ = bf16[1040,128]{1,0:T(8,128)(2,1)S(1)} collective-permute-done((bf16[1040,128]{1,0:T(8,128)(2,1)S(1)}, bf16[1040,128]{1,0:T(8,128)(2,1)S(1)}, u32[]{:S(2)}, u32[]{:S(2)}) %collective-permute-start.11) | collective-permute-done | bytes 266272 | tf_op jit(solution)/shard_map/ppermute | solution.py:143
  61.5 1.0 %collective-permute-start.10 = (bf16[1040,128]{1,0:T(8,128)(2,1)S(1)}, bf16[1040,128]{1,0:T(8,128)(2,1)S(1)}, u32[]{:S(2)}, u32[]{:S(2)}) collective-permute-start(bf16[1040,128]{1,0:T(8,128)(2,1)S(1)} %shard_map.46.refs_8_), channel_id=1, source_target_pairs={{0,1},{1,2},{2,3},{3,0},{4,5},{5,6},{6,7},{7,4},{8,9},{9,10},{10,1... | collective-permute-start | bytes 798728 | tf_op jit(solution)/shard_map/ppermute | solution.py:143
  62.6 8.0 %collective-permute-done.10.refs_9_ = bf16[1040,128]{1,0:T(8,128)(2,1)S(1)} collective-permute-done((bf16[1040,128]{1,0:T(8,128)(2,1)S(1)}, bf16[1040,128]{1,0:T(8,128)(2,1)S(1)}, u32[]{:S(2)}, u32[]{:S(2)}) %collective-permute-start.10) | collective-permute-done | bytes 266272 | tf_op jit(solution)/shard_map/ppermute | solution.py:143
  70.6 0.0 collective-permute-done.6.refs_4_
  70.6 0.0 collective-permute-done.9.refs_7_
  70.6 0.0 collective-permute-done.8.refs_6_
  70.6 0.0 collective-permute-done.7.refs_5_
  70.6 0.0 copy-done.3
  70.6 10.4 %shard_map.47 = (f32[264,128]{1,0:T(8,128)S(1)}, f32[264,128]{1,0:T(8,128)S(1)}, f32[264,128]{1,0:T(8,128)S(1)}, f32[264,128]{1,0:T(8,128)S(1)}) custom-call(s32[2,1,4]{2,1,0:T(1,128)S(1)} %copy-done.3, bf16[4160,128]{1,0:T(8,128)(2,1)S(1)} %pad_maximum_fusion.refs_0_, bf16[4160,128]{1,0:T(8,128)(2,1)S(1)} %collective-permute-done.3.refs_1_, ...), custom_call_target="tpu_custom_call" | custom-call | flops 536870912 | bytes 10485760 | tf_op jit(solution)/shard_map/pallas_call | solution.py:150
  81.0 0.1 collective-permute-start.13
  81.1 3.2 %collective-permute-start.14 = (f32[264,128]{1,0:T(8,128)S(1)}, f32[264,128]{1,0:T(8,128)S(1)}, u32[]{:S(2)}, u32[]{:S(2)}) collective-permute-start(f32[264,128]{1,0:T(8,128)S(1)} %get-tuple-element.11), channel_id=1, source_target_pairs={{0,2},{1,3},{2,0},{3,1},{4,6},{5,7},{6,4},{7,5},{8,10},{9,11},{10,... | collective-permute-start | bytes 405512 | tf_op jit(solution)/shard_map/ppermute | solution.py:167
  84.3 0.2 collective-permute-start.15
  84.4 4.4 %collective-permute-done.13.refs_1_ = f32[264,128]{1,0:T(8,128)S(1)} collective-permute-done((f32[264,128]{1,0:T(8,128)S(1)}, f32[264,128]{1,0:T(8,128)S(1)}, u32[]{:S(2)}, u32[]{:S(2)}) %collective-permute-start.13) | collective-permute-done | bytes 135200 | tf_op jit(solution)/shard_map/ppermute | solution.py:167
  88.8 0.0 collective-permute-done.14.refs_2_
  88.8 0.8 collective-permute-done.15.refs_3_
  89.6 0.0 copy-done.1
  89.6 0.8 shard_map.48
Async XLA Ops:
  0.0 0.9 %copy-start = (bf16[2,1,4,128,128]{4,3,2,1,0:T(8,128)(2,1)S(1)}, bf16[2,1,4,128,128]{4,3,2,1,0:T(8,128)(2,1)}, u32[]{:S(2)}) copy-start(bf16[2,1,4,128,128]{4,3,2,1,0:T(8,128)(2,1)} %tiles_ref.1) | copy-start | bytes 786436
  1.0 0.7 copy-start.2
  2.2 68.4 %copy-start.3 = (s32[2,1,4]{2,1,0:T(1,128)S(1)}, s32[2,1,4]{2,1,0:T(1,128)}, u32[]{:S(2)}) copy-start(s32[2,1,4]{2,1,0:T(1,128)} %kept_ref.1) | copy-start | bytes 100
  2.2 8.0 %collective-permute-start.2 = (bf16[1040,128]{1,0:T(8,128)(2,1)S(1)}, bf16[1040,128]{1,0:T(8,128)(2,1)S(1)}, u32[]{:S(2)}, u32[]{:S(2)}) collective-permute-start(bf16[1040,128]{1,0:T(8,128)(2,1)S(1)} %shard_map.46.refs_8_), channel_id=1, source_target_pairs={{0,64},{4,20},{8,72},{12,28},{16,80},{20,4},{24,88},{28,12},{32,96... | collective-permute-start | bytes 798728 | tf_op jit(solution)/shard_map/ppermute | solution.py:141
  5.3 7.9 %collective-permute-start.1 = (bf16[1040,128]{1,0:T(8,128)(2,1)S(1)}, bf16[1040,128]{1,0:T(8,128)(2,1)S(1)}, u32[]{:S(2)}, u32[]{:S(2)}) collective-permute-start(bf16[1040,128]{1,0:T(8,128)(2,1)S(1)} %shard_map.46.refs_8_), channel_id=1, source_target_pairs={{0,96},{4,28},{8,104},{12,4},{16,112},{20,12},{24,120},{28,20},{32... | collective-permute-start | bytes 798728 | tf_op jit(solution)/shard_map/ppermute | solution.py:141
  6.5 7.6 %collective-permute-start = (bf16[1040,128]{1,0:T(8,128)(2,1)S(1)}, bf16[1040,128]{1,0:T(8,128)(2,1)S(1)}, u32[]{:S(2)}, u32[]{:S(2)}) collective-permute-start(bf16[1040,128]{1,0:T(8,128)(2,1)S(1)} %shard_map.46.refs_8_), channel_id=1, source_target_pairs={{0,32},{4,12},{8,40},{12,20},{16,48},{20,28},{24,56},{28,4},{32,64... | collective-permute-start | bytes 798728 | tf_op jit(solution)/shard_map/ppermute | solution.py:141
  14.2 75.5 %copy-start.1 = (s32[2,4,128]{2,1,0:T(4,128)S(1)}, s32[2,4,128]{2,1,0:T(4,128)}, u32[]{:S(2)}) copy-start(s32[2,4,128]{2,1,0:T(4,128)} %mask_ref.1) | copy-start | bytes 12292
  14.2 16.7 %collective-permute-start.5 = (bf16[4160,128]{1,0:T(8,128)(2,1)S(1)}, bf16[4160,128]{1,0:T(8,128)(2,1)S(1)}, u32[]{:S(2)}, u32[]{:S(2)}) collective-permute-start(bf16[4160,128]{1,0:T(8,128)(2,1)S(1)} %pad_maximum_fusion.refs_0_), channel_id=1, source_target_pairs={{0,16},{4,68},{8,24},{12,76},{16,0},{20,84},{24,8},{28,92},{32,48}... | collective-permute-start | bytes 3194888 | tf_op jit(solution)/shard_map/ppermute | solution.py:144
  17.2 24.9 %collective-permute-start.4 = (bf16[4160,128]{1,0:T(8,128)(2,1)S(1)}, bf16[4160,128]{1,0:T(8,128)(2,1)S(1)}, u32[]{:S(2)}, u32[]{:S(2)}) collective-permute-start(bf16[4160,128]{1,0:T(8,128)(2,1)S(1)} %pad_maximum_fusion.refs_0_), channel_id=1, source_target_pairs={{0,24},{4,100},{8,0},{12,108},{16,8},{20,116},{24,16},{28,124},{32... | collective-permute-start | bytes 3194888 | tf_op jit(solution)/shard_map/ppermute | solution.py:144
  18.2 24.4 %collective-permute-start.3 = (bf16[4160,128]{1,0:T(8,128)(2,1)S(1)}, bf16[4160,128]{1,0:T(8,128)(2,1)S(1)}, u32[]{:S(2)}, u32[]{:S(2)}) collective-permute-start(bf16[4160,128]{1,0:T(8,128)(2,1)S(1)} %pad_maximum_fusion.refs_0_), channel_id=1, source_target_pairs={{0,8},{4,36},{8,16},{12,44},{16,24},{20,52},{24,0},{28,60},{32,40}... | collective-permute-start | bytes 3194888 | tf_op jit(solution)/shard_map/ppermute | solution.py:144
  19.3 51.3 %collective-permute-start.6 = (bf16[4160,128]{1,0:T(8,128)(2,1)S(1)}, bf16[4160,128]{1,0:T(8,128)(2,1)S(1)}, u32[]{:S(2)}, u32[]{:S(2)}) collective-permute-start(bf16[4160,128]{1,0:T(8,128)(2,1)S(1)} %pad_maximum_fusion.refs_0_), channel_id=1, source_target_pairs={{0,4},{4,0},{1,5},{5,1},{2,6},{6,2},{3,7},{7,3},{8,12},{12,8},{9,1... | collective-permute-start | bytes 3194888 | tf_op jit(solution)/shard_map/ppermute | solution.py:146
  30.8 39.7 %collective-permute-start.9 = (bf16[4160,128]{1,0:T(8,128)(2,1)S(1)}, bf16[4160,128]{1,0:T(8,128)(2,1)S(1)}, u32[]{:S(2)}, u32[]{:S(2)}) collective-permute-start(bf16[4160,128]{1,0:T(8,128)(2,1)S(1)} %collective-permute-done.5.refs_3_), channel_id=1, source_target_pairs={{0,4},{4,0},{1,5},{5,1},{2,6},{6,2},{3,7},{7,3},{8,12},{12,8},{9,1... | collective-permute-start | bytes 3194888 | tf_op jit(solution)/shard_map/ppermute | solution.py:146
  42.1 28.4 %collective-permute-start.8 = (bf16[4160,128]{1,0:T(8,128)(2,1)S(1)}, bf16[4160,128]{1,0:T(8,128)(2,1)S(1)}, u32[]{:S(2)}, u32[]{:S(2)}) collective-permute-start(bf16[4160,128]{1,0:T(8,128)(2,1)S(1)} %collective-permute-done.4.refs_2_), channel_id=1, source_target_pairs={{0,4},{4,0},{1,5},{5,1},{2,6},{6,2},{3,7},{7,3},{8,12},{12,8},{9,1... | collective-permute-start | bytes 3194888 | tf_op jit(solution)/shard_map/ppermute | solution.py:146
  42.6 28.0 %collective-permute-start.7 = (bf16[4160,128]{1,0:T(8,128)(2,1)S(1)}, bf16[4160,128]{1,0:T(8,128)(2,1)S(1)}, u32[]{:S(2)}, u32[]{:S(2)}) collective-permute-start(bf16[4160,128]{1,0:T(8,128)(2,1)S(1)} %collective-permute-done.3.refs_1_), channel_id=1, source_target_pairs={{0,4},{4,0},{1,5},{5,1},{2,6},{6,2},{3,7},{7,3},{8,12},{12,8},{9,1... | collective-permute-start | bytes 3194888 | tf_op jit(solution)/shard_map/ppermute | solution.py:146
  42.7 10.3 %collective-permute-start.12 = (bf16[1040,128]{1,0:T(8,128)(2,1)S(1)}, bf16[1040,128]{1,0:T(8,128)(2,1)S(1)}, u32[]{:S(2)}, u32[]{:S(2)}) collective-permute-start(bf16[1040,128]{1,0:T(8,128)(2,1)S(1)} %shard_map.46.refs_8_), channel_id=1, source_target_pairs={{0,2},{1,3},{2,0},{3,1},{4,6},{5,7},{6,4},{7,5},{8,10},{9,11},{10,... | collective-permute-start | bytes 798728 | tf_op jit(solution)/shard_map/ppermute | solution.py:143
  53.0 8.5 %collective-permute-start.11 = (bf16[1040,128]{1,0:T(8,128)(2,1)S(1)}, bf16[1040,128]{1,0:T(8,128)(2,1)S(1)}, u32[]{:S(2)}, u32[]{:S(2)}) collective-permute-start(bf16[1040,128]{1,0:T(8,128)(2,1)S(1)} %shard_map.46.refs_8_), channel_id=1, source_target_pairs={{0,3},{1,0},{2,1},{3,2},{4,7},{5,4},{6,5},{7,6},{8,11},{9,8},{10,9... | collective-permute-start | bytes 798728 | tf_op jit(solution)/shard_map/ppermute | solution.py:143
  61.5 9.1 %collective-permute-start.10 = (bf16[1040,128]{1,0:T(8,128)(2,1)S(1)}, bf16[1040,128]{1,0:T(8,128)(2,1)S(1)}, u32[]{:S(2)}, u32[]{:S(2)}) collective-permute-start(bf16[1040,128]{1,0:T(8,128)(2,1)S(1)} %shard_map.46.refs_8_), channel_id=1, source_target_pairs={{0,1},{1,2},{2,3},{3,0},{4,5},{5,6},{6,7},{7,4},{8,9},{9,10},{10,1... | collective-permute-start | bytes 798728 | tf_op jit(solution)/shard_map/ppermute | solution.py:143
  81.0 7.8 %collective-permute-start.13 = (f32[264,128]{1,0:T(8,128)S(1)}, f32[264,128]{1,0:T(8,128)S(1)}, u32[]{:S(2)}, u32[]{:S(2)}) collective-permute-start(f32[264,128]{1,0:T(8,128)S(1)} %get-tuple-element.10), channel_id=1, source_target_pairs={{0,1},{1,2},{2,3},{3,0},{4,5},{5,6},{6,7},{7,4},{8,9},{9,10},{10,1... | collective-permute-start | bytes 405512 | tf_op jit(solution)/shard_map/ppermute | solution.py:167
  81.1 7.8 %collective-permute-start.14 = (f32[264,128]{1,0:T(8,128)S(1)}, f32[264,128]{1,0:T(8,128)S(1)}, u32[]{:S(2)}, u32[]{:S(2)}) collective-permute-start(f32[264,128]{1,0:T(8,128)S(1)} %get-tuple-element.11), channel_id=1, source_target_pairs={{0,2},{1,3},{2,0},{3,1},{4,6},{5,7},{6,4},{7,5},{8,10},{9,11},{10,... | collective-permute-start | bytes 405512 | tf_op jit(solution)/shard_map/ppermute | solution.py:167
  84.3 5.4 %collective-permute-start.15 = (f32[264,128]{1,0:T(8,128)S(1)}, f32[264,128]{1,0:T(8,128)S(1)}, u32[]{:S(2)}, u32[]{:S(2)}) collective-permute-start(f32[264,128]{1,0:T(8,128)S(1)} %get-tuple-element.12), channel_id=1, source_target_pairs={{0,3},{1,0},{2,1},{3,2},{4,7},{5,4},{6,5},{7,6},{8,11},{9,8},{10,9... | collective-permute-start | bytes 405512 | tf_op jit(solution)/shard_map/ppermute | solution.py:167

commit v2 on v1

--- a/solution.py
+++ b/solution.py
@@ -13,6 +13,7 @@
 BANDS = 4
 BLOCKS = 16
 COLUMNS = 64
+LINE = 4
 BODY = PANELS * SLOTS * TILE
 UNIT = BODY + 16
 CHUNK = PANELS * TILE + 8
@@ -49,56 +50,55 @@
     unit_ref[BODY:] = ids.astype(jnp.float32).astype(jnp.bfloat16)
 
 
-def expand_kernel(lefts, kept_ref, *refs):
-    left_refs, right_refs = refs[:lefts], refs[lefts : lefts + BANDS]
-    chunk_refs = refs[lefts + BANDS : lefts + 2 * BANDS]
-    acc, right, wide, ids, where, sem = refs[lefts + 2 * BANDS :]
+def join_kernel(*refs):
+    line_refs, right_refs, (line_ref, tiles_ref, ids_ref) = refs[:LINE], refs[LINE : LINE + BANDS], refs[LINE + BANDS :]
+    for u, ref in enumerate(line_refs):
+        line_ref[u * UNIT : (u + 1) * UNIT] = ref[...]
+    for b, ref in enumerate(right_refs):
+        ids_ref[8 * b : 8 * b + 8] = ref[BODY:].astype(jnp.float32).astype(jnp.int32)[:8]
+        for p in range(PANELS):
+            tiles_ref[p, b * SLOTS : (b + 1) * SLOTS] = ref[p * SLOTS * TILE : (p + 1) * SLOTS * TILE].reshape(
+                SLOTS, TILE, TILE
+            )
+
+
+def expand_kernel(lefts, kept_ref, tiles_ref, right_ids_ref, *refs):
+    left_refs, chunk_refs = refs[: len(lefts)], refs[len(lefts) : len(lefts) + BANDS]
+    all_ref, acc, wide, ids, place, sem = refs[len(lefts) + BANDS :]
     band = lax.axis_index("layer")
-
-    for a, ref in enumerate(left_refs):
-        for u in range(4):
+    units = sum(lefts)
+
+    done = 0
+    for ref, count in zip(left_refs, lefts):
+        all_ref[done * UNIT : (done + count) * UNIT] = ref[...]
+        for u in range(count):
             row = ref[u * UNIT + BODY : (u + 1) * UNIT].astype(jnp.float32).astype(jnp.int32)
-            wide[pl.ds(a * 4 + u, 1)] = row[:1]
-    for b, ref in enumerate(right_refs):
-        row = ref[BODY:].astype(jnp.float32).astype(jnp.int32)
-        wide[pl.ds(lefts * 4 + b, 1)] = row[:1]
-        for p in range(PANELS):
-            right[p, pl.ds(b * SLOTS, SLOTS)] = ref[p * SLOTS * TILE : (p + 1) * SLOTS * TILE].reshape(SLOTS, TILE, TILE)
+            wide[pl.ds(done + u, 1)] = row[:1]
+        done += count
+    for b in range(BANDS):
+        wide[pl.ds(units + b, 1)] = right_ids_ref[8 * b : 8 * b + 1]
     copy = pltpu.make_async_copy(wide, ids, sem)
     copy.start()
     acc[...] = jnp.zeros_like(acc)
     copy.wait()
 
+    def fill(u, carry):
+        for j in range(PANELS):
+            place[ids[u, 8 * j + 4]] = u * PANELS + j
+        return carry
+
+    lax.fori_loop(0, units, fill, 0, unroll=8)
+
     for p in range(PANELS):
-        for j in range(COLUMNS):
-            where[p, j] = -1
-    for p in range(PANELS):
-        for b in range(BANDS):
+        for s in range(BANDS * SLOTS):
+            found = place[ids[units + s // SLOTS, 8 * p + s % SLOTS]]
+            unit, j = found // PANELS, found % PANELS
+            start = pl.multiple_of(unit * UNIT + j * SLOTS * TILE, 16)
+            product = jnp.dot(
+                all_ref[pl.ds(start, SLOTS * TILE)], tiles_ref[p, s], preferred_element_type=jnp.float32
+            )
             for k in range(SLOTS):
-                where[p, ids[lefts * 4 + b, 8 * p + k]] = b * SLOTS + k
-
-    for a, ref in enumerate(left_refs):
-
-        def step(i, carry, a=a, ref=ref):
-            unit = a * 4 + i // PANELS
-            j = lax.rem(i, PANELS)
-            column = ids[unit, 8 * j + 4]
-            start = pl.multiple_of((i // PANELS) * UNIT + j * SLOTS * TILE, 16)
-            for p in range(PANELS):
-                slot = where[p, column]
-
-                @pl.when(slot >= 0)
-                def _():
-                    product = jnp.dot(
-                        ref[pl.ds(start, SLOTS * TILE)], right[p, slot], preferred_element_type=jnp.float32
-                    )
-                    for k in range(SLOTS):
-                        block = ids[unit, 8 * j + k] - BLOCKS * band
-                        acc[p, block] += product[k * TILE : (k + 1) * TILE]
-
-            return carry
-
-        lax.fori_loop(0, 4 * PANELS, step, 0)
+                acc[p, ids[unit, 8 * j + k] % BLOCKS] += product[k * TILE : (k + 1) * TILE]
 
     for p in range(PANELS):
 
@@ -106,7 +106,7 @@
             value = acc[p, r]
             return total + jnp.sum((value * value).reshape(TILE // 8, 8, TILE), axis=0)
 
-        total = lax.fori_loop(0, BLOCKS, add, jnp.zeros((8, TILE), jnp.float32))
+        total = lax.fori_loop(0, BLOCKS, add, jnp.zeros((8, TILE), jnp.float32), unroll=4)
         total = jnp.sum(total, axis=0, keepdims=True)
         for s in range(BANDS):
             slot = lax.rem(band + s, BANDS)
@@ -138,31 +138,48 @@
         compiler_params=LIMIT,
     )(band_rows, tile_values)
 
+    def swap(value):
+        return lax.ppermute(value, "core", [(0, 1), (1, 0)])
+
+    def swap(value):
+        return lax.ppermute(value, "core", [(0, 1), (1, 0)])
+
     lines = [lax.ppermute(unit, CELL, cells(a, b)) for a, b in (((1, 0), (0, 1)), ((3, 0), (0, 3)), ((2, 0), (0, 2)))]
     line = jnp.concatenate([unit, *lines], axis=0)
     rights = [unit] + [lax.ppermute(unit, "layer", ring(s)) for s in (1, 3, 2)]
-    rest = [lax.ppermute(line, CELL, cells(a, b)) for a, b in (((0, 1), (1, 0)), ((0, 3), (3, 0)), ((0, 2), (2, 0)))]
-    lefts = [line, *rest]
-    lefts = lefts + [lax.ppermute(one, "core", [(0, 1), (1, 0)]) for one in lefts]
-
-    count = len(lefts)
-    ids = count * 4 + 8
+    up, down = [lax.ppermute(line, CELL, cells(a, b)) for a, b in (((0, 1), (1, 0)), ((0, 3), (3, 0)))]
+    line_again, tiles, right_ids = pl.pallas_call(
+        join_kernel,
+        out_shape=[
+            jax.ShapeDtypeStruct((LINE * UNIT, TILE), jnp.bfloat16),
+            jax.ShapeDtypeStruct((PANELS, BANDS * SLOTS, TILE, TILE), jnp.bfloat16),
+            jax.ShapeDtypeStruct((8 * BANDS, TILE), jnp.int32),
+        ],
+        in_specs=[VMEM] * (LINE + BANDS),
+        out_specs=[VMEM] * 3,
+        compiler_params=LIMIT,
+    )(unit, *lines, *rights)
+    far = lax.ppermute(line_again, CELL, cells((0, 2), (2, 0)))
+
+    lefts = [line, up, down, swap(line), swap(up), swap(down), far, swap(far)]
+    counts = tuple(one.shape[0] // UNIT for one in lefts)
+    units = sum(counts)
     chunks = pl.pallas_call(
-        functools.partial(expand_kernel, count),
+        functools.partial(expand_kernel, counts),
         out_shape=[jax.ShapeDtypeStruct((CHUNK, TILE), jnp.float32)] * BANDS,
-        in_specs=[SMEM] + [VMEM] * (count + BANDS),
+        in_specs=[SMEM] + [VMEM] * (len(lefts) + 2),
         out_specs=[VMEM] * BANDS,
         scratch_shapes=[
+            pltpu.VMEM((units * UNIT, TILE), jnp.bfloat16),
             pltpu.VMEM((PANELS, BLOCKS, TILE, TILE), jnp.float32),
-            pltpu.VMEM((PANELS, BANDS * SLOTS, TILE, TILE), jnp.bfloat16),
-            pltpu.VMEM((ids, TILE), jnp.int32),
-            pltpu.SMEM((ids, TILE), jnp.int32),
-            pltpu.SMEM((PANELS, COLUMNS), jnp.int32),
+            pltpu.VMEM((units + 8, TILE), jnp.int32),
+            pltpu.SMEM((units + 8, TILE), jnp.int32),
+            pltpu.SMEM((COLUMNS,), jnp.int32),
             pltpu.SemaphoreType.DMA,
         ],
         compiler_params=LIMIT,
         cost_estimate=pl.CostEstimate(flops=2**29, bytes_accessed=10 * 2**20, transcendentals=0),
-    )(kept_rows, *lefts, *rights)
+    )(kept_rows, tiles, right_ids, *lefts)
 
     chunks = [chunks[0]] + [lax.ppermute(chunks[s], "layer", ring(s)) for s in (1, 2, 3)]
     return pl.pallas_call(

time: 90.5 us -> 70.1 us (0.77)
  the two profiles are of different devices: /device:TPU:32 before, /device:TPU:1 now
where the time goes in v2:
time: 70.1 us; the launch traced here: 70 us
  starting transfers between devices  33.2 us (47%)
  waiting for transfers between devices  30.2 us (43%)
  Pallas kernels  4.84 us (7%)
  local copies, waits for them, and re-layouts  1.64 us (2%)
    ppermute x4, starting transfers between devices, swap(): return lax.ppermute(value, 'core', [(0, 1), (1, 0)])  13.1 us
    ppermute x2, waiting for transfers between devices, per_device(): lax.ppermute(line, CELL, cells(a, b))  7.47 us
    ppermute x1, waiting for transfers between devices, per_device(): far = lax.ppermute(line_again, CELL, cells((0, 2), (2, 0)))  7.16 us
    ppermute x3, starting transfers between devices, per_device(): lax.ppermute(unit, CELL, cells(a, b))  5.68 us
    ppermute x3, starting transfers between devices, per_device(): rights = [unit] + [lax.ppermute(unit, 'layer', ring(s)) for s in (1, 3, 2)]  5.29 us
    ppermute x3, waiting for transfers between devices, per_device(): rights = [unit] + [lax.ppermute(unit, 'layer', ring(s)) for s in (1, 3, 2)]  5.24 us
    ppermute x3, waiting for transfers between devices, per_device(): lax.ppermute(chunks[s], 'layer', ring(s))  5.16 us
    ppermute x3, starting transfers between devices, per_device(): lax.ppermute(chunks[s], 'layer', ring(s))  5.09 us
  transfers between devices with their start and end apart: 16, of which 11 were waited for; matrix products, arithmetic and copies ran while one was open for 0% of the time, Pallas kernels for 0%

profile of v2, /device:TPU:1, one launch (start us, length us, event | category | flops | bytes accessed | tf_op | source)
XLA Modules:
  0.0 70.0 jit_solution(12554922283440736763)
XLA Ops:
  0.0 0.0 copy-start
  0.0 0.9 %copy-done = bf16[2,1,4,128,128]{4,3,2,1,0:T(8,128)(2,1)S(1)} copy-done((bf16[2,1,4,128,128]{4,3,2,1,0:T(8,128)(2,1)S(1)}, bf16[2,1,4,128,128]{4,3,2,1,0:T(8,128)(2,1)}, u32[]{:S(2)}) %copy-start) | copy-done | bytes 262168
  1.0 0.0 copy-start.2
  1.0 0.7 copy-done.2
  1.6 0.6 shard_map.46.refs_0_.refs_4_
  2.2 3.8 %collective-permute-start.5 = (bf16[1040,128]{1,0:T(8,128)(2,1)S(1)}, bf16[1040,128]{1,0:T(8,128)(2,1)S(1)}, u32[]{:S(2)}, u32[]{:S(2)}) collective-permute-start(bf16[1040,128]{1,0:T(8,128)(2,1)S(1)} %shard_map.46.refs_0_.refs_4_), channel_id=1, source_target_pairs={{0,2},{1,3},{2,0},{3,1},{4,6},{5,7},{6,4},{7,5},{8,10},{9,11},{10,... | collective-permute-start | bytes 798728 | tf_op jit(solution)/shard_map/ppermute | solution.py:149
  6.0 0.8 %collective-permute-start.4 = (bf16[1040,128]{1,0:T(8,128)(2,1)S(1)}, bf16[1040,128]{1,0:T(8,128)(2,1)S(1)}, u32[]{:S(2)}, u32[]{:S(2)}) collective-permute-start(bf16[1040,128]{1,0:T(8,128)(2,1)S(1)} %shard_map.46.refs_0_.refs_4_), channel_id=1, source_target_pairs={{0,3},{1,0},{2,1},{3,2},{4,7},{5,4},{6,5},{7,6},{8,11},{9,8},{10,9... | collective-permute-start | bytes 798728 | tf_op jit(solution)/shard_map/ppermute | solution.py:149
  6.8 0.7 collective-permute-start.3
  7.5 3.6 %collective-permute-start.2 = (bf16[1040,128]{1,0:T(8,128)(2,1)S(1)}, bf16[1040,128]{1,0:T(8,128)(2,1)S(1)}, u32[]{:S(2)}, u32[]{:S(2)}) collective-permute-start(bf16[1040,128]{1,0:T(8,128)(2,1)S(1)} %shard_map.46.refs_0_.refs_4_), channel_id=1, source_target_pairs={{0,64},{4,20},{8,72},{12,28},{16,80},{20,4},{24,88},{28,12},{32,96... | collective-permute-start | bytes 798728 | tf_op jit(solution)/shard_map/ppermute | solution.py:147
  11.1 0.4 collective-permute-start.1
  11.5 0.3 collective-permute-done.5.refs_7_
  11.9 1.6 %collective-permute-start = (bf16[1040,128]{1,0:T(8,128)(2,1)S(1)}, bf16[1040,128]{1,0:T(8,128)(2,1)S(1)}, u32[]{:S(2)}, u32[]{:S(2)}) collective-permute-start(bf16[1040,128]{1,0:T(8,128)(2,1)S(1)} %shard_map.46.refs_0_.refs_4_), channel_id=1, source_target_pairs={{0,32},{4,12},{8,40},{12,20},{16,48},{20,28},{24,56},{28,4},{32,64... | collective-permute-start | bytes 798728 | tf_op jit(solution)/shard_map/ppermute | solution.py:147
  13.5 4.5 %collective-permute-done.4.refs_6_ = bf16[1040,128]{1,0:T(8,128)(2,1)S(1)} collective-permute-done((bf16[1040,128]{1,0:T(8,128)(2,1)S(1)}, bf16[1040,128]{1,0:T(8,128)(2,1)S(1)}, u32[]{:S(2)}, u32[]{:S(2)}) %collective-permute-start.4) | collective-permute-done | bytes 266272 | tf_op jit(solution)/shard_map/ppermute | solution.py:149
  18.0 0.4 collective-permute-done.3.refs_5_
  18.4 0.0 collective-permute-done.2.refs_3_
  18.4 0.4 collective-permute-done.1.refs_2_
  18.8 0.9 %collective-permute-done.refs_1_ = bf16[1040,128]{1,0:T(8,128)(2,1)S(1)} collective-permute-done((bf16[1040,128]{1,0:T(8,128)(2,1)S(1)}, bf16[1040,128]{1,0:T(8,128)(2,1)S(1)}, u32[]{:S(2)}, u32[]{:S(2)}) %collective-permute-start) | collective-permute-done | bytes 266272 | tf_op jit(solution)/shard_map/ppermute | solution.py:147
  19.7 0.1 shard_map.47
  19.9 0.0 copy-start.3
  19.9 2.5 %collective-permute-start.11 = (bf16[4160,128]{1,0:T(8,128)(2,1)S(1)}, bf16[4160,128]{1,0:T(8,128)(2,1)S(1)}, u32[]{:S(2)}, u32[]{:S(2)}) collective-permute-start(bf16[4160,128]{1,0:T(8,128)(2,1)S(1)} %get-tuple-element.14), channel_id=1, source_target_pairs={{0,16},{4,68},{8,24},{12,76},{16,0},{20,84},{24,8},{28,92},{32,48}... | collective-permute-start | bytes 3194888 | tf_op jit(solution)/shard_map/ppermute | solution.py:162
  22.4 0.1 pad_maximum_fusion.refs_0_
  22.5 0.9 %collective-permute-start.7 = (bf16[4160,128]{1,0:T(8,128)(2,1)S(1)}, bf16[4160,128]{1,0:T(8,128)(2,1)S(1)}, u32[]{:S(2)}, u32[]{:S(2)}) collective-permute-start(bf16[4160,128]{1,0:T(8,128)(2,1)S(1)} %pad_maximum_fusion.refs_0_), channel_id=1, source_target_pairs={{0,24},{4,100},{8,0},{12,108},{16,8},{20,116},{24,16},{28,124},{32... | collective-permute-start | bytes 3194888 | tf_op jit(solution)/shard_map/ppermute | solution.py:150
  23.4 0.6 collective-permute-start.6
  24.0 4.5 %collective-permute-start.8 = (bf16[4160,128]{1,0:T(8,128)(2,1)S(1)}, bf16[4160,128]{1,0:T(8,128)(2,1)S(1)}, u32[]{:S(2)}, u32[]{:S(2)}) collective-permute-start(bf16[4160,128]{1,0:T(8,128)(2,1)S(1)} %pad_maximum_fusion.refs_0_), channel_id=1, source_target_pairs={{0,4},{4,0},{1,5},{5,1},{2,6},{6,2},{3,7},{7,3},{8,12},{12,8},{9,1... | collective-permute-start | bytes 3194888 | tf_op jit(solution)/shard_map/ppermute | solution.py:145
  28.5 7.2 %collective-permute-done.11.refs_6_ = bf16[4160,128]{1,0:T(8,128)(2,1)S(1)} collective-permute-done((bf16[4160,128]{1,0:T(8,128)(2,1)S(1)}, bf16[4160,128]{1,0:T(8,128)(2,1)S(1)}, u32[]{:S(2)}, u32[]{:S(2)}) %collective-permute-start.11) | collective-permute-done | bytes 1064992 | tf_op jit(solution)/shard_map/ppermute | solution.py:162
  35.6 3.7 %collective-permute-start.12 = (bf16[4160,128]{1,0:T(8,128)(2,1)S(1)}, bf16[4160,128]{1,0:T(8,128)(2,1)S(1)}, u32[]{:S(2)}, u32[]{:S(2)}) collective-permute-start(bf16[4160,128]{1,0:T(8,128)(2,1)S(1)} %collective-permute-done.11.refs_6_), channel_id=1, source_target_pairs={{0,4},{4,0},{1,5},{5,1},{2,6},{6,2},{3,7},{7,3},{8,12},{12,8},{9,1... | collective-permute-start | bytes 3194888 | tf_op jit(solution)/shard_map/ppermute | solution.py:145
  39.4 7.5 %collective-permute-done.7.refs_2_ = bf16[4160,128]{1,0:T(8,128)(2,1)S(1)} collective-permute-done((bf16[4160,128]{1,0:T(8,128)(2,1)S(1)}, bf16[4160,128]{1,0:T(8,128)(2,1)S(1)}, u32[]{:S(2)}, u32[]{:S(2)}) %collective-permute-start.7) | collective-permute-done | bytes 1064992 | tf_op jit(solution)/shard_map/ppermute | solution.py:150
  46.8 4.9 %collective-permute-start.10 = (bf16[4160,128]{1,0:T(8,128)(2,1)S(1)}, bf16[4160,128]{1,0:T(8,128)(2,1)S(1)}, u32[]{:S(2)}, u32[]{:S(2)}) collective-permute-start(bf16[4160,128]{1,0:T(8,128)(2,1)S(1)} %collective-permute-done.7.refs_2_), channel_id=1, source_target_pairs={{0,4},{4,0},{1,5},{5,1},{2,6},{6,2},{3,7},{7,3},{8,12},{12,8},{9,1... | collective-permute-start | bytes 3194888 | tf_op jit(solution)/shard_map/ppermute | solution.py:145
  51.7 0.0 collective-permute-done.6.refs_1_
  51.7 0.0 collective-permute-start.9
  51.7 0.0 collective-permute-done.8.refs_3_
  51.8 0.0 collective-permute-done.12.refs_7_
  51.8 2.3 %collective-permute-done.10.refs_5_ = bf16[4160,128]{1,0:T(8,128)(2,1)S(1)} collective-permute-done((bf16[4160,128]{1,0:T(8,128)(2,1)S(1)}, bf16[4160,128]{1,0:T(8,128)(2,1)S(1)}, u32[]{:S(2)}, u32[]{:S(2)}) %collective-permute-start.10) | collective-permute-done | bytes 1064992 | tf_op jit(solution)/shard_map/ppermute | solution.py:145
  54.1 1.5 %collective-permute-done.9.refs_4_ = bf16[4160,128]{1,0:T(8,128)(2,1)S(1)} collective-permute-done((bf16[4160,128]{1,0:T(8,128)(2,1)S(1)}, bf16[4160,128]{1,0:T(8,128)(2,1)S(1)}, u32[]{:S(2)}, u32[]{:S(2)}) %collective-permute-start.9) | collective-permute-done | bytes 1064992 | tf_op jit(solution)/shard_map/ppermute | solution.py:145
  55.6 0.0 copy-done.3
  55.6 0.0 copy-start.1
  55.6 3.3 %shard_map.48 = (f32[264,128]{1,0:T(8,128)S(1)}, f32[264,128]{1,0:T(8,128)S(1)}, f32[264,128]{1,0:T(8,128)S(1)}, f32[264,128]{1,0:T(8,128)S(1)}) custom-call(s32[2,1,4]{2,1,0:T(1,128)S(1)} %copy-done.3, bf16[2,16,128,128]{3,2,1,0:T(8,128)(2,1)S(1)} %get-tuple-element.12.tiles_ref, s32[32,128]{1,0:T(8,128)S(1)} %get-tuple-element.13.right_ids_ref, ...), custom_call_target="tpu_custom_call" | custom-call | flops 536870912 | bytes 10485760 | tf_op jit(solution)/shard_map/pallas_call | solution.py:167
  58.9 1.4 %collective-permute-start.13 = (f32[264,128]{1,0:T(8,128)S(1)}, f32[264,128]{1,0:T(8,128)S(1)}, u32[]{:S(2)}, u32[]{:S(2)}) collective-permute-start(f32[264,128]{1,0:T(8,128)S(1)} %get-tuple-element.16), channel_id=1, source_target_pairs={{0,1},{1,2},{2,3},{3,0},{4,5},{5,6},{6,7},{7,4},{8,9},{9,10},{10,1... | collective-permute-start | bytes 405512 | tf_op jit(solution)/shard_map/ppermute | solution.py:184
  60.3 2.6 %collective-permute-start.14 = (f32[264,128]{1,0:T(8,128)S(1)}, f32[264,128]{1,0:T(8,128)S(1)}, u32[]{:S(2)}, u32[]{:S(2)}) collective-permute-start(f32[264,128]{1,0:T(8,128)S(1)} %get-tuple-element.17), channel_id=1, source_target_pairs={{0,2},{1,3},{2,0},{3,1},{4,6},{5,7},{6,4},{7,5},{8,10},{9,11},{10,... | collective-permute-start | bytes 405512 | tf_op jit(solution)/shard_map/ppermute | solution.py:184
  63.0 1.1 %collective-permute-start.15 = (f32[264,128]{1,0:T(8,128)S(1)}, f32[264,128]{1,0:T(8,128)S(1)}, u32[]{:S(2)}, u32[]{:S(2)}) collective-permute-start(f32[264,128]{1,0:T(8,128)S(1)} %get-tuple-element.18), channel_id=1, source_target_pairs={{0,3},{1,0},{2,1},{3,2},{4,7},{5,4},{6,5},{7,6},{8,11},{9,8},{10,9... | collective-permute-start | bytes 405512 | tf_op jit(solution)/shard_map/ppermute | solution.py:184
  64.0 1.2 %collective-permute-done.13.refs_1_ = f32[264,128]{1,0:T(8,128)S(1)} collective-permute-done((f32[264,128]{1,0:T(8,128)S(1)}, f32[264,128]{1,0:T(8,128)S(1)}, u32[]{:S(2)}, u32[]{:S(2)}) %collective-permute-start.13) | collective-permute-done | bytes 135200 | tf_op jit(solution)/shard_map/ppermute | solution.py:184
  65.2 4.0 %collective-permute-done.14.refs_2_ = f32[264,128]{1,0:T(8,128)S(1)} collective-permute-done((f32[264,128]{1,0:T(8,128)S(1)}, f32[264,128]{1,0:T(8,128)S(1)}, u32[]{:S(2)}, u32[]{:S(2)}) %collective-permute-start.14) | collective-permute-done | bytes 135200 | tf_op jit(solution)/shard_map/ppermute | solution.py:184
  69.2 0.0 collective-permute-done.15.refs_3_
  69.2 0.0 copy-done.1
  69.2 0.8 %shard_map.49 = bf16[2,4,1,128,128]{4,3,2,1,0:T(8,128)(2,1)} custom-call(s32[2,4,128]{2,1,0:T(4,128)S(1)} %copy-done.1, f32[264,128]{1,0:T(8,128)S(1)} %get-tuple-element.15.refs_0_, f32[264,128]{1,0:T(8,128)S(1)} %collective-permute-done.13.refs_1_, f32[264,128]{1,0:T(8,128)S(1)} %collective-permute-done.14.refs_2_, ...), custom_call_target="tpu_custom_call" | custom-call | tf_op jit(solution)/shard_map/pallas_call | solution.py:185
Async XLA Ops:
  0.0 0.9 %copy-start = (bf16[2,1,4,128,128]{4,3,2,1,0:T(8,128)(2,1)S(1)}, bf16[2,1,4,128,128]{4,3,2,1,0:T(8,128)(2,1)}, u32[]{:S(2)}) copy-start(bf16[2,1,4,128,128]{4,3,2,1,0:T(8,128)(2,1)} %tiles_ref.1) | copy-start | bytes 786436
  1.0 0.7 copy-start.2
  2.2 9.7 %collective-permute-start.5 = (bf16[1040,128]{1,0:T(8,128)(2,1)S(1)}, bf16[1040,128]{1,0:T(8,128)(2,1)S(1)}, u32[]{:S(2)}, u32[]{:S(2)}) collective-permute-start(bf16[1040,128]{1,0:T(8,128)(2,1)S(1)} %shard_map.46.refs_0_.refs_4_), channel_id=1, source_target_pairs={{0,2},{1,3},{2,0},{3,1},{4,6},{5,7},{6,4},{7,5},{8,10},{9,11},{10,... | collective-permute-start | bytes 798728 | tf_op jit(solution)/shard_map/ppermute | solution.py:149
  6.0 11.9 %collective-permute-start.4 = (bf16[1040,128]{1,0:T(8,128)(2,1)S(1)}, bf16[1040,128]{1,0:T(8,128)(2,1)S(1)}, u32[]{:S(2)}, u32[]{:S(2)}) collective-permute-start(bf16[1040,128]{1,0:T(8,128)(2,1)S(1)} %shard_map.46.refs_0_.refs_4_), channel_id=1, source_target_pairs={{0,3},{1,0},{2,1},{3,2},{4,7},{5,4},{6,5},{7,6},{8,11},{9,8},{10,9... | collective-permute-start | bytes 798728 | tf_op jit(solution)/shard_map/ppermute | solution.py:149
  6.8 11.6 %collective-permute-start.3 = (bf16[1040,128]{1,0:T(8,128)(2,1)S(1)}, bf16[1040,128]{1,0:T(8,128)(2,1)S(1)}, u32[]{:S(2)}, u32[]{:S(2)}) collective-permute-start(bf16[1040,128]{1,0:T(8,128)(2,1)S(1)} %shard_map.46.refs_0_.refs_4_), channel_id=1, source_target_pairs={{0,1},{1,2},{2,3},{3,0},{4,5},{5,6},{6,7},{7,4},{8,9},{9,10},{10,1... | collective-permute-start | bytes 798728 | tf_op jit(solution)/shard_map/ppermute | solution.py:149
  7.5 10.9 %collective-permute-start.2 = (bf16[1040,128]{1,0:T(8,128)(2,1)S(1)}, bf16[1040,128]{1,0:T(8,128)(2,1)S(1)}, u32[]{:S(2)}, u32[]{:S(2)}) collective-permute-start(bf16[1040,128]{1,0:T(8,128)(2,1)S(1)} %shard_map.46.refs_0_.refs_4_), channel_id=1, source_target_pairs={{0,64},{4,20},{8,72},{12,28},{16,80},{20,4},{24,88},{28,12},{32,96... | collective-permute-start | bytes 798728 | tf_op jit(solution)/shard_map/ppermute | solution.py:147
  11.1 7.7 %collective-permute-start.1 = (bf16[1040,128]{1,0:T(8,128)(2,1)S(1)}, bf16[1040,128]{1,0:T(8,128)(2,1)S(1)}, u32[]{:S(2)}, u32[]{:S(2)}) collective-permute-start(bf16[1040,128]{1,0:T(8,128)(2,1)S(1)} %shard_map.46.refs_0_.refs_4_), channel_id=1, source_target_pairs={{0,96},{4,28},{8,104},{12,4},{16,112},{20,12},{24,120},{28,20},{32... | collective-permute-start | bytes 798728 | tf_op jit(solution)/shard_map/ppermute | solution.py:147
  11.9 7.9 %collective-permute-start = (bf16[1040,128]{1,0:T(8,128)(2,1)S(1)}, bf16[1040,128]{1,0:T(8,128)(2,1)S(1)}, u32[]{:S(2)}, u32[]{:S(2)}) collective-permute-start(bf16[1040,128]{1,0:T(8,128)(2,1)S(1)} %shard_map.46.refs_0_.refs_4_), channel_id=1, source_target_pairs={{0,32},{4,12},{8,40},{12,20},{16,48},{20,28},{24,56},{28,4},{32,64... | collective-permute-start | bytes 798728 | tf_op jit(solution)/shard_map/ppermute | solution.py:147
  19.9 35.7 %copy-start.3 = (s32[2,1,4]{2,1,0:T(1,128)S(1)}, s32[2,1,4]{2,1,0:T(1,128)}, u32[]{:S(2)}) copy-start(s32[2,1,4]{2,1,0:T(1,128)} %kept_ref.1) | copy-start | bytes 100
  19.9 15.7 %collective-permute-start.11 = (bf16[4160,128]{1,0:T(8,128)(2,1)S(1)}, bf16[4160,128]{1,0:T(8,128)(2,1)S(1)}, u32[]{:S(2)}, u32[]{:S(2)}) collective-permute-start(bf16[4160,128]{1,0:T(8,128)(2,1)S(1)} %get-tuple-element.14), channel_id=1, source_target_pairs={{0,16},{4,68},{8,24},{12,76},{16,0},{20,84},{24,8},{28,92},{32,48}... | collective-permute-start | bytes 3194888 | tf_op jit(solution)/shard_map/ppermute | solution.py:162
  22.5 24.3 %collective-permute-start.7 = (bf16[4160,128]{1,0:T(8,128)(2,1)S(1)}, bf16[4160,128]{1,0:T(8,128)(2,1)S(1)}, u32[]{:S(2)}, u32[]{:S(2)}) collective-permute-start(bf16[4160,128]{1,0:T(8,128)(2,1)S(1)} %pad_maximum_fusion.refs_0_), channel_id=1, source_target_pairs={{0,24},{4,100},{8,0},{12,108},{16,8},{20,116},{24,16},{28,124},{32... | collective-permute-start | bytes 3194888 | tf_op jit(solution)/shard_map/ppermute | solution.py:150
  23.4 28.3 %collective-permute-start.6 = (bf16[4160,128]{1,0:T(8,128)(2,1)S(1)}, bf16[4160,128]{1,0:T(8,128)(2,1)S(1)}, u32[]{:S(2)}, u32[]{:S(2)}) collective-permute-start(bf16[4160,128]{1,0:T(8,128)(2,1)S(1)} %pad_maximum_fusion.refs_0_), channel_id=1, source_target_pairs={{0,8},{4,36},{8,16},{12,44},{16,24},{20,52},{24,0},{28,60},{32,40}... | collective-permute-start | bytes 3194888 | tf_op jit(solution)/shard_map/ppermute | solution.py:150
  24.0 27.7 %collective-permute-start.8 = (bf16[4160,128]{1,0:T(8,128)(2,1)S(1)}, bf16[4160,128]{1,0:T(8,128)(2,1)S(1)}, u32[]{:S(2)}, u32[]{:S(2)}) collective-permute-start(bf16[4160,128]{1,0:T(8,128)(2,1)S(1)} %pad_maximum_fusion.refs_0_), channel_id=1, source_target_pairs={{0,4},{4,0},{1,5},{5,1},{2,6},{6,2},{3,7},{7,3},{8,12},{12,8},{9,1... | collective-permute-start | bytes 3194888 | tf_op jit(solution)/shard_map/ppermute | solution.py:145
  35.6 16.1 %collective-permute-start.12 = (bf16[4160,128]{1,0:T(8,128)(2,1)S(1)}, bf16[4160,128]{1,0:T(8,128)(2,1)S(1)}, u32[]{:S(2)}, u32[]{:S(2)}) collective-permute-start(bf16[4160,128]{1,0:T(8,128)(2,1)S(1)} %collective-permute-done.11.refs_6_), channel_id=1, source_target_pairs={{0,4},{4,0},{1,5},{5,1},{2,6},{6,2},{3,7},{7,3},{8,12},{12,8},{9,1... | collective-permute-start | bytes 3194888 | tf_op jit(solution)/shard_map/ppermute | solution.py:145
  46.8 7.2 %collective-permute-start.10 = (bf16[4160,128]{1,0:T(8,128)(2,1)S(1)}, bf16[4160,128]{1,0:T(8,128)(2,1)S(1)}, u32[]{:S(2)}, u32[]{:S(2)}) collective-permute-start(bf16[4160,128]{1,0:T(8,128)(2,1)S(1)} %collective-permute-done.7.refs_2_), channel_id=1, source_target_pairs={{0,4},{4,0},{1,5},{5,1},{2,6},{6,2},{3,7},{7,3},{8,12},{12,8},{9,1... | collective-permute-start | bytes 3194888 | tf_op jit(solution)/shard_map/ppermute | solution.py:145
  51.7 3.8 %collective-permute-start.9 = (bf16[4160,128]{1,0:T(8,128)(2,1)S(1)}, bf16[4160,128]{1,0:T(8,128)(2,1)S(1)}, u32[]{:S(2)}, u32[]{:S(2)}) collective-permute-start(bf16[4160,128]{1,0:T(8,128)(2,1)S(1)} %collective-permute-done.6.refs_1_), channel_id=1, source_target_pairs={{0,4},{4,0},{1,5},{5,1},{2,6},{6,2},{3,7},{7,3},{8,12},{12,8},{9,1... | collective-permute-start | bytes 3194888 | tf_op jit(solution)/shard_map/ppermute | solution.py:145
  55.6 13.6 %copy-start.1 = (s32[2,4,128]{2,1,0:T(4,128)S(1)}, s32[2,4,128]{2,1,0:T(4,128)}, u32[]{:S(2)}) copy-start(s32[2,4,128]{2,1,0:T(4,128)} %mask_ref.1) | copy-start | bytes 12292
  58.9 6.3 %collective-permute-start.13 = (f32[264,128]{1,0:T(8,128)S(1)}, f32[264,128]{1,0:T(8,128)S(1)}, u32[]{:S(2)}, u32[]{:S(2)}) collective-permute-start(f32[264,128]{1,0:T(8,128)S(1)} %get-tuple-element.16), channel_id=1, source_target_pairs={{0,1},{1,2},{2,3},{3,0},{4,5},{5,6},{6,7},{7,4},{8,9},{9,10},{10,1... | collective-permute-start | bytes 405512 | tf_op jit(solution)/shard_map/ppermute | solution.py:184
  60.3 8.8 %collective-permute-start.14 = (f32[264,128]{1,0:T(8,128)S(1)}, f32[264,128]{1,0:T(8,128)S(1)}, u32[]{:S(2)}, u32[]{:S(2)}) collective-permute-start(f32[264,128]{1,0:T(8,128)S(1)} %get-tuple-element.17), channel_id=1, source_target_pairs={{0,2},{1,3},{2,0},{3,1},{4,6},{5,7},{6,4},{7,5},{8,10},{9,11},{10,... | collective-permute-start | bytes 405512 | tf_op jit(solution)/shard_map/ppermute | solution.py:184
  63.0 6.2 %collective-permute-start.15 = (f32[264,128]{1,0:T(8,128)S(1)}, f32[264,128]{1,0:T(8,128)S(1)}, u32[]{:S(2)}, u32[]{:S(2)}) collective-permute-start(f32[264,128]{1,0:T(8,128)S(1)} %get-tuple-element.18), channel_id=1, source_target_pairs={{0,3},{1,0},{2,1},{3,2},{4,7},{5,4},{6,5},{7,6},{8,11},{9,8},{10,9... | collective-permute-start | bytes 405512 | tf_op jit(solution)/shard_map/ppermute | solution.py:184

commit v3 on v2

--- a/solution.py
+++ b/solution.py
@@ -50,6 +50,10 @@
     unit_ref[BODY:] = ids.astype(jnp.float32).astype(jnp.bfloat16)
 
 
+def again_kernel(unit_ref, *refs):
+    refs[-1][...] = unit_ref[...]
+
+
 def join_kernel(*refs):
     line_refs, right_refs, (line_ref, tiles_ref, ids_ref) = refs[:LINE], refs[LINE : LINE + BANDS], refs[LINE + BANDS :]
     for u, ref in enumerate(line_refs):
@@ -146,7 +150,14 @@
 
     lines = [lax.ppermute(unit, CELL, cells(a, b)) for a, b in (((1, 0), (0, 1)), ((3, 0), (0, 3)), ((2, 0), (0, 2)))]
     line = jnp.concatenate([unit, *lines], axis=0)
-    rights = [unit] + [lax.ppermute(unit, "layer", ring(s)) for s in (1, 3, 2)]
+    unit_again = pl.pallas_call(
+        again_kernel,
+        out_shape=jax.ShapeDtypeStruct((UNIT, TILE), jnp.bfloat16),
+        in_specs=[VMEM] * LINE,
+        out_specs=VMEM,
+        compiler_params=LIMIT,
+    )(unit, *lines)
+    rights = [unit] + [lax.ppermute(unit_again, "layer", ring(s)) for s in (1, 3, 2)]
     up, down = [lax.ppermute(line, CELL, cells(a, b)) for a, b in (((0, 1), (1, 0)), ((0, 3), (3, 0)))]
     line_again, tiles, right_ids = pl.pallas_call(
         join_kernel,
@@ -159,9 +170,9 @@
         out_specs=[VMEM] * 3,
         compiler_params=LIMIT,
     )(unit, *lines, *rights)
-    far = lax.ppermute(line_again, CELL, cells((0, 2), (2, 0)))
-
-    lefts = [line, up, down, swap(line), swap(up), swap(down), far, swap(far)]
+    far = lax.ppermute(line, CELL, cells((0, 2), (2, 0)))
+
+    lefts = [line, up, down, swap(line_again), swap(up), swap(down), far, swap(far)]
     counts = tuple(one.shape[0] // UNIT for one in lefts)
     units = sum(counts)
     chunks = pl.pallas_call(

time: 70.1 us -> 63.4 us (0.904)
  waiting for transfers between devices: 30.2 us -> 26 us
  starting transfers between devices: 33.2 us -> 30.6 us
    ppermute x2, waiting for transfers between devices: 7.47 us -> 1.84 us  [per_device(): lax.ppermute(line, CELL, cells(a, b))]
    ppermute x3, waiting for transfers between devices: 1.32 us -> 6.27 us  [per_device(): lax.ppermute(unit, CELL, cells(a, b))]
    ppermute x4, waiting for transfers between devices: 12.4 us -> 8.91 us  [the longest x3 8.91 us: per_device(): lax.ppermute(unit_again, 'layer', ring(s))]
    ppermute x4, starting transfers between devices: 13.1 us -> 10.5 us  [swap(): return lax.ppermute(value, 'core', [(0, 1), (1, 0)])]
  transfers between devices with their start and end apart: 16 -> 16, of which waited for: 11 -> 10; matrix products, arithmetic and copies ran while one was open for 0% -> 0% of each run, Pallas kernels for 0% -> 0%
where the time goes in v3:
time: 63.4 us; the launch traced here: 63.2 us
  starting transfers between devices  30.6 us (48%)
  waiting for transfers between devices  26 us (41%)
  Pallas kernels  4.85 us (8%)
  local copies, waits for them, and re-layouts  1.64 us (3%)
    ppermute x4, starting transfers between devices, swap(): return lax.ppermute(value, 'core', [(0, 1), (1, 0)])  10.5 us
    ppermute x3, waiting for transfers between devices, per_device(): lax.ppermute(unit_again, 'layer', ring(s))  8.91 us
    ppermute x3, waiting for transfers between devices, per_device(): lax.ppermute(unit, CELL, cells(a, b))  6.27 us
    ppermute x3, starting transfers between devices, per_device(): lax.ppermute(unit, CELL, cells(a, b))  5.97 us
    ppermute x3, waiting for transfers between devices, per_device(): lax.ppermute(chunks[s], 'layer', ring(s))  5.14 us
    ppermute x3, starting transfers between devices, per_device(): lax.ppermute(unit_again, 'layer', ring(s))  5.11 us
    ppermute x3, starting transfers between devices, per_device(): lax.ppermute(chunks[s], 'layer', ring(s))  5.05 us
    ppermute x4, waiting for transfers between devices, swap(): return lax.ppermute(value, 'core', [(0, 1), (1, 0)])  3.82 us
  transfers between devices with their start and end apart: 16, of which 10 were waited for; matrix products, arithmetic and copies ran while one was open for 0% of the time, Pallas kernels for 0%

profile of v3, /device:TPU:1, one launch (start us, length us, event | category | flops | bytes accessed | tf_op | source)
XLA Modules:
  0.0 63.2 jit_solution(17559213429041943391)
XLA Ops:
  0.0 0.0 copy-start
  0.0 0.9 %copy-done = bf16[2,1,4,128,128]{4,3,2,1,0:T(8,128)(2,1)S(1)} copy-done((bf16[2,1,4,128,128]{4,3,2,1,0:T(8,128)(2,1)S(1)}, bf16[2,1,4,128,128]{4,3,2,1,0:T(8,128)(2,1)}, u32[]{:S(2)}) %copy-start) | copy-done | bytes 262168
  1.0 0.0 copy-start.2
  1.0 0.7 %copy-done.2 = s32[2,1,4]{2,1,0:T(1,128)S(1)} copy-done((s32[2,1,4]{2,1,0:T(1,128)S(1)}, s32[2,1,4]{2,1,0:T(1,128)}, u32[]{:S(2)}) %copy-start.2) | copy-done | bytes 56
  1.6 0.6 shard_map.46.unit_ref.refs_0_.refs_4_
  2.2 4.5 %collective-permute-start.2 = (bf16[1040,128]{1,0:T(8,128)(2,1)S(1)}, bf16[1040,128]{1,0:T(8,128)(2,1)S(1)}, u32[]{:S(2)}, u32[]{:S(2)}) collective-permute-start(bf16[1040,128]{1,0:T(8,128)(2,1)S(1)} %shard_map.46.unit_ref.refs_0_.refs_4_), channel_id=1, source_target_pairs={{0,64},{4,20},{8,72},{12,28},{16,80},{20,4},{24,88},{28,12},{32,96... | collective-permute-start | bytes 798728 | tf_op jit(solution)/shard_map/ppermute | solution.py:151
  6.7 0.4 collective-permute-start.1
  7.2 1.0 %collective-permute-start = (bf16[1040,128]{1,0:T(8,128)(2,1)S(1)}, bf16[1040,128]{1,0:T(8,128)(2,1)S(1)}, u32[]{:S(2)}, u32[]{:S(2)}) collective-permute-start(bf16[1040,128]{1,0:T(8,128)(2,1)S(1)} %shard_map.46.unit_ref.refs_0_.refs_4_), channel_id=1, source_target_pairs={{0,32},{4,12},{8,40},{12,20},{16,48},{20,28},{24,56},{28,4},{32,64... | collective-permute-start | bytes 798728 | tf_op jit(solution)/shard_map/ppermute | solution.py:151
  8.2 2.6 %collective-permute-done.2.refs_2_.refs_3_ = bf16[1040,128]{1,0:T(8,128)(2,1)S(1)} collective-permute-done((bf16[1040,128]{1,0:T(8,128)(2,1)S(1)}, bf16[1040,128]{1,0:T(8,128)(2,1)S(1)}, u32[]{:S(2)}, u32[]{:S(2)}) %collective-permute-start.2) | collective-permute-done | bytes 266272 | tf_op jit(solution)/shard_map/ppermute | solution.py:151
  10.8 3.6 %collective-permute-done.1.refs_1_.refs_2_ = bf16[1040,128]{1,0:T(8,128)(2,1)S(1)} collective-permute-done((bf16[1040,128]{1,0:T(8,128)(2,1)S(1)}, bf16[1040,128]{1,0:T(8,128)(2,1)S(1)}, u32[]{:S(2)}, u32[]{:S(2)}) %collective-permute-start.1) | collective-permute-done | bytes 266272 | tf_op jit(solution)/shard_map/ppermute | solution.py:151
  14.4 0.0 collective-permute-done.refs_0_.refs_1_
  14.5 0.1 pad_maximum_fusion.refs_0_
  14.5 2.5 %collective-permute-start.11 = (bf16[4160,128]{1,0:T(8,128)(2,1)S(1)}, bf16[4160,128]{1,0:T(8,128)(2,1)S(1)}, u32[]{:S(2)}, u32[]{:S(2)}) collective-permute-start(bf16[4160,128]{1,0:T(8,128)(2,1)S(1)} %pad_maximum_fusion.refs_0_), channel_id=1, source_target_pairs={{0,16},{4,68},{8,24},{12,76},{16,0},{20,84},{24,8},{28,92},{32,48}... | collective-permute-start | bytes 3194888 | tf_op jit(solution)/shard_map/ppermute | solution.py:173
  17.1 0.9 %collective-permute-start.7 = (bf16[4160,128]{1,0:T(8,128)(2,1)S(1)}, bf16[4160,128]{1,0:T(8,128)(2,1)S(1)}, u32[]{:S(2)}, u32[]{:S(2)}) collective-permute-start(bf16[4160,128]{1,0:T(8,128)(2,1)S(1)} %pad_maximum_fusion.refs_0_), channel_id=1, source_target_pairs={{0,24},{4,100},{8,0},{12,108},{16,8},{20,116},{24,16},{28,124},{32... | collective-permute-start | bytes 3194888 | tf_op jit(solution)/shard_map/ppermute | solution.py:161
  18.0 0.6 collective-permute-start.6
  18.6 0.0 copy-start.3
  18.6 3.0 %collective-permute-start.5 = (bf16[1040,128]{1,0:T(8,128)(2,1)S(1)}, bf16[1040,128]{1,0:T(8,128)(2,1)S(1)}, u32[]{:S(2)}, u32[]{:S(2)}) collective-permute-start(bf16[1040,128]{1,0:T(8,128)(2,1)S(1)} %shard_map.47), channel_id=1, source_target_pairs={{0,2},{1,3},{2,0},{3,1},{4,6},{5,7},{6,4},{7,5},{8,10},{9,11},{10,... | collective-permute-start | bytes 798728 | tf_op jit(solution)/shard_map/ppermute | solution.py:160
  21.6 0.8 %collective-permute-start.4 = (bf16[1040,128]{1,0:T(8,128)(2,1)S(1)}, bf16[1040,128]{1,0:T(8,128)(2,1)S(1)}, u32[]{:S(2)}, u32[]{:S(2)}) collective-permute-start(bf16[1040,128]{1,0:T(8,128)(2,1)S(1)} %shard_map.47), channel_id=1, source_target_pairs={{0,3},{1,0},{2,1},{3,2},{4,7},{5,4},{6,5},{7,6},{8,11},{9,8},{10,9... | collective-permute-start | bytes 798728 | tf_op jit(solution)/shard_map/ppermute | solution.py:160
  22.3 3.4 %collective-permute-done.5.refs_7_ = bf16[1040,128]{1,0:T(8,128)(2,1)S(1)} collective-permute-done((bf16[1040,128]{1,0:T(8,128)(2,1)S(1)}, bf16[1040,128]{1,0:T(8,128)(2,1)S(1)}, u32[]{:S(2)}, u32[]{:S(2)}) %collective-permute-start.5) | collective-permute-done | bytes 266272 | tf_op jit(solution)/shard_map/ppermute | solution.py:160
  25.7 1.3 %collective-permute-start.3 = (bf16[1040,128]{1,0:T(8,128)(2,1)S(1)}, bf16[1040,128]{1,0:T(8,128)(2,1)S(1)}, u32[]{:S(2)}, u32[]{:S(2)}) collective-permute-start(bf16[1040,128]{1,0:T(8,128)(2,1)S(1)} %shard_map.47), channel_id=1, source_target_pairs={{0,1},{1,2},{2,3},{3,0},{4,5},{5,6},{6,7},{7,4},{8,9},{9,10},{10,1... | collective-permute-start | bytes 798728 | tf_op jit(solution)/shard_map/ppermute | solution.py:160
  27.1 5.3 %collective-permute-done.4.refs_6_ = bf16[1040,128]{1,0:T(8,128)(2,1)S(1)} collective-permute-done((bf16[1040,128]{1,0:T(8,128)(2,1)S(1)}, bf16[1040,128]{1,0:T(8,128)(2,1)S(1)}, u32[]{:S(2)}, u32[]{:S(2)}) %collective-permute-start.4) | collective-permute-done | bytes 266272 | tf_op jit(solution)/shard_map/ppermute | solution.py:160
  32.3 0.3 collective-permute-done.3.refs_5_
  32.6 0.1 shard_map.48
  32.7 6.8 %collective-permute-start.8 = (bf16[4160,128]{1,0:T(8,128)(2,1)S(1)}, bf16[4160,128]{1,0:T(8,128)(2,1)S(1)}, u32[]{:S(2)}, u32[]{:S(2)}) collective-permute-start(bf16[4160,128]{1,0:T(8,128)(2,1)S(1)} %get-tuple-element.14), channel_id=1, source_target_pairs={{0,4},{4,0},{1,5},{5,1},{2,6},{6,2},{3,7},{7,3},{8,12},{12,8},{9,1... | collective-permute-start | bytes 3194888 | tf_op jit(solution)/shard_map/ppermute | solution.py:149
  39.6 0.0 collective-permute-done.11.refs_6_
  39.6 0.1 collective-permute-start.12
  39.7 1.8 %collective-permute-done.7.refs_2_ = bf16[4160,128]{1,0:T(8,128)(2,1)S(1)} collective-permute-done((bf16[4160,128]{1,0:T(8,128)(2,1)S(1)}, bf16[4160,128]{1,0:T(8,128)(2,1)S(1)}, u32[]{:S(2)}, u32[]{:S(2)}) %collective-permute-start.7) | collective-permute-done | bytes 1064992 | tf_op jit(solution)/shard_map/ppermute | solution.py:161
  41.5 3.5 %collective-permute-start.10 = (bf16[4160,128]{1,0:T(8,128)(2,1)S(1)}, bf16[4160,128]{1,0:T(8,128)(2,1)S(1)}, u32[]{:S(2)}, u32[]{:S(2)}) collective-permute-start(bf16[4160,128]{1,0:T(8,128)(2,1)S(1)} %collective-permute-done.7.refs_2_), channel_id=1, source_target_pairs={{0,4},{4,0},{1,5},{5,1},{2,6},{6,2},{3,7},{7,3},{8,12},{12,8},{9,1... | collective-permute-start | bytes 3194888 | tf_op jit(solution)/shard_map/ppermute | solution.py:149
  45.0 0.0 collective-permute-done.6.refs_1_
  45.0 0.0 collective-permute-start.9
  45.0 0.0 collective-permute-done.8.refs_3_
  45.0 0.0 collective-permute-done.12.refs_7_
  45.1 2.3 %collective-permute-done.10.refs_5_ = bf16[4160,128]{1,0:T(8,128)(2,1)S(1)} collective-permute-done((bf16[4160,128]{1,0:T(8,128)(2,1)S(1)}, bf16[4160,128]{1,0:T(8,128)(2,1)S(1)}, u32[]{:S(2)}, u32[]{:S(2)}) %collective-permute-start.10) | collective-permute-done | bytes 1064992 | tf_op jit(solution)/shard_map/ppermute | solution.py:149
  47.3 1.5 %collective-permute-done.9.refs_4_ = bf16[4160,128]{1,0:T(8,128)(2,1)S(1)} collective-permute-done((bf16[4160,128]{1,0:T(8,128)(2,1)S(1)}, bf16[4160,128]{1,0:T(8,128)(2,1)S(1)}, u32[]{:S(2)}, u32[]{:S(2)}) %collective-permute-start.9) | collective-permute-done | bytes 1064992 | tf_op jit(solution)/shard_map/ppermute | solution.py:149
  48.9 0.0 copy-done.3
  48.9 0.0 copy-start.1
  48.9 3.3 %shard_map.49 = (f32[264,128]{1,0:T(8,128)S(1)}, f32[264,128]{1,0:T(8,128)S(1)}, f32[264,128]{1,0:T(8,128)S(1)}, f32[264,128]{1,0:T(8,128)S(1)}) custom-call(s32[2,1,4]{2,1,0:T(1,128)S(1)} %copy-done.3, bf16[2,16,128,128]{3,2,1,0:T(8,128)(2,1)S(1)} %get-tuple-element.12.tiles_ref, s32[32,128]{1,0:T(8,128)S(1)} %get-tuple-element.13.right_ids_ref, ...), custom_call_target="tpu_custom_call" | custom-call | flops 536870912 | bytes 10485760 | tf_op jit(solution)/shard_map/pallas_call | solution.py:178
  52.2 1.4 %collective-permute-start.13 = (f32[264,128]{1,0:T(8,128)S(1)}, f32[264,128]{1,0:T(8,128)S(1)}, u32[]{:S(2)}, u32[]{:S(2)}) collective-permute-start(f32[264,128]{1,0:T(8,128)S(1)} %get-tuple-element.16), channel_id=1, source_target_pairs={{0,1},{1,2},{2,3},{3,0},{4,5},{5,6},{6,7},{7,4},{8,9},{9,10},{10,1... | collective-permute-start | bytes 405512 | tf_op jit(solution)/shard_map/ppermute | solution.py:195
  53.6 2.6 %collective-permute-start.14 = (f32[264,128]{1,0:T(8,128)S(1)}, f32[264,128]{1,0:T(8,128)S(1)}, u32[]{:S(2)}, u32[]{:S(2)}) collective-permute-start(f32[264,128]{1,0:T(8,128)S(1)} %get-tuple-element.17), channel_id=1, source_target_pairs={{0,2},{1,3},{2,0},{3,1},{4,6},{5,7},{6,4},{7,5},{8,10},{9,11},{10,... | collective-permute-start | bytes 405512 | tf_op jit(solution)/shard_map/ppermute | solution.py:195
  56.2 1.1 %collective-permute-start.15 = (f32[264,128]{1,0:T(8,128)S(1)}, f32[264,128]{1,0:T(8,128)S(1)}, u32[]{:S(2)}, u32[]{:S(2)}) collective-permute-start(f32[264,128]{1,0:T(8,128)S(1)} %get-tuple-element.18), channel_id=1, source_target_pairs={{0,3},{1,0},{2,1},{3,2},{4,7},{5,4},{6,5},{7,6},{8,11},{9,8},{10,9... | collective-permute-start | bytes 405512 | tf_op jit(solution)/shard_map/ppermute | solution.py:195
  57.3 1.1 %collective-permute-done.13.refs_1_ = f32[264,128]{1,0:T(8,128)S(1)} collective-permute-done((f32[264,128]{1,0:T(8,128)S(1)}, f32[264,128]{1,0:T(8,128)S(1)}, u32[]{:S(2)}, u32[]{:S(2)}) %collective-permute-start.13) | collective-permute-done | bytes 135200 | tf_op jit(solution)/shard_map/ppermute | solution.py:195
  58.4 4.0 %collective-permute-done.14.refs_2_ = f32[264,128]{1,0:T(8,128)S(1)} collective-permute-done((f32[264,128]{1,0:T(8,128)S(1)}, f32[264,128]{1,0:T(8,128)S(1)}, u32[]{:S(2)}, u32[]{:S(2)}) %collective-permute-start.14) | collective-permute-done | bytes 135200 | tf_op jit(solution)/shard_map/ppermute | solution.py:195
  62.4 0.0 collective-permute-done.15.refs_3_
  62.4 0.0 copy-done.1
  62.4 0.8 %shard_map.50 = bf16[2,4,1,128,128]{4,3,2,1,0:T(8,128)(2,1)} custom-call(s32[2,4,128]{2,1,0:T(4,128)S(1)} %copy-done.1, f32[264,128]{1,0:T(8,128)S(1)} %get-tuple-element.15.refs_0_, f32[264,128]{1,0:T(8,128)S(1)} %collective-permute-done.13.refs_1_, f32[264,128]{1,0:T(8,128)S(1)} %collective-permute-done.14.refs_2_, ...), custom_call_target="tpu_custom_call" | custom-call | tf_op jit(solution)/shard_map/pallas_call | solution.py:196
  (1 shorter events, 0.0 us)
Async XLA Ops:
  0.0 0.9 %copy-start = (bf16[2,1,4,128,128]{4,3,2,1,0:T(8,128)(2,1)S(1)}, bf16[2,1,4,128,128]{4,3,2,1,0:T(8,128)(2,1)}, u32[]{:S(2)}) copy-start(bf16[2,1,4,128,128]{4,3,2,1,0:T(8,128)(2,1)} %tiles_ref.1) | copy-start | bytes 786436
  1.0 0.7 %copy-start.2 = (s32[2,1,4]{2,1,0:T(1,128)S(1)}, s32[2,1,4]{2,1,0:T(1,128)}, u32[]{:S(2)}) copy-start(s32[2,1,4]{2,1,0:T(1,128)} %rows_ref.1) | copy-start | bytes 100
  2.2 8.6 %collective-permute-start.2 = (bf16[1040,128]{1,0:T(8,128)(2,1)S(1)}, bf16[1040,128]{1,0:T(8,128)(2,1)S(1)}, u32[]{:S(2)}, u32[]{:S(2)}) collective-permute-start(bf16[1040,128]{1,0:T(8,128)(2,1)S(1)} %shard_map.46.unit_ref.refs_0_.refs_4_), channel_id=1, source_target_pairs={{0,64},{4,20},{8,72},{12,28},{16,80},{20,4},{24,88},{28,12},{32,96... | collective-permute-start | bytes 798728 | tf_op jit(solution)/shard_map/ppermute | solution.py:151
  6.7 7.7 %collective-permute-start.1 = (bf16[1040,128]{1,0:T(8,128)(2,1)S(1)}, bf16[1040,128]{1,0:T(8,128)(2,1)S(1)}, u32[]{:S(2)}, u32[]{:S(2)}) collective-permute-start(bf16[1040,128]{1,0:T(8,128)(2,1)S(1)} %shard_map.46.unit_ref.refs_0_.refs_4_), channel_id=1, source_target_pairs={{0,96},{4,28},{8,104},{12,4},{16,112},{20,12},{24,120},{28,20},{32... | collective-permute-start | bytes 798728 | tf_op jit(solution)/shard_map/ppermute | solution.py:151
  7.2 7.3 %collective-permute-start = (bf16[1040,128]{1,0:T(8,128)(2,1)S(1)}, bf16[1040,128]{1,0:T(8,128)(2,1)S(1)}, u32[]{:S(2)}, u32[]{:S(2)}) collective-permute-start(bf16[1040,128]{1,0:T(8,128)(2,1)S(1)} %shard_map.46.unit_ref.refs_0_.refs_4_), channel_id=1, source_target_pairs={{0,32},{4,12},{8,40},{12,20},{16,48},{20,28},{24,56},{28,4},{32,64... | collective-permute-start | bytes 798728 | tf_op jit(solution)/shard_map/ppermute | solution.py:151
  14.5 25.0 %collective-permute-start.11 = (bf16[4160,128]{1,0:T(8,128)(2,1)S(1)}, bf16[4160,128]{1,0:T(8,128)(2,1)S(1)}, u32[]{:S(2)}, u32[]{:S(2)}) collective-permute-start(bf16[4160,128]{1,0:T(8,128)(2,1)S(1)} %pad_maximum_fusion.refs_0_), channel_id=1, source_target_pairs={{0,16},{4,68},{8,24},{12,76},{16,0},{20,84},{24,8},{28,92},{32,48}... | collective-permute-start | bytes 3194888 | tf_op jit(solution)/shard_map/ppermute | solution.py:173
  17.1 24.4 %collective-permute-start.7 = (bf16[4160,128]{1,0:T(8,128)(2,1)S(1)}, bf16[4160,128]{1,0:T(8,128)(2,1)S(1)}, u32[]{:S(2)}, u32[]{:S(2)}) collective-permute-start(bf16[4160,128]{1,0:T(8,128)(2,1)S(1)} %pad_maximum_fusion.refs_0_), channel_id=1, source_target_pairs={{0,24},{4,100},{8,0},{12,108},{16,8},{20,116},{24,16},{28,124},{32... | collective-permute-start | bytes 3194888 | tf_op jit(solution)/shard_map/ppermute | solution.py:161
  18.0 27.1 %collective-permute-start.6 = (bf16[4160,128]{1,0:T(8,128)(2,1)S(1)}, bf16[4160,128]{1,0:T(8,128)(2,1)S(1)}, u32[]{:S(2)}, u32[]{:S(2)}) collective-permute-start(bf16[4160,128]{1,0:T(8,128)(2,1)S(1)} %pad_maximum_fusion.refs_0_), channel_id=1, source_target_pairs={{0,8},{4,36},{8,16},{12,44},{16,24},{20,52},{24,0},{28,60},{32,40}... | collective-permute-start | bytes 3194888 | tf_op jit(solution)/shard_map/ppermute | solution.py:161
  18.6 30.3 %copy-start.3 = (s32[2,1,4]{2,1,0:T(1,128)S(1)}, s32[2,1,4]{2,1,0:T(1,128)}, u32[]{:S(2)}) copy-start(s32[2,1,4]{2,1,0:T(1,128)} %kept_ref.1) | copy-start | bytes 100
  18.6 7.1 %collective-permute-start.5 = (bf16[1040,128]{1,0:T(8,128)(2,1)S(1)}, bf16[1040,128]{1,0:T(8,128)(2,1)S(1)}, u32[]{:S(2)}, u32[]{:S(2)}) collective-permute-start(bf16[1040,128]{1,0:T(8,128)(2,1)S(1)} %shard_map.47), channel_id=1, source_target_pairs={{0,2},{1,3},{2,0},{3,1},{4,6},{5,7},{6,4},{7,5},{8,10},{9,11},{10,... | collective-permute-start | bytes 798728 | tf_op jit(solution)/shard_map/ppermute | solution.py:160
  21.6 10.8 %collective-permute-start.4 = (bf16[1040,128]{1,0:T(8,128)(2,1)S(1)}, bf16[1040,128]{1,0:T(8,128)(2,1)S(1)}, u32[]{:S(2)}, u32[]{:S(2)}) collective-permute-start(bf16[1040,128]{1,0:T(8,128)(2,1)S(1)} %shard_map.47), channel_id=1, source_target_pairs={{0,3},{1,0},{2,1},{3,2},{4,7},{5,4},{6,5},{7,6},{8,11},{9,8},{10,9... | collective-permute-start | bytes 798728 | tf_op jit(solution)/shard_map/ppermute | solution.py:160
  25.7 6.9 %collective-permute-start.3 = (bf16[1040,128]{1,0:T(8,128)(2,1)S(1)}, bf16[1040,128]{1,0:T(8,128)(2,1)S(1)}, u32[]{:S(2)}, u32[]{:S(2)}) collective-permute-start(bf16[1040,128]{1,0:T(8,128)(2,1)S(1)} %shard_map.47), channel_id=1, source_target_pairs={{0,1},{1,2},{2,3},{3,0},{4,5},{5,6},{6,7},{7,4},{8,9},{9,10},{10,1... | collective-permute-start | bytes 798728 | tf_op jit(solution)/shard_map/ppermute | solution.py:160
  32.7 12.3 %collective-permute-start.8 = (bf16[4160,128]{1,0:T(8,128)(2,1)S(1)}, bf16[4160,128]{1,0:T(8,128)(2,1)S(1)}, u32[]{:S(2)}, u32[]{:S(2)}) collective-permute-start(bf16[4160,128]{1,0:T(8,128)(2,1)S(1)} %get-tuple-element.14), channel_id=1, source_target_pairs={{0,4},{4,0},{1,5},{5,1},{2,6},{6,2},{3,7},{7,3},{8,12},{12,8},{9,1... | collective-permute-start | bytes 3194888 | tf_op jit(solution)/shard_map/ppermute | solution.py:149
  39.6 5.5 %collective-permute-start.12 = (bf16[4160,128]{1,0:T(8,128)(2,1)S(1)}, bf16[4160,128]{1,0:T(8,128)(2,1)S(1)}, u32[]{:S(2)}, u32[]{:S(2)}) collective-permute-start(bf16[4160,128]{1,0:T(8,128)(2,1)S(1)} %collective-permute-done.11.refs_6_), channel_id=1, source_target_pairs={{0,4},{4,0},{1,5},{5,1},{2,6},{6,2},{3,7},{7,3},{8,12},{12,8},{9,1... | collective-permute-start | bytes 3194888 | tf_op jit(solution)/shard_map/ppermute | solution.py:149
  41.5 5.9 %collective-permute-start.10 = (bf16[4160,128]{1,0:T(8,128)(2,1)S(1)}, bf16[4160,128]{1,0:T(8,128)(2,1)S(1)}, u32[]{:S(2)}, u32[]{:S(2)}) collective-permute-start(bf16[4160,128]{1,0:T(8,128)(2,1)S(1)} %collective-permute-done.7.refs_2_), channel_id=1, source_target_pairs={{0,4},{4,0},{1,5},{5,1},{2,6},{6,2},{3,7},{7,3},{8,12},{12,8},{9,1... | collective-permute-start | bytes 3194888 | tf_op jit(solution)/shard_map/ppermute | solution.py:149
  45.0 3.8 %collective-permute-start.9 = (bf16[4160,128]{1,0:T(8,128)(2,1)S(1)}, bf16[4160,128]{1,0:T(8,128)(2,1)S(1)}, u32[]{:S(2)}, u32[]{:S(2)}) collective-permute-start(bf16[4160,128]{1,0:T(8,128)(2,1)S(1)} %collective-permute-done.6.refs_1_), channel_id=1, source_target_pairs={{0,4},{4,0},{1,5},{5,1},{2,6},{6,2},{3,7},{7,3},{8,12},{12,8},{9,1... | collective-permute-start | bytes 3194888 | tf_op jit(solution)/shard_map/ppermute | solution.py:149
  48.9 13.5 %copy-start.1 = (s32[2,4,128]{2,1,0:T(4,128)S(1)}, s32[2,4,128]{2,1,0:T(4,128)}, u32[]{:S(2)}) copy-start(s32[2,4,128]{2,1,0:T(4,128)} %mask_ref.1) | copy-start | bytes 12292
  52.2 6.2 %collective-permute-start.13 = (f32[264,128]{1,0:T(8,128)S(1)}, f32[264,128]{1,0:T(8,128)S(1)}, u32[]{:S(2)}, u32[]{:S(2)}) collective-permute-start(f32[264,128]{1,0:T(8,128)S(1)} %get-tuple-element.16), channel_id=1, source_target_pairs={{0,1},{1,2},{2,3},{3,0},{4,5},{5,6},{6,7},{7,4},{8,9},{9,10},{10,1... | collective-permute-start | bytes 405512 | tf_op jit(solution)/shard_map/ppermute | solution.py:195
  53.6 8.8 %collective-permute-start.14 = (f32[264,128]{1,0:T(8,128)S(1)}, f32[264,128]{1,0:T(8,128)S(1)}, u32[]{:S(2)}, u32[]{:S(2)}) collective-permute-start(f32[264,128]{1,0:T(8,128)S(1)} %get-tuple-element.17), channel_id=1, source_target_pairs={{0,2},{1,3},{2,0},{3,1},{4,6},{5,7},{6,4},{7,5},{8,10},{9,11},{10,... | collective-permute-start | bytes 405512 | tf_op jit(solution)/shard_map/ppermute | solution.py:195
  56.2 6.2 %collective-permute-start.15 = (f32[264,128]{1,0:T(8,128)S(1)}, f32[264,128]{1,0:T(8,128)S(1)}, u32[]{:S(2)}, u32[]{:S(2)}) collective-permute-start(f32[264,128]{1,0:T(8,128)S(1)} %get-tuple-element.18), channel_id=1, source_target_pairs={{0,3},{1,0},{2,1},{3,2},{4,7},{5,4},{6,5},{7,6},{8,11},{9,8},{10,9... | collective-permute-start | bytes 405512 | tf_op jit(solution)/shard_map/ppermute | solution.py:195

commit v4 on v2

--- a/solution.py
+++ b/solution.py
@@ -19,6 +19,7 @@
 CHUNK = PANELS * TILE + 8
 CELL = ("x", "z", "core")
 VMEM = pl.BlockSpec(memory_space=pltpu.VMEM)
+HBM = pl.BlockSpec(memory_space=pltpu.HBM)
 SMEM = pl.BlockSpec(memory_space=pltpu.SMEM)
 LIMIT = pltpu.CompilerParams(vmem_limit_bytes=40 * 1024 * 1024)
 
@@ -37,23 +38,48 @@
     return pairs
 
 
-def pack_kernel(rows_ref, tiles_ref, unit_ref):
+def pack_kernel(rows_ref, tiles_ref, unit_ref, rows, sems):
+    tiles_copies = [
+        pltpu.make_async_copy(
+            tiles_ref.at[j, 0, k], unit_ref.at[pl.ds((j * SLOTS + k) * TILE, TILE)], sems.at[j * SLOTS + k]
+        )
+        for j in range(PANELS)
+        for k in range(SLOTS)
+    ]
+    rows_copy = pltpu.make_async_copy(rows_ref, rows, sems.at[PANELS * SLOTS])
+    rows_copy.start()
+    for copy in tiles_copies:
+        copy.start()
     band = lax.axis_index("layer")
     cell = (lax.axis_index("x") * 4 + lax.axis_index("z")) * 2 + lax.axis_index("core")
-    unit_ref[:BODY] = tiles_ref[...].reshape(BODY, TILE)
     lane = lax.broadcasted_iota(jnp.int32, (16, TILE), 1)
     ids = jnp.zeros((16, TILE), jnp.int32)
     for j in range(PANELS):
+        ids = jnp.where(lane == 8 * j + 4, cell * PANELS + j, ids)
+    rows_copy.wait()
+    for j in range(PANELS):
         for k in range(SLOTS):
-            ids = jnp.where(lane == 8 * j + k, rows_ref[j, 0, k] + BLOCKS * band, ids)
-        ids = jnp.where(lane == 8 * j + 4, cell * PANELS + j, ids)
+            ids = jnp.where(lane == 8 * j + k, rows[j, 0, k] + BLOCKS * band, ids)
     unit_ref[BODY:] = ids.astype(jnp.float32).astype(jnp.bfloat16)
-
-
-def join_kernel(*refs):
-    line_refs, right_refs, (line_ref, tiles_ref, ids_ref) = refs[:LINE], refs[LINE : LINE + BANDS], refs[LINE + BANDS :]
-    for u, ref in enumerate(line_refs):
-        line_ref[u * UNIT : (u + 1) * UNIT] = ref[...]
+    for copy in tiles_copies:
+        copy.wait()
+
+
+def second_kernel(*refs):
+    unit_ref, one_ref, other_ref = refs[:3]
+    second_ref, again_ref = refs[-2:]
+    second_ref[:UNIT] = one_ref[...]
+    second_ref[UNIT:] = other_ref[...]
+    again_ref[...] = unit_ref[...]
+
+
+def join_kernel(count, *refs):
+    line_refs, right_refs = refs[:count], refs[count : count + BANDS]
+    line_ref, tiles_ref, ids_ref = refs[count + BANDS :]
+    done = 0
+    for ref in line_refs:
+        line_ref[done : done + ref.shape[0]] = ref[...]
+        done += ref.shape[0]
     for b, ref in enumerate(right_refs):
         ids_ref[8 * b : 8 * b + 8] = ref[BODY:].astype(jnp.float32).astype(jnp.int32)[:8]
         for p in range(PANELS):
@@ -133,35 +159,50 @@
     unit = pl.pallas_call(
         pack_kernel,
         out_shape=jax.ShapeDtypeStruct((UNIT, TILE), jnp.bfloat16),
-        in_specs=[SMEM, VMEM],
+        in_specs=[HBM, HBM],
         out_specs=VMEM,
+        scratch_shapes=[
+            pltpu.SMEM((PANELS, 1, SLOTS), jnp.int32),
+            pltpu.SemaphoreType.DMA((PANELS * SLOTS + 1,)),
+        ],
         compiler_params=LIMIT,
     )(band_rows, tile_values)
 
     def swap(value):
         return lax.ppermute(value, "core", [(0, 1), (1, 0)])
 
-    def swap(value):
-        return lax.ppermute(value, "core", [(0, 1), (1, 0)])
-
-    lines = [lax.ppermute(unit, CELL, cells(a, b)) for a, b in (((1, 0), (0, 1)), ((3, 0), (0, 3)), ((2, 0), (0, 2)))]
-    line = jnp.concatenate([unit, *lines], axis=0)
-    rights = [unit] + [lax.ppermute(unit, "layer", ring(s)) for s in (1, 3, 2)]
-    up, down = [lax.ppermute(line, CELL, cells(a, b)) for a, b in (((0, 1), (1, 0)), ((0, 3), (3, 0)))]
+    def along(value, axis, shift):
+        steps = ((shift, 0), (0, shift))
+        return lax.ppermute(value, CELL, cells(steps[axis], steps[1 - axis]))
+
+    near, back, away = [along(unit, 0, shift) for shift in (2, 1, 3)]
+    first = jnp.concatenate([unit, near], axis=0)
+    rights = [lax.ppermute(unit, "layer", ring(s)) for s in (1, 3)]
+    second, unit_again = pl.pallas_call(
+        second_kernel,
+        out_shape=[jax.ShapeDtypeStruct((n * UNIT, TILE), jnp.bfloat16) for n in (2, 1)],
+        in_specs=[VMEM] * (3 + 2),
+        out_specs=[VMEM] * 2,
+        compiler_params=LIMIT,
+    )(unit, back, away, *rights)
+    rights = [unit, *rights, lax.ppermute(unit_again, "layer", ring(2))]
     line_again, tiles, right_ids = pl.pallas_call(
-        join_kernel,
+        functools.partial(join_kernel, 2),
         out_shape=[
             jax.ShapeDtypeStruct((LINE * UNIT, TILE), jnp.bfloat16),
             jax.ShapeDtypeStruct((PANELS, BANDS * SLOTS, TILE, TILE), jnp.bfloat16),
             jax.ShapeDtypeStruct((8 * BANDS, TILE), jnp.int32),
         ],
-        in_specs=[VMEM] * (LINE + BANDS),
+        in_specs=[VMEM] * (2 + BANDS),
         out_specs=[VMEM] * 3,
         compiler_params=LIMIT,
-    )(unit, *lines, *rights)
-    far = lax.ppermute(line_again, CELL, cells((0, 2), (2, 0)))
-
-    lefts = [line, up, down, swap(line), swap(up), swap(down), far, swap(far)]
+    )(first, second, *rights)
+    up, down = along(first, 1, 1), along(first, 1, 3)
+    up_b, down_b = along(second, 1, 1), along(second, 1, 3)
+    fars = [along(up[:UNIT], 1, 1), along(down[UNIT:], 1, 3)]
+    fars_b = [along(up_b[:UNIT], 1, 1), along(down_b[UNIT:], 1, 3)]
+    parts = [*fars_b, *fars, up_b, down_b, up, down]
+    lefts = [first, second, *parts, swap(line_again), *[swap(one) for one in parts]]
     counts = tuple(one.shape[0] // UNIT for one in lefts)
     units = sum(counts)
     chunks = pl.pallas_call(

time: 70.1 us -> 61.3 us (0.87); the launches traced: 70 us -> 60.3 us
  waiting for transfers between devices: 30.2 us -> 19.1 us
  starting transfers between devices: 33.2 us -> 34 us
    ppermute x9 -> x14, waiting for transfers between devices: 21.2 us -> 10.4 us  [the longest x11 9.54 us: along(): return lax.ppermute(value, CELL, cells(steps[axis], steps[1 - axis]))]
    ppermute x9 -> x14, starting transfers between devices: 15 us -> 21.4 us  [the longest x11 16.1 us: along(): return lax.ppermute(value, CELL, cells(steps[axis], steps[1 - axis]))]
    ppermute x4 -> x9, starting transfers between devices: 13.1 us -> 8.78 us  [swap(): return lax.ppermute(value, 'core', [(0, 1), (1, 0)])]
    ppermute x3, starting transfers between devices: 5.09 us -> 3.84 us  [per_device(): lax.ppermute(chunks[s], 'layer', ring(s))]
    ppermute x4 -> x9, waiting for transfers between devices: 3.82 us -> 3.35 us  [swap(): return lax.ppermute(value, 'core', [(0, 1), (1, 0)])]
  transfers between devices with their start and end apart: 16 -> 26, of which waited for: 11 -> 11; matrix products, arithmetic and copies ran while one was open for 0% -> 0% of each run, Pallas kernels for 0% -> 0%
where the time goes in v4:
time: 61.3 us; the launch traced here: 60.3 us
  starting transfers between devices  34 us (55%)
  waiting for transfers between devices  19.1 us (31%)
  Pallas kernels  5.24 us (9%)
  local copies, waits for them, and re-layouts  1.72 us (3%)
    ppermute x11, starting transfers between devices, along(): return lax.ppermute(value, CELL, cells(steps[axis], steps[1 - axis]))  16.1 us
    ppermute x11, waiting for transfers between devices, along(): return lax.ppermute(value, CELL, cells(steps[axis], steps[1 - axis]))  9.54 us
    ppermute x9, starting transfers between devices, swap(): return lax.ppermute(value, 'core', [(0, 1), (1, 0)])  8.78 us
    ppermute x3, waiting for transfers between devices, per_device(): lax.ppermute(chunks[s], 'layer', ring(s))  5.39 us
    ppermute x3, starting transfers between devices, per_device(): lax.ppermute(chunks[s], 'layer', ring(s))  3.84 us
    ppermute x2, starting transfers between devices, per_device(): rights = [lax.ppermute(unit, 'layer', ring(s)) for s in (1, 3)]  3.71 us
    pallas_call x1, Pallas kernels, per_device(): pl.pallas_call(functools.partial(expand_kernel, counts), out_shape=[jax.S...  3.61 us
    ppermute x9, waiting for transfers between devices, swap(): return lax.ppermute(value, 'core', [(0, 1), (1, 0)])  3.35 us
  transfers between devices with their start and end apart: 26, of which 11 were waited for; matrix products, arithmetic and copies ran while one was open for 0% of the time, Pallas kernels for 0%

profile of v4, /device:TPU:1, one launch (start us, length us, event | category | flops | bytes accessed | tf_op | source)
XLA Modules:
  0.0 60.3 jit_solution(5854716752025947128)
XLA Ops:
  0.0 0.9 %copy-done = bf16[2,1,4,128,128]{4,3,2,1,0:T(8,128)(2,1)S(1)} copy-done((bf16[2,1,4,128,128]{4,3,2,1,0:T(8,128)(2,1)S(1)}, bf16[2,1,4,128,128]{4,3,2,1,0:T(8,128)(2,1)}, u32[]{:S(2)}) %copy-start) | copy-done | bytes 262168
  1.0 0.7 %copy-done.2 = s32[2,1,4]{2,1,0:T(1,128)S(1)} copy-done((s32[2,1,4]{2,1,0:T(1,128)S(1)}, s32[2,1,4]{2,1,0:T(1,128)}, u32[]{:S(2)}) %copy-start.2) | copy-done | bytes 56
  1.6 0.7 %shard_map.46.refs_0_.refs_2_ = bf16[1040,128]{1,0:T(8,128)(2,1)S(1)} custom-call(s32[2,1,4]{2,1,0:T(1,128)S(1)} %copy-done.2, bf16[2,1,4,128,128]{4,3,2,1,0:T(8,128)(2,1)S(1)} %copy-done), custom_call_target="tpu_custom_call" | custom-call | tf_op jit(solution)/shard_map/pallas_call | solution.py:159
  2.3 2.2 %collective-permute-start.3 = (bf16[1040,128]{1,0:T(8,128)(2,1)S(1)}, bf16[1040,128]{1,0:T(8,128)(2,1)S(1)}, u32[]{:S(2)}, u32[]{:S(2)}) collective-permute-start(bf16[1040,128]{1,0:T(8,128)(2,1)S(1)} %shard_map.46.refs_0_.refs_2_), channel_id=1, source_target_pairs={{0,1},{1,2},{2,3},{3,0},{4,5},{5,6},{6,7},{7,4},{8,9},{9,10},{10,1... | collective-permute-start | bytes 798728 | tf_op jit(solution)/shard_map/ppermute | solution.py:180
  4.5 1.5 %collective-permute-start.4 = (bf16[1040,128]{1,0:T(8,128)(2,1)S(1)}, bf16[1040,128]{1,0:T(8,128)(2,1)S(1)}, u32[]{:S(2)}, u32[]{:S(2)}) collective-permute-start(bf16[1040,128]{1,0:T(8,128)(2,1)S(1)} %shard_map.46.refs_0_.refs_2_), channel_id=1, source_target_pairs={{0,3},{1,0},{2,1},{3,2},{4,7},{5,4},{6,5},{7,6},{8,11},{9,8},{10,9... | collective-permute-start | bytes 798728 | tf_op jit(solution)/shard_map/ppermute | solution.py:180
  6.0 1.6 %collective-permute-start.1 = (bf16[1040,128]{1,0:T(8,128)(2,1)S(1)}, bf16[1040,128]{1,0:T(8,128)(2,1)S(1)}, u32[]{:S(2)}, u32[]{:S(2)}) collective-permute-start(bf16[1040,128]{1,0:T(8,128)(2,1)S(1)} %shard_map.46.refs_0_.refs_2_), channel_id=1, source_target_pairs={{0,32},{4,12},{8,40},{12,20},{16,48},{20,28},{24,56},{28,4},{32,64... | collective-permute-start | bytes 798728 | tf_op jit(solution)/shard_map/ppermute | solution.py:176
  7.6 2.1 %collective-permute-start.2 = (bf16[1040,128]{1,0:T(8,128)(2,1)S(1)}, bf16[1040,128]{1,0:T(8,128)(2,1)S(1)}, u32[]{:S(2)}, u32[]{:S(2)}) collective-permute-start(bf16[1040,128]{1,0:T(8,128)(2,1)S(1)} %shard_map.46.refs_0_.refs_2_), channel_id=1, source_target_pairs={{0,96},{4,28},{8,104},{12,4},{16,112},{20,12},{24,120},{28,20},{32... | collective-permute-start | bytes 798728 | tf_op jit(solution)/shard_map/ppermute | solution.py:176
  9.8 1.3 %collective-permute-start = (bf16[1040,128]{1,0:T(8,128)(2,1)S(1)}, bf16[1040,128]{1,0:T(8,128)(2,1)S(1)}, u32[]{:S(2)}, u32[]{:S(2)}) collective-permute-start(bf16[1040,128]{1,0:T(8,128)(2,1)S(1)} %shard_map.46.refs_0_.refs_2_), channel_id=1, source_target_pairs={{0,64},{4,20},{8,72},{12,28},{16,80},{20,4},{24,88},{28,12},{32,96... | collective-permute-start | bytes 798728 | tf_op jit(solution)/shard_map/ppermute | solution.py:176
  11.1 0.8 %collective-permute-done.3.refs_3_ = bf16[1040,128]{1,0:T(8,128)(2,1)S(1)} collective-permute-done((bf16[1040,128]{1,0:T(8,128)(2,1)S(1)}, bf16[1040,128]{1,0:T(8,128)(2,1)S(1)}, u32[]{:S(2)}, u32[]{:S(2)}) %collective-permute-start.3) | collective-permute-done | bytes 266272 | tf_op jit(solution)/shard_map/ppermute | solution.py:180
  11.9 0.0 collective-permute-done.4.refs_4_
  11.9 2.0 %collective-permute-done.1.refs_1_ = bf16[1040,128]{1,0:T(8,128)(2,1)S(1)} collective-permute-done((bf16[1040,128]{1,0:T(8,128)(2,1)S(1)}, bf16[1040,128]{1,0:T(8,128)(2,1)S(1)}, u32[]{:S(2)}, u32[]{:S(2)}) %collective-permute-start.1) | collective-permute-done | bytes 266272 | tf_op jit(solution)/shard_map/ppermute | solution.py:176
  13.9 2.1 %collective-permute-done.2.refs_2_ = bf16[1040,128]{1,0:T(8,128)(2,1)S(1)} collective-permute-done((bf16[1040,128]{1,0:T(8,128)(2,1)S(1)}, bf16[1040,128]{1,0:T(8,128)(2,1)S(1)}, u32[]{:S(2)}, u32[]{:S(2)}) %collective-permute-start.2) | collective-permute-done | bytes 266272 | tf_op jit(solution)/shard_map/ppermute | solution.py:176
  16.0 0.1 shard_map.47
  16.0 1.3 %collective-permute-start.6 = (bf16[2080,128]{1,0:T(8,128)(2,1)S(1)}, bf16[2080,128]{1,0:T(8,128)(2,1)S(1)}, u32[]{:S(2)}, u32[]{:S(2)}) collective-permute-start(bf16[2080,128]{1,0:T(8,128)(2,1)S(1)} %get-tuple-element.14.refs_1_), channel_id=1, source_target_pairs={{0,8},{4,36},{8,16},{12,44},{16,24},{20,52},{24,0},{28,60},{32,40}... | collective-permute-start | bytes 1597448 | tf_op jit(solution)/shard_map/ppermute | solution.py:176
  17.3 1.5 %collective-permute-start.8 = (bf16[2080,128]{1,0:T(8,128)(2,1)S(1)}, bf16[2080,128]{1,0:T(8,128)(2,1)S(1)}, u32[]{:S(2)}, u32[]{:S(2)}) collective-permute-start(bf16[2080,128]{1,0:T(8,128)(2,1)S(1)} %get-tuple-element.14.refs_1_), channel_id=1, source_target_pairs={{0,24},{4,100},{8,0},{12,108},{16,8},{20,116},{24,16},{28,124},{32... | collective-permute-start | bytes 1597448 | tf_op jit(solution)/shard_map/ppermute | solution.py:176
  18.8 0.1 collective-permute-start.10
  18.9 2.7 %collective-permute-start.12 = (bf16[2080,128]{1,0:T(8,128)(2,1)S(1)}, bf16[2080,128]{1,0:T(8,128)(2,1)S(1)}, u32[]{:S(2)}, u32[]{:S(2)}) collective-permute-start(bf16[2080,128]{1,0:T(8,128)(2,1)S(1)} %pad_maximum_fusion.refs_0_), channel_id=1, source_target_pairs={{0,24},{4,100},{8,0},{12,108},{16,8},{20,116},{24,16},{28,124},{32... | collective-permute-start | bytes 1597448 | tf_op jit(solution)/shard_map/ppermute | solution.py:176
  21.6 1.6 %collective-permute-start.5 = (bf16[1040,128]{1,0:T(8,128)(2,1)S(1)}, bf16[1040,128]{1,0:T(8,128)(2,1)S(1)}, u32[]{:S(2)}, u32[]{:S(2)}) collective-permute-start(bf16[1040,128]{1,0:T(8,128)(2,1)S(1)} %get-tuple-element.15), channel_id=1, source_target_pairs={{0,2},{1,3},{2,0},{3,1},{4,6},{5,7},{6,4},{7,5},{8,10},{9,11},{10,... | collective-permute-start | bytes 798728 | tf_op jit(solution)/shard_map/ppermute | solution.py:188
  23.1 2.6 %collective-permute-done.6.refs_6_ = bf16[2080,128]{1,0:T(8,128)(2,1)S(1)} collective-permute-done((bf16[2080,128]{1,0:T(8,128)(2,1)S(1)}, bf16[2080,128]{1,0:T(8,128)(2,1)S(1)}, u32[]{:S(2)}, u32[]{:S(2)}) %collective-permute-start.6) | collective-permute-done | bytes 532512 | tf_op jit(solution)/shard_map/ppermute | solution.py:176
  25.8 0.1 collective-permute-start.7
  25.9 2.7 %collective-permute-start.9 = (bf16[1040,128]{1,0:T(8,128)(2,1)S(1)}, bf16[1040,128]{1,0:T(8,128)(2,1)S(1)}, u32[]{:S(2)}, u32[]{:S(2)}) collective-permute-start(bf16[1040,128]{1,0:T(8,128)(2,1)S(1)} %slice.17), channel_id=1, source_target_pairs={{0,24},{4,100},{8,0},{12,108},{16,8},{20,116},{24,16},{28,124},{32... | collective-permute-start | bytes 798728 | tf_op jit(solution)/shard_map/ppermute | solution.py:176
  28.6 2.8 %collective-permute-done.10.refs_8_ = bf16[2080,128]{1,0:T(8,128)(2,1)S(1)} collective-permute-done((bf16[2080,128]{1,0:T(8,128)(2,1)S(1)}, bf16[2080,128]{1,0:T(8,128)(2,1)S(1)}, u32[]{:S(2)}, u32[]{:S(2)}) %collective-permute-start.10) | collective-permute-done | bytes 532512 | tf_op jit(solution)/shard_map/ppermute | solution.py:176
  31.5 0.1 collective-permute-start.11
  31.6 0.0 copy-start.3
  31.6 2.7 %collective-permute-start.13 = (bf16[1040,128]{1,0:T(8,128)(2,1)S(1)}, bf16[1040,128]{1,0:T(8,128)(2,1)S(1)}, u32[]{:S(2)}, u32[]{:S(2)}) collective-permute-start(bf16[1040,128]{1,0:T(8,128)(2,1)S(1)} %slice.19), channel_id=1, source_target_pairs={{0,24},{4,100},{8,0},{12,108},{16,8},{20,116},{24,16},{28,124},{32... | collective-permute-start | bytes 798728 | tf_op jit(solution)/shard_map/ppermute | solution.py:176
  34.3 0.1 shard_map.48
  34.5 3.5 %collective-permute-start.14 = (bf16[4160,128]{1,0:T(8,128)(2,1)S(1)}, bf16[4160,128]{1,0:T(8,128)(2,1)S(1)}, u32[]{:S(2)}, u32[]{:S(2)}) collective-permute-start(bf16[4160,128]{1,0:T(8,128)(2,1)S(1)} %get-tuple-element.18), channel_id=1, source_target_pairs={{0,4},{4,0},{1,5},{5,1},{2,6},{6,2},{3,7},{7,3},{8,12},{12,8},{9,1... | collective-permute-start | bytes 3194888 | tf_op jit(solution)/shard_map/ppermute | solution.py:172
  37.9 0.1 collective-permute-start.19
  38.0 0.4 collective-permute-start.20
  38.5 3.5 %collective-permute-start.15 = (bf16[1040,128]{1,0:T(8,128)(2,1)S(1)}, bf16[1040,128]{1,0:T(8,128)(2,1)S(1)}, u32[]{:S(2)}, u32[]{:S(2)}) collective-permute-start(bf16[1040,128]{1,0:T(8,128)(2,1)S(1)} %collective-permute-done.7.refs_2_), channel_id=1, source_target_pairs={{0,4},{4,0},{1,5},{5,1},{2,6},{6,2},{3,7},{7,3},{8,12},{12,8},{9,1... | collective-permute-start | bytes 798728 | tf_op jit(solution)/shard_map/ppermute | solution.py:172
  42.0 0.0 collective-permute-start.16
  42.0 1.2 %collective-permute-done.15.refs_11_ = bf16[1040,128]{1,0:T(8,128)(2,1)S(1)} collective-permute-done((bf16[1040,128]{1,0:T(8,128)(2,1)S(1)}, bf16[1040,128]{1,0:T(8,128)(2,1)S(1)}, u32[]{:S(2)}, u32[]{:S(2)}) %collective-permute-start.15) | collective-permute-done | bytes 266272 | tf_op jit(solution)/shard_map/ppermute | solution.py:172
  43.2 0.4 collective-permute-start.21
  43.5 0.0 collective-permute-done.16.refs_12_
  43.5 0.4 collective-permute-start.22
  43.9 0.1 collective-permute-start.17
  44.1 0.4 collective-permute-start.18
  44.4 1.8 %collective-permute-done.17.refs_13_ = bf16[1040,128]{1,0:T(8,128)(2,1)S(1)} collective-permute-done((bf16[1040,128]{1,0:T(8,128)(2,1)S(1)}, bf16[1040,128]{1,0:T(8,128)(2,1)S(1)}, u32[]{:S(2)}, u32[]{:S(2)}) %collective-permute-start.17) | collective-permute-done | bytes 266272 | tf_op jit(solution)/shard_map/ppermute | solution.py:172
  46.2 0.4 collective-permute-done.18.refs_14_
  46.6 0.0 copy-start.1
  46.6 3.6 %shard_map.49 = (f32[264,128]{1,0:T(8,128)S(1)}, f32[264,128]{1,0:T(8,128)S(1)}, f32[264,128]{1,0:T(8,128)S(1)}, f32[264,128]{1,0:T(8,128)S(1)}) custom-call(s32[2,1,4]{2,1,0:T(1,128)S(1)} %copy-done.3, bf16[2,16,128,128]{3,2,1,0:T(8,128)(2,1)S(1)} %get-tuple-element.16.tiles_ref, s32[32,128]{1,0:T(8,128)S(1)} %get-tuple-element.17.right_ids_ref, ...), custom_call_target="tpu_custom_call" | custom-call | flops 536870912 | bytes 10485760 | tf_op jit(solution)/shard_map/pallas_call | solution.py:208
  50.3 0.2 collective-permute-start.23
  50.4 2.6 %collective-permute-start.24 = (f32[264,128]{1,0:T(8,128)S(1)}, f32[264,128]{1,0:T(8,128)S(1)}, u32[]{:S(2)}, u32[]{:S(2)}) collective-permute-start(f32[264,128]{1,0:T(8,128)S(1)} %get-tuple-element.21), channel_id=1, source_target_pairs={{0,2},{1,3},{2,0},{3,1},{4,6},{5,7},{6,4},{7,5},{8,10},{9,11},{10,... | collective-permute-start | bytes 405512 | tf_op jit(solution)/shard_map/ppermute | solution.py:225
  53.0 1.1 %collective-permute-start.25 = (f32[264,128]{1,0:T(8,128)S(1)}, f32[264,128]{1,0:T(8,128)S(1)}, u32[]{:S(2)}, u32[]{:S(2)}) collective-permute-start(f32[264,128]{1,0:T(8,128)S(1)} %get-tuple-element.22), channel_id=1, source_target_pairs={{0,3},{1,0},{2,1},{3,2},{4,7},{5,4},{6,5},{7,6},{8,11},{9,8},{10,9... | collective-permute-start | bytes 405512 | tf_op jit(solution)/shard_map/ppermute | solution.py:225
  54.1 2.2 %collective-permute-done.23.refs_1_ = f32[264,128]{1,0:T(8,128)S(1)} collective-permute-done((f32[264,128]{1,0:T(8,128)S(1)}, f32[264,128]{1,0:T(8,128)S(1)}, u32[]{:S(2)}, u32[]{:S(2)}) %collective-permute-start.23) | collective-permute-done | bytes 135200 | tf_op jit(solution)/shard_map/ppermute | solution.py:225
  56.3 2.9 %collective-permute-done.24.refs_2_ = f32[264,128]{1,0:T(8,128)S(1)} collective-permute-done((f32[264,128]{1,0:T(8,128)S(1)}, f32[264,128]{1,0:T(8,128)S(1)}, u32[]{:S(2)}, u32[]{:S(2)}) %collective-permute-start.24) | collective-permute-done | bytes 135200 | tf_op jit(solution)/shard_map/ppermute | solution.py:225
  59.2 0.2 collective-permute-done.25.refs_3_
  59.5 0.8 %shard_map.50 = bf16[2,4,1,128,128]{4,3,2,1,0:T(8,128)(2,1)} custom-call(s32[2,4,128]{2,1,0:T(4,128)S(1)} %copy-done.1, f32[264,128]{1,0:T(8,128)S(1)} %get-tuple-element.19.refs_0_, f32[264,128]{1,0:T(8,128)S(1)} %collective-permute-done.23.refs_1_, f32[264,128]{1,0:T(8,128)S(1)} %collective-permute-done.24.refs_2_, ...), custom_call_target="tpu_custom_call" | custom-call | tf_op jit(solution)/shard_map/pallas_call | solution.py:226
  (22 shorter events, 0.2 us)
Async XLA Ops:
  0.0 0.9 %copy-start = (bf16[2,1,4,128,128]{4,3,2,1,0:T(8,128)(2,1)S(1)}, bf16[2,1,4,128,128]{4,3,2,1,0:T(8,128)(2,1)}, u32[]{:S(2)}) copy-start(bf16[2,1,4,128,128]{4,3,2,1,0:T(8,128)(2,1)} %tiles_ref.1) | copy-start | bytes 786436
  1.0 0.7 %copy-start.2 = (s32[2,1,4]{2,1,0:T(1,128)S(1)}, s32[2,1,4]{2,1,0:T(1,128)}, u32[]{:S(2)}) copy-start(s32[2,1,4]{2,1,0:T(1,128)} %rows_ref.1) | copy-start | bytes 100
  2.3 9.6 %collective-permute-start.3 = (bf16[1040,128]{1,0:T(8,128)(2,1)S(1)}, bf16[1040,128]{1,0:T(8,128)(2,1)S(1)}, u32[]{:S(2)}, u32[]{:S(2)}) collective-permute-start(bf16[1040,128]{1,0:T(8,128)(2,1)S(1)} %shard_map.46.refs_0_.refs_2_), channel_id=1, source_target_pairs={{0,1},{1,2},{2,3},{3,0},{4,5},{5,6},{6,7},{7,4},{8,9},{9,10},{10,1... | collective-permute-start | bytes 798728 | tf_op jit(solution)/shard_map/ppermute | solution.py:180
  4.5 7.4 %collective-permute-start.4 = (bf16[1040,128]{1,0:T(8,128)(2,1)S(1)}, bf16[1040,128]{1,0:T(8,128)(2,1)S(1)}, u32[]{:S(2)}, u32[]{:S(2)}) collective-permute-start(bf16[1040,128]{1,0:T(8,128)(2,1)S(1)} %shard_map.46.refs_0_.refs_2_), channel_id=1, source_target_pairs={{0,3},{1,0},{2,1},{3,2},{4,7},{5,4},{6,5},{7,6},{8,11},{9,8},{10,9... | collective-permute-start | bytes 798728 | tf_op jit(solution)/shard_map/ppermute | solution.py:180
  6.0 7.9 %collective-permute-start.1 = (bf16[1040,128]{1,0:T(8,128)(2,1)S(1)}, bf16[1040,128]{1,0:T(8,128)(2,1)S(1)}, u32[]{:S(2)}, u32[]{:S(2)}) collective-permute-start(bf16[1040,128]{1,0:T(8,128)(2,1)S(1)} %shard_map.46.refs_0_.refs_2_), channel_id=1, source_target_pairs={{0,32},{4,12},{8,40},{12,20},{16,48},{20,28},{24,56},{28,4},{32,64... | collective-permute-start | bytes 798728 | tf_op jit(solution)/shard_map/ppermute | solution.py:176
  7.6 8.3 %collective-permute-start.2 = (bf16[1040,128]{1,0:T(8,128)(2,1)S(1)}, bf16[1040,128]{1,0:T(8,128)(2,1)S(1)}, u32[]{:S(2)}, u32[]{:S(2)}) collective-permute-start(bf16[1040,128]{1,0:T(8,128)(2,1)S(1)} %shard_map.46.refs_0_.refs_2_), channel_id=1, source_target_pairs={{0,96},{4,28},{8,104},{12,4},{16,112},{20,12},{24,120},{28,20},{32... | collective-permute-start | bytes 798728 | tf_op jit(solution)/shard_map/ppermute | solution.py:176
  9.8 9.0 %collective-permute-start = (bf16[1040,128]{1,0:T(8,128)(2,1)S(1)}, bf16[1040,128]{1,0:T(8,128)(2,1)S(1)}, u32[]{:S(2)}, u32[]{:S(2)}) collective-permute-start(bf16[1040,128]{1,0:T(8,128)(2,1)S(1)} %shard_map.46.refs_0_.refs_2_), channel_id=1, source_target_pairs={{0,64},{4,20},{8,72},{12,28},{16,80},{20,4},{24,88},{28,12},{32,96... | collective-permute-start | bytes 798728 | tf_op jit(solution)/shard_map/ppermute | solution.py:176
  16.0 9.7 %collective-permute-start.6 = (bf16[2080,128]{1,0:T(8,128)(2,1)S(1)}, bf16[2080,128]{1,0:T(8,128)(2,1)S(1)}, u32[]{:S(2)}, u32[]{:S(2)}) collective-permute-start(bf16[2080,128]{1,0:T(8,128)(2,1)S(1)} %get-tuple-element.14.refs_1_), channel_id=1, source_target_pairs={{0,8},{4,36},{8,16},{12,44},{16,24},{20,52},{24,0},{28,60},{32,40}... | collective-permute-start | bytes 1597448 | tf_op jit(solution)/shard_map/ppermute | solution.py:176
  17.3 8.5 %collective-permute-start.8 = (bf16[2080,128]{1,0:T(8,128)(2,1)S(1)}, bf16[2080,128]{1,0:T(8,128)(2,1)S(1)}, u32[]{:S(2)}, u32[]{:S(2)}) collective-permute-start(bf16[2080,128]{1,0:T(8,128)(2,1)S(1)} %get-tuple-element.14.refs_1_), channel_id=1, source_target_pairs={{0,24},{4,100},{8,0},{12,108},{16,8},{20,116},{24,16},{28,124},{32... | collective-permute-start | bytes 1597448 | tf_op jit(solution)/shard_map/ppermute | solution.py:176
  18.8 12.6 %collective-permute-start.10 = (bf16[2080,128]{1,0:T(8,128)(2,1)S(1)}, bf16[2080,128]{1,0:T(8,128)(2,1)S(1)}, u32[]{:S(2)}, u32[]{:S(2)}) collective-permute-start(bf16[2080,128]{1,0:T(8,128)(2,1)S(1)} %pad_maximum_fusion.refs_0_), channel_id=1, source_target_pairs={{0,8},{4,36},{8,16},{12,44},{16,24},{20,52},{24,0},{28,60},{32,40}... | collective-permute-start | bytes 1597448 | tf_op jit(solution)/shard_map/ppermute | solution.py:176
  18.9 12.6 %collective-permute-start.12 = (bf16[2080,128]{1,0:T(8,128)(2,1)S(1)}, bf16[2080,128]{1,0:T(8,128)(2,1)S(1)}, u32[]{:S(2)}, u32[]{:S(2)}) collective-permute-start(bf16[2080,128]{1,0:T(8,128)(2,1)S(1)} %pad_maximum_fusion.refs_0_), channel_id=1, source_target_pairs={{0,24},{4,100},{8,0},{12,108},{16,8},{20,116},{24,16},{28,124},{32... | collective-permute-start | bytes 1597448 | tf_op jit(solution)/shard_map/ppermute | solution.py:176
  21.6 12.7 %collective-permute-start.5 = (bf16[1040,128]{1,0:T(8,128)(2,1)S(1)}, bf16[1040,128]{1,0:T(8,128)(2,1)S(1)}, u32[]{:S(2)}, u32[]{:S(2)}) collective-permute-start(bf16[1040,128]{1,0:T(8,128)(2,1)S(1)} %get-tuple-element.15), channel_id=1, source_target_pairs={{0,2},{1,3},{2,0},{3,1},{4,6},{5,7},{6,4},{7,5},{8,10},{9,11},{10,... | collective-permute-start | bytes 798728 | tf_op jit(solution)/shard_map/ppermute | solution.py:188
  25.8 12.2 %collective-permute-start.7 = (bf16[1040,128]{1,0:T(8,128)(2,1)S(1)}, bf16[1040,128]{1,0:T(8,128)(2,1)S(1)}, u32[]{:S(2)}, u32[]{:S(2)}) collective-permute-start(bf16[1040,128]{1,0:T(8,128)(2,1)S(1)} %slice.16), channel_id=1, source_target_pairs={{0,8},{4,36},{8,16},{12,44},{16,24},{20,52},{24,0},{28,60},{32,40}... | collective-permute-start | bytes 798728 | tf_op jit(solution)/shard_map/ppermute | solution.py:176
  25.9 12.2 %collective-permute-start.9 = (bf16[1040,128]{1,0:T(8,128)(2,1)S(1)}, bf16[1040,128]{1,0:T(8,128)(2,1)S(1)}, u32[]{:S(2)}, u32[]{:S(2)}) collective-permute-start(bf16[1040,128]{1,0:T(8,128)(2,1)S(1)} %slice.17), channel_id=1, source_target_pairs={{0,24},{4,100},{8,0},{12,108},{16,8},{20,116},{24,16},{28,124},{32... | collective-permute-start | bytes 798728 | tf_op jit(solution)/shard_map/ppermute | solution.py:176
  31.5 7.0 %collective-permute-start.11 = (bf16[1040,128]{1,0:T(8,128)(2,1)S(1)}, bf16[1040,128]{1,0:T(8,128)(2,1)S(1)}, u32[]{:S(2)}, u32[]{:S(2)}) collective-permute-start(bf16[1040,128]{1,0:T(8,128)(2,1)S(1)} %slice.18), channel_id=1, source_target_pairs={{0,8},{4,36},{8,16},{12,44},{16,24},{20,52},{24,0},{28,60},{32,40}... | collective-permute-start | bytes 798728 | tf_op jit(solution)/shard_map/ppermute | solution.py:176
  31.6 15.0 %copy-start.3 = (s32[2,1,4]{2,1,0:T(1,128)S(1)}, s32[2,1,4]{2,1,0:T(1,128)}, u32[]{:S(2)}) copy-start(s32[2,1,4]{2,1,0:T(1,128)} %kept_ref.1) | copy-start | bytes 100
  31.6 10.4 %collective-permute-start.13 = (bf16[1040,128]{1,0:T(8,128)(2,1)S(1)}, bf16[1040,128]{1,0:T(8,128)(2,1)S(1)}, u32[]{:S(2)}, u32[]{:S(2)}) collective-permute-start(bf16[1040,128]{1,0:T(8,128)(2,1)S(1)} %slice.19), channel_id=1, source_target_pairs={{0,24},{4,100},{8,0},{12,108},{16,8},{20,116},{24,16},{28,124},{32... | collective-permute-start | bytes 798728 | tf_op jit(solution)/shard_map/ppermute | solution.py:176
  34.5 12.2 %collective-permute-start.14 = (bf16[4160,128]{1,0:T(8,128)(2,1)S(1)}, bf16[4160,128]{1,0:T(8,128)(2,1)S(1)}, u32[]{:S(2)}, u32[]{:S(2)}) collective-permute-start(bf16[4160,128]{1,0:T(8,128)(2,1)S(1)} %get-tuple-element.18), channel_id=1, source_target_pairs={{0,4},{4,0},{1,5},{5,1},{2,6},{6,2},{3,7},{7,3},{8,12},{12,8},{9,1... | collective-permute-start | bytes 3194888 | tf_op jit(solution)/shard_map/ppermute | solution.py:172
  37.9 6.0 %collective-permute-start.19 = (bf16[2080,128]{1,0:T(8,128)(2,1)S(1)}, bf16[2080,128]{1,0:T(8,128)(2,1)S(1)}, u32[]{:S(2)}, u32[]{:S(2)}) collective-permute-start(bf16[2080,128]{1,0:T(8,128)(2,1)S(1)} %collective-permute-done.6.refs_6_), channel_id=1, source_target_pairs={{0,4},{4,0},{1,5},{5,1},{2,6},{6,2},{3,7},{7,3},{8,12},{12,8},{9,1... | collective-permute-start | bytes 1597448 | tf_op jit(solution)/shard_map/ppermute | solution.py:172
  38.0 6.0 %collective-permute-start.20 = (bf16[2080,128]{1,0:T(8,128)(2,1)S(1)}, bf16[2080,128]{1,0:T(8,128)(2,1)S(1)}, u32[]{:S(2)}, u32[]{:S(2)}) collective-permute-start(bf16[2080,128]{1,0:T(8,128)(2,1)S(1)} %collective-permute-done.8.refs_7_), channel_id=1, source_target_pairs={{0,4},{4,0},{1,5},{5,1},{2,6},{6,2},{3,7},{7,3},{8,12},{12,8},{9,1... | collective-permute-start | bytes 1597448 | tf_op jit(solution)/shard_map/ppermute | solution.py:172
  38.5 4.7 %collective-permute-start.15 = (bf16[1040,128]{1,0:T(8,128)(2,1)S(1)}, bf16[1040,128]{1,0:T(8,128)(2,1)S(1)}, u32[]{:S(2)}, u32[]{:S(2)}) collective-permute-start(bf16[1040,128]{1,0:T(8,128)(2,1)S(1)} %collective-permute-done.7.refs_2_), channel_id=1, source_target_pairs={{0,4},{4,0},{1,5},{5,1},{2,6},{6,2},{3,7},{7,3},{8,12},{12,8},{9,1... | collective-permute-start | bytes 798728 | tf_op jit(solution)/shard_map/ppermute | solution.py:172
  42.0 1.5 %collective-permute-start.16 = (bf16[1040,128]{1,0:T(8,128)(2,1)S(1)}, bf16[1040,128]{1,0:T(8,128)(2,1)S(1)}, u32[]{:S(2)}, u32[]{:S(2)}) collective-permute-start(bf16[1040,128]{1,0:T(8,128)(2,1)S(1)} %collective-permute-done.9.refs_3_), channel_id=1, source_target_pairs={{0,4},{4,0},{1,5},{5,1},{2,6},{6,2},{3,7},{7,3},{8,12},{12,8},{9,1... | collective-permute-start | bytes 798728 | tf_op jit(solution)/shard_map/ppermute | solution.py:172
  43.2 3.4 %collective-permute-start.21 = (bf16[2080,128]{1,0:T(8,128)(2,1)S(1)}, bf16[2080,128]{1,0:T(8,128)(2,1)S(1)}, u32[]{:S(2)}, u32[]{:S(2)}) collective-permute-start(bf16[2080,128]{1,0:T(8,128)(2,1)S(1)} %collective-permute-done.10.refs_8_), channel_id=1, source_target_pairs={{0,4},{4,0},{1,5},{5,1},{2,6},{6,2},{3,7},{7,3},{8,12},{12,8},{9,1... | collective-permute-start | bytes 1597448 | tf_op jit(solution)/shard_map/ppermute | solution.py:172
  43.5 3.1 %collective-permute-start.22 = (bf16[2080,128]{1,0:T(8,128)(2,1)S(1)}, bf16[2080,128]{1,0:T(8,128)(2,1)S(1)}, u32[]{:S(2)}, u32[]{:S(2)}) collective-permute-start(bf16[2080,128]{1,0:T(8,128)(2,1)S(1)} %collective-permute-done.12.refs_9_), channel_id=1, source_target_pairs={{0,4},{4,0},{1,5},{5,1},{2,6},{6,2},{3,7},{7,3},{8,12},{12,8},{9,1... | collective-permute-start | bytes 1597448 | tf_op jit(solution)/shard_map/ppermute | solution.py:172
  43.9 2.3 %collective-permute-start.17 = (bf16[1040,128]{1,0:T(8,128)(2,1)S(1)}, bf16[1040,128]{1,0:T(8,128)(2,1)S(1)}, u32[]{:S(2)}, u32[]{:S(2)}) collective-permute-start(bf16[1040,128]{1,0:T(8,128)(2,1)S(1)} %collective-permute-done.11.refs_4_), channel_id=1, source_target_pairs={{0,4},{4,0},{1,5},{5,1},{2,6},{6,2},{3,7},{7,3},{8,12},{12,8},{9,1... | collective-permute-start | bytes 798728 | tf_op jit(solution)/shard_map/ppermute | solution.py:172
  44.1 2.5 %collective-permute-start.18 = (bf16[1040,128]{1,0:T(8,128)(2,1)S(1)}, bf16[1040,128]{1,0:T(8,128)(2,1)S(1)}, u32[]{:S(2)}, u32[]{:S(2)}) collective-permute-start(bf16[1040,128]{1,0:T(8,128)(2,1)S(1)} %collective-permute-done.13.refs_5_), channel_id=1, source_target_pairs={{0,4},{4,0},{1,5},{5,1},{2,6},{6,2},{3,7},{7,3},{8,12},{12,8},{9,1... | collective-permute-start | bytes 798728 | tf_op jit(solution)/shard_map/ppermute | solution.py:172
  46.6 12.9 %copy-start.1 = (s32[2,4,128]{2,1,0:T(4,128)S(1)}, s32[2,4,128]{2,1,0:T(4,128)}, u32[]{:S(2)}) copy-start(s32[2,4,128]{2,1,0:T(4,128)} %mask_ref.1) | copy-start | bytes 12292
  50.3 6.1 %collective-permute-start.23 = (f32[264,128]{1,0:T(8,128)S(1)}, f32[264,128]{1,0:T(8,128)S(1)}, u32[]{:S(2)}, u32[]{:S(2)}) collective-permute-start(f32[264,128]{1,0:T(8,128)S(1)} %get-tuple-element.20), channel_id=1, source_target_pairs={{0,1},{1,2},{2,3},{3,0},{4,5},{5,6},{6,7},{7,4},{8,9},{9,10},{10,1... | collective-permute-start | bytes 405512 | tf_op jit(solution)/shard_map/ppermute | solution.py:225
  50.4 8.8 %collective-permute-start.24 = (f32[264,128]{1,0:T(8,128)S(1)}, f32[264,128]{1,0:T(8,128)S(1)}, u32[]{:S(2)}, u32[]{:S(2)}) collective-permute-start(f32[264,128]{1,0:T(8,128)S(1)} %get-tuple-element.21), channel_id=1, source_target_pairs={{0,2},{1,3},{2,0},{3,1},{4,6},{5,7},{6,4},{7,5},{8,10},{9,11},{10,... | collective-permute-start | bytes 405512 | tf_op jit(solution)/shard_map/ppermute | solution.py:225
  53.0 6.5 %collective-permute-start.25 = (f32[264,128]{1,0:T(8,128)S(1)}, f32[264,128]{1,0:T(8,128)S(1)}, u32[]{:S(2)}, u32[]{:S(2)}) collective-permute-start(f32[264,128]{1,0:T(8,128)S(1)} %get-tuple-element.22), channel_id=1, source_target_pairs={{0,3},{1,0},{2,1},{3,2},{4,7},{5,4},{6,5},{7,6},{8,11},{9,8},{10,9... | collective-permute-start | bytes 405512 | tf_op jit(solution)/shard_map/ppermute | solution.py:225

commit v5 on v2

v5 whole, which is shorter than its diff:
```python
import functools

import jax
import jax.numpy as jnp
from jax import lax
from jax.experimental import pallas as pl
from jax.experimental.pallas import tpu as pltpu
from jax.sharding import Mesh, PartitionSpec as P

TILE = 128
SLOTS = 4
PANELS = 2
BANDS = 4
BLOCKS = 16
SIDE = 4
BODY = PANELS * SLOTS * TILE
UNIT = BODY + 16
CHUNK = PANELS * TILE + 8
GROUP = 8
LANES = TILE // GROUP
CELL = ("x", "z", "core")
VMEM = pl.BlockSpec(memory_space=pltpu.VMEM)
SMEM = pl.BlockSpec(memory_space=pltpu.SMEM)
LIMIT = pltpu.CompilerParams(vmem_limit_bytes=40 * 1024 * 1024)


def ring(shift):
    return [(i, (i + shift) % SIDE) for i in range(SIDE)]


def cells(first, second):
    pairs = []
    for x in range(SIDE):
        for z in range(SIDE):
            for core, (dx, dz) in enumerate((first, second)):
                target = ((x + dx) % SIDE) * SIDE + (z + dz) % SIDE
                pairs.append(((x * SIDE + z) * 2 + core, target * 2 + core))
    return pairs


def along(value, axis, shift):
    steps = ((shift, 0), (0, shift))
    return lax.ppermute(value, CELL, cells(steps[axis], steps[1 - axis]))


def swap(value):
    return lax.ppermute(value, "core", [(0, 1), (1, 0)])


def cell_number(x, z, core):
    return (x * SIDE + z) * 2 + core


def id_rows(band_rows):
    cell = cell_number(*(lax.axis_index(name) for name in CELL))
    rows = jnp.pad(band_rows[:, 0], ((0, 0), (0, GROUP - SLOTS))).reshape(1, LANES)
    row = lax.broadcasted_iota(jnp.int32, (16, TILE), 0)
    group = lax.broadcasted_iota(jnp.int32, (16, TILE), 1) // LANES
    here = ((row == cell // GROUP) & (group == cell % GROUP)) | ((row == GROUP) & (group == 0))
    return jnp.where(here, jnp.tile(rows, (1, GROUP)), 0).astype(jnp.bfloat16)


def buffer_kernel(count, *refs):
    unit_refs, (buffer_ref, again_ref) = refs[:count], refs[-2:]
    for u, ref in enumerate(unit_refs[1:] if count == 3 else unit_refs):
        buffer_ref[u * UNIT : (u + 1) * UNIT] = ref[...]
    again_ref[...] = unit_refs[0][...]


def join_kernel(count, *refs):
    line_refs, right_refs = refs[:count], refs[count : count + BANDS]
    line_ref, tiles_ref, ids_ref = refs[count + BANDS :]
    done = 0
    for ref in line_refs:
        line_ref[done : done + ref.shape[0]] = ref[...]
        done += ref.shape[0]
    for b, ref in enumerate(right_refs):
        ids_ref[b : b + 1] = ref[BODY:].astype(jnp.float32).astype(jnp.int32)[GROUP : GROUP + 1]
        for p in range(PANELS):
            tiles_ref[p, b * SLOTS : (b + 1) * SLOTS] = ref[p * SLOTS * TILE : (p + 1) * SLOTS * TILE].reshape(
                SLOTS, TILE, TILE
            )


def expand_kernel(origins, right_shifts, chunk_shifts, kept_ref, tiles_ref, right_ids_ref, *refs):
    left_refs, chunk_refs = refs[: len(origins)], refs[len(origins) : len(origins) + BANDS]
    all_ref, acc, table, ids, place, sem = refs[len(origins) + BANDS :]
    band, x, z, core = (lax.axis_index(name) for name in ("layer",) + CELL)

    sums, done = None, 0
    for ref, units in zip(left_refs, origins):
        for u in range(len(units)):
            block = ref[u * UNIT + BODY : (u + 1) * UNIT].astype(jnp.float32)
            sums = block if sums is None else sums + block
    table[: BANDS] = sums.astype(jnp.int32)[: BANDS]
    table[BANDS : 2 * BANDS] = right_ids_ref[...]
    copy = pltpu.make_async_copy(table, ids, sem)
    copy.start()
    for ref, units in zip(left_refs, origins):
        all_ref[done * UNIT : (done + len(units)) * UNIT] = ref[...]
        for u, (one, other, across) in enumerate(units):
            owner = 1 - core if across else core
            dx, dz = jnp.where(owner == 0, one, other), jnp.where(owner == 0, other, one)
            place[cell_number((x - dx) & (SIDE - 1), (z - dz) & (SIDE - 1), owner)] = done + u
        done += len(units)
    acc[...] = jnp.zeros_like(acc)
    copy.wait()

    for p in range(PANELS):
        for s in range(BANDS * SLOTS):
            source = (band - right_shifts[s // SLOTS]) & (BANDS - 1)
            panel = source * BLOCKS + ids[BANDS + s // SLOTS, GROUP * p + s % SLOTS]
            cell, j = panel // PANELS, panel % PANELS
            start = pl.multiple_of(place[cell] * UNIT + j * SLOTS * TILE, 16)
            product = jnp.dot(
                all_ref[pl.ds(start, SLOTS * TILE)], tiles_ref[p, s], preferred_element_type=jnp.float32
            )
            for k in range(SLOTS):
                block = ids[cell // GROUP, (cell % GROUP) * LANES + GROUP * j + k]
                acc[p, block] += product[k * TILE : (k + 1) * TILE]

    for p in range(PANELS):

        def add(r, total):
            value = acc[p, r]
            return total + jnp.sum((value * value).reshape(TILE // 8, 8, TILE), axis=0)

        total = lax.fori_loop(0, BLOCKS, add, jnp.zeros((8, TILE), jnp.float32), unroll=4)
        total = jnp.sum(total, axis=0, keepdims=True)
        for s, shift in enumerate(chunk_shifts):
            value = acc[p, kept_ref[p, 0, (band + shift) & (BANDS - 1)]]
            chunk_refs[s][p * TILE : (p + 1) * TILE] = value * value
            chunk_refs[s][PANELS * TILE + 4 * p : PANELS * TILE + 4 * p + 4] = jnp.broadcast_to(total, (4, TILE))


def finish_kernel(chunk_shifts, mask_ref, *refs):
    chunk_refs, out_ref = refs[:BANDS], refs[BANDS]
    band = lax.axis_index("layer")
    for p in range(PANELS):
        row = PANELS * TILE + 4 * p
        total = sum(ref[row : row + 1] for ref in chunk_refs)
        scale = (BANDS * BLOCKS * TILE) / total
        for s, shift in enumerate(chunk_shifts):
            source = (band - shift) & (BANDS - 1)
            keep = mask_ref[p, pl.ds(source, 1)].astype(jnp.float32).astype(jnp.bfloat16)
            value = (chunk_refs[s][p * TILE : (p + 1) * TILE] * scale).astype(jnp.bfloat16)
            out_ref[p, source, 0] = value * keep


def per_device(tile_values, band_rows, kept_rows, prune_mask):
    unit = jnp.concatenate([tile_values.reshape(BODY, TILE), id_rows(band_rows)], axis=0)
    rights = [lax.ppermute(unit, "layer", ring(s)) for s in (1, 3)]
    near, back, away = [along(unit, 0, shift) for shift in (2, 1, 3)]
    second = jnp.concatenate([back, away], axis=0)
    first, unit_again = pl.pallas_call(
        functools.partial(buffer_kernel, 2),
        out_shape=[jax.ShapeDtypeStruct((n * UNIT, TILE), jnp.bfloat16) for n in (2, 1)],
        in_specs=[VMEM] * 4,
        out_specs=[VMEM] * 2,
        compiler_params=LIMIT,
    )(unit, near, *rights)
    rights = [unit, *rights, lax.ppermute(unit_again, "layer", ring(2))]
    right_shifts = (0, 1, 3, 2)
    joined, tiles, right_ids = pl.pallas_call(
        functools.partial(join_kernel, 2),
        out_shape=[
            jax.ShapeDtypeStruct((SIDE * UNIT, TILE), jnp.bfloat16),
            jax.ShapeDtypeStruct((PANELS, BANDS * SLOTS, TILE, TILE), jnp.bfloat16),
            jax.ShapeDtypeStruct((BANDS, TILE), jnp.int32),
        ],
        in_specs=[VMEM] * (2 + BANDS),
        out_specs=[VMEM] * 3,
        compiler_params=LIMIT,
    )(first, second, *rights)
    up, down = along(first, 1, 1), along(first, 1, 3)
    up_b, down_b = along(second, 1, 1), along(second, 1, 3)
    fars = [along(up[:UNIT], 1, 1), along(down[UNIT:], 1, 3)]
    fars_b = [along(up_b[:UNIT], 1, 1), along(down_b[UNIT:], 1, 3)]
    one, two = (0, 2), (1, 3)
    parts = {
        "up": (up, [(a, 1) for a in one]),
        "down": (down, [(a, 3) for a in one]),
        "up_b": (up_b, [(a, 1) for a in two]),
        "down_b": (down_b, [(a, 3) for a in two]),
        "far_0": (fars[0], [(one[0], 2)]),
        "far_1": (fars[1], [(one[1], 2)]),
        "far_b0": (fars_b[0], [(two[0], 2)]),
        "far_b1": (fars_b[1], [(two[1], 2)]),
    }
    kept = [parts[name] for name in ("far_b0", "far_b1", "far_0", "far_1", "up_b", "down_b", "up", "down")]
    swapped = [parts[name] for name in ("up", "down", "up_b", "down_b", "far_b0", "far_b1", "far_0", "far_1")]
    line = [(first, [(a, 0) for a in one]), (second, [(a, 0) for a in two])]
    lefts = [one for one, _ in line + kept] + [swap(joined)] + [swap(part) for part, _ in swapped]
    origins = [[(a, b, False) for a, b in where] for _, where in line + kept]
    origins += [[(a, 0, True) for a in one + two]] + [[(a, b, True) for a, b in where] for _, where in swapped]
    counts = [len(where) for where in origins]
    units = sum(counts)
    chunk_shifts = (0, 1, 2, 3)
    chunks = pl.pallas_call(
        functools.partial(expand_kernel, origins, right_shifts, chunk_shifts),
        out_shape=[jax.ShapeDtypeStruct((CHUNK, TILE), jnp.float32)] * BANDS,
        in_specs=[SMEM] + [VMEM] * (len(lefts) + 2),
        out_specs=[VMEM] * BANDS,
        scratch_shapes=[
            pltpu.VMEM((units * UNIT, TILE), jnp.bfloat16),
            pltpu.VMEM((PANELS, BLOCKS, TILE, TILE), jnp.float32),
            pltpu.VMEM((2 * BANDS, TILE), jnp.int32),
            pltpu.SMEM((2 * BANDS, TILE), jnp.int32),
            pltpu.SMEM((units,), jnp.int32),
            pltpu.SemaphoreType.DMA,
        ],
        compiler_params=LIMIT,
        cost_estimate=pl.CostEstimate(flops=2**29, bytes_accessed=10 * 2**20, transcendentals=0),
    )(kept_rows, tiles, right_ids, *lefts)

    chunks = [chunks[0]] + [lax.ppermute(chunks[s], "layer", ring(chunk_shifts[s])) for s in (1, 2, 3)]
    return pl.pallas_call(
        functools.partial(finish_kernel, chunk_shifts),
        out_shape=jax.ShapeDtypeStruct((PANELS, BANDS, 1, TILE, TILE), jnp.bfloat16),
        in_specs=[VMEM] * (1 + BANDS),
        out_specs=VMEM,
        compiler_params=LIMIT,
    )(prune_mask, *chunks)


def solution(mesh):
    parts = Mesh(mesh.devices.reshape(SIDE, SIDE, 2, BANDS), CELL + ("layer",))
    return jax.shard_map(
        per_device,
        mesh=parts,
        in_specs=(
            P(CELL, "layer", None, None, None),
            P(CELL, "layer", None),
            P(CELL, "layer", None),
            P(CELL, None, None),
        ),
        out_specs=P(CELL, None, "layer", None, None),
        check_vma=False,
    )
```

time: 70.1 us -> 57.8 us (0.82)
  waiting for transfers between devices: 30.2 us -> 15 us
  starting transfers between devices: 33.2 us -> 35.9 us
  other arithmetic: 0.07 us -> 1.07 us
  Pallas kernels: 4.84 us -> 3.93 us
    ppermute x12 -> x17, waiting for transfers between devices: 26.4 us -> 11.6 us  [the longest x11 5.58 us: along(): return lax.ppermute(value, CELL, cells(steps[axis], steps[1 - axis]))]
    ppermute x12 -> x17, starting transfers between devices: 20.1 us -> 28 us  [the longest x11 17.6 us: along(): return lax.ppermute(value, CELL, cells(steps[axis], steps[1 - axis]))]
    ppermute x4 -> x9, starting transfers between devices: 13.1 us -> 7.93 us  [swap(): return lax.ppermute(value, 'core', [(0, 1), (1, 0)])]
    unnamed x8 -> x5, local copies, waits for them, and re-layouts: 1.64 us -> 0.03 us
    pallas_call x4, Pallas kernels: 4.84 us -> 3.93 us  [the longest x1 2.96 us: per_device(): pl.pallas_call(functools.partial(expand_kernel, origins, right_shifts, ch...]
    concatenate x1, other arithmetic: 0.07 us -> 0.97 us  [per_device(): jnp.concatenate([tile_values.reshape(BODY, TILE), id_rows(band_rows)], ax...]
    ppermute x4 -> x9, waiting for transfers between devices: 3.82 us -> 3.35 us  [swap(): return lax.ppermute(value, 'core', [(0, 1), (1, 0)])]
  transfers between devices with their start and end apart: 16 -> 26, of which waited for: 11 -> 10; matrix products, arithmetic and copies ran while one was open for 0% -> 0% of each run, Pallas kernels for 0% -> 0%
where the time goes in v5:
time: 57.8 us; the launch traced here: 57 us
  starting transfers between devices  35.9 us (62%)
  waiting for transfers between devices  15 us (26%)
  Pallas kernels  3.93 us (7%)
  other arithmetic  1.07 us (2%)
  local copies, waits for them, and re-layouts  1 us (2%)
    ppermute x11, starting transfers between devices, along(): return lax.ppermute(value, CELL, cells(steps[axis], steps[1 - axis]))  17.6 us
    ppermute x9, starting transfers between devices, swap(): return lax.ppermute(value, 'core', [(0, 1), (1, 0)])  7.93 us
    ppermute x11, waiting for transfers between devices, along(): return lax.ppermute(value, CELL, cells(steps[axis], steps[1 - axis]))  5.58 us
    ppermute x3, waiting for transfers between devices, per_device(): lax.ppermute(chunks[s], 'layer', ring(chunk_shifts[s]))  5.18 us
    ppermute x3, starting transfers between devices, per_device(): lax.ppermute(chunks[s], 'layer', ring(chunk_shifts[s]))  5.05 us
    ppermute x9, waiting for transfers between devices, swap(): return lax.ppermute(value, 'core', [(0, 1), (1, 0)])  3.35 us
    pallas_call x1, Pallas kernels, per_device(): pl.pallas_call(functools.partial(expand_kernel, origins, right_shifts, ch...  2.96 us
    ppermute x2, starting transfers between devices, per_device(): rights = [lax.ppermute(unit, 'layer', ring(s)) for s in (1, 3)]  2.74 us
  transfers between devices with their start and end apart: 26, of which 10 were waited for; matrix products, arithmetic and copies ran while one was open for 0% of the time, Pallas kernels for 0%

profile of v5, /device:TPU:1, one launch (start us, length us, event | category | flops | bytes accessed | tf_op | source)
XLA Modules:
  0.0 57.0 jit_solution(18279062661268405476)
XLA Ops:
  0.0 0.7 %pad.4 = s32[2,8]{1,0:T(2,128)S(1)} pad(s32[2,4]{1,0:T(2,128)} %bitcast.3, s32[]{:T(128)} %constant.57.clone.1), padding=0_0x0_4 | pad | bytes 100 | tf_op jit(solution)/shard_map/jit(_pad)/pad | solution.py:56
  0.7 0.1 tile.10
  0.8 0.1 tile.12
  0.9 0.1 select_convert_fusion
  1.0 1.0 %pad_maximum_fusion.refs_0_.refs_2_ = bf16[1040,128]{1,0:T(8,128)(2,1)S(1)} fusion(bf16[16,128]{1,0:T(8,128)(2,1)S(1)} %select_convert_fusion, bf16[1024,128]{1,0:T(8,128)(2,1)} %bitcast.2), kind=kLoop, calls=%fused_computation | loop fusion | flops 532480 | bytes 532480 | tf_op jit(solution)/shard_map/concatenate | solution.py:151
  2.0 2.5 %collective-permute-start.3 = (bf16[1040,128]{1,0:T(8,128)(2,1)S(1)}, bf16[1040,128]{1,0:T(8,128)(2,1)S(1)}, u32[]{:S(2)}, u32[]{:S(2)}) collective-permute-start(bf16[1040,128]{1,0:T(8,128)(2,1)S(1)} %pad_maximum_fusion.refs_0_.refs_2_), channel_id=1, source_target_pairs={{0,32},{4,12},{8,40},{12,20},{16,48},{20,28},{24,56},{28,4},{32,64... | collective-permute-start | bytes 798728 | tf_op jit(solution)/shard_map/ppermute | solution.py:43
  4.5 2.2 %collective-permute-start.4 = (bf16[1040,128]{1,0:T(8,128)(2,1)S(1)}, bf16[1040,128]{1,0:T(8,128)(2,1)S(1)}, u32[]{:S(2)}, u32[]{:S(2)}) collective-permute-start(bf16[1040,128]{1,0:T(8,128)(2,1)S(1)} %pad_maximum_fusion.refs_0_.refs_2_), channel_id=1, source_target_pairs={{0,96},{4,28},{8,104},{12,4},{16,112},{20,12},{24,120},{28,20},{32... | collective-permute-start | bytes 798728 | tf_op jit(solution)/shard_map/ppermute | solution.py:43
  6.7 1.2 %collective-permute-start = (bf16[1040,128]{1,0:T(8,128)(2,1)S(1)}, bf16[1040,128]{1,0:T(8,128)(2,1)S(1)}, u32[]{:S(2)}, u32[]{:S(2)}) collective-permute-start(bf16[1040,128]{1,0:T(8,128)(2,1)S(1)} %pad_maximum_fusion.refs_0_.refs_2_), channel_id=1, source_target_pairs={{0,64},{4,20},{8,72},{12,28},{16,80},{20,4},{24,88},{28,12},{32,96... | collective-permute-start | bytes 798728 | tf_op jit(solution)/shard_map/ppermute | solution.py:43
  7.9 1.3 %collective-permute-start.1 = (bf16[1040,128]{1,0:T(8,128)(2,1)S(1)}, bf16[1040,128]{1,0:T(8,128)(2,1)S(1)}, u32[]{:S(2)}, u32[]{:S(2)}) collective-permute-start(bf16[1040,128]{1,0:T(8,128)(2,1)S(1)} %pad_maximum_fusion.refs_0_.refs_2_), channel_id=1, source_target_pairs={{0,1},{1,2},{2,3},{3,0},{4,5},{5,6},{6,7},{7,4},{8,9},{9,10},{10,1... | collective-permute-start | bytes 798728 | tf_op jit(solution)/shard_map/ppermute | solution.py:152
  9.2 1.4 %collective-permute-start.2 = (bf16[1040,128]{1,0:T(8,128)(2,1)S(1)}, bf16[1040,128]{1,0:T(8,128)(2,1)S(1)}, u32[]{:S(2)}, u32[]{:S(2)}) collective-permute-start(bf16[1040,128]{1,0:T(8,128)(2,1)S(1)} %pad_maximum_fusion.refs_0_.refs_2_), channel_id=1, source_target_pairs={{0,3},{1,0},{2,1},{3,2},{4,7},{5,4},{6,5},{7,6},{8,11},{9,8},{10,9... | collective-permute-start | bytes 798728 | tf_op jit(solution)/shard_map/ppermute | solution.py:152
  10.7 0.0 collective-permute-done.3
  10.7 2.2 %collective-permute-done.4 = bf16[1040,128]{1,0:T(8,128)(2,1)S(1)} collective-permute-done((bf16[1040,128]{1,0:T(8,128)(2,1)S(1)}, bf16[1040,128]{1,0:T(8,128)(2,1)S(1)}, u32[]{:S(2)}, u32[]{:S(2)}) %collective-permute-start.4) | collective-permute-done | bytes 266272 | tf_op jit(solution)/shard_map/ppermute | solution.py:43
  12.9 1.3 %collective-permute-start.6 = (bf16[2080,128]{1,0:T(8,128)(2,1)S(1)}, bf16[2080,128]{1,0:T(8,128)(2,1)S(1)}, u32[]{:S(2)}, u32[]{:S(2)}) collective-permute-start(bf16[2080,128]{1,0:T(8,128)(2,1)S(1)} %constant_dynamic-update-slice_fusion.refs_1_), channel_id=1, source_target_pairs={{0,8},{4,36},{8,16},{12,44},{16,24},{20,52},{24,0},{28,60},{32,40}... | collective-permute-start | bytes 1597448 | tf_op jit(solution)/shard_map/ppermute | solution.py:43
  14.2 1.5 %collective-permute-start.8 = (bf16[2080,128]{1,0:T(8,128)(2,1)S(1)}, bf16[2080,128]{1,0:T(8,128)(2,1)S(1)}, u32[]{:S(2)}, u32[]{:S(2)}) collective-permute-start(bf16[2080,128]{1,0:T(8,128)(2,1)S(1)} %constant_dynamic-update-slice_fusion.refs_1_), channel_id=1, source_target_pairs={{0,24},{4,100},{8,0},{12,108},{16,8},{20,116},{24,16},{28,124},{32... | collective-permute-start | bytes 1597448 | tf_op jit(solution)/shard_map/ppermute | solution.py:43
  15.7 0.8 %collective-permute-done.1.refs_2_.refs_3_ = bf16[1040,128]{1,0:T(8,128)(2,1)S(1)} collective-permute-done((bf16[1040,128]{1,0:T(8,128)(2,1)S(1)}, bf16[1040,128]{1,0:T(8,128)(2,1)S(1)}, u32[]{:S(2)}, u32[]{:S(2)}) %collective-permute-start.1) | collective-permute-done | bytes 266272 | tf_op jit(solution)/shard_map/ppermute | solution.py:152
  16.5 0.1 shard_map.46
  16.6 2.2 %collective-permute-start.10 = (bf16[2080,128]{1,0:T(8,128)(2,1)S(1)}, bf16[2080,128]{1,0:T(8,128)(2,1)S(1)}, u32[]{:S(2)}, u32[]{:S(2)}) collective-permute-start(bf16[2080,128]{1,0:T(8,128)(2,1)S(1)} %get-tuple-element.14.refs_0_), channel_id=1, source_target_pairs={{0,8},{4,36},{8,16},{12,44},{16,24},{20,52},{24,0},{28,60},{32,40}... | collective-permute-start | bytes 1597448 | tf_op jit(solution)/shard_map/ppermute | solution.py:43
  18.8 1.1 %collective-permute-start.12 = (bf16[2080,128]{1,0:T(8,128)(2,1)S(1)}, bf16[2080,128]{1,0:T(8,128)(2,1)S(1)}, u32[]{:S(2)}, u32[]{:S(2)}) collective-permute-start(bf16[2080,128]{1,0:T(8,128)(2,1)S(1)} %get-tuple-element.14.refs_0_), channel_id=1, source_target_pairs={{0,24},{4,100},{8,0},{12,108},{16,8},{20,116},{24,16},{28,124},{32... | collective-permute-start | bytes 1597448 | tf_op jit(solution)/shard_map/ppermute | solution.py:43
  19.9 2.6 %collective-permute-start.5 = (bf16[1040,128]{1,0:T(8,128)(2,1)S(1)}, bf16[1040,128]{1,0:T(8,128)(2,1)S(1)}, u32[]{:S(2)}, u32[]{:S(2)}) collective-permute-start(bf16[1040,128]{1,0:T(8,128)(2,1)S(1)} %get-tuple-element.15), channel_id=1, source_target_pairs={{0,2},{1,3},{2,0},{3,1},{4,6},{5,7},{6,4},{7,5},{8,10},{9,11},{10,... | collective-permute-start | bytes 798728 | tf_op jit(solution)/shard_map/ppermute | solution.py:162
  22.5 0.1 collective-permute-done.6.refs_6_
  22.7 0.1 collective-permute-start.7
  22.8 2.7 %collective-permute-start.9 = (bf16[1040,128]{1,0:T(8,128)(2,1)S(1)}, bf16[1040,128]{1,0:T(8,128)(2,1)S(1)}, u32[]{:S(2)}, u32[]{:S(2)}) collective-permute-start(bf16[1040,128]{1,0:T(8,128)(2,1)S(1)} %slice.17), channel_id=1, source_target_pairs={{0,24},{4,100},{8,0},{12,108},{16,8},{20,116},{24,16},{28,124},{32... | collective-permute-start | bytes 798728 | tf_op jit(solution)/shard_map/ppermute | solution.py:43
  25.5 2.8 %collective-permute-done.10.refs_8_ = bf16[2080,128]{1,0:T(8,128)(2,1)S(1)} collective-permute-done((bf16[2080,128]{1,0:T(8,128)(2,1)S(1)}, bf16[2080,128]{1,0:T(8,128)(2,1)S(1)}, u32[]{:S(2)}, u32[]{:S(2)}) %collective-permute-start.10) | collective-permute-done | bytes 532512 | tf_op jit(solution)/shard_map/ppermute | solution.py:43
  28.4 0.1 collective-permute-start.11
  28.5 0.0 copy-start.1
  28.5 2.7 %collective-permute-start.13 = (bf16[1040,128]{1,0:T(8,128)(2,1)S(1)}, bf16[1040,128]{1,0:T(8,128)(2,1)S(1)}, u32[]{:S(2)}, u32[]{:S(2)}) collective-permute-start(bf16[1040,128]{1,0:T(8,128)(2,1)S(1)} %slice.19), channel_id=1, source_target_pairs={{0,24},{4,100},{8,0},{12,108},{16,8},{20,116},{24,16},{28,124},{32... | collective-permute-start | bytes 798728 | tf_op jit(solution)/shard_map/ppermute | solution.py:43
  31.2 0.1 shard_map.47
  31.4 3.0 %collective-permute-start.14 = (bf16[4160,128]{1,0:T(8,128)(2,1)S(1)}, bf16[4160,128]{1,0:T(8,128)(2,1)S(1)}, u32[]{:S(2)}, u32[]{:S(2)}) collective-permute-start(bf16[4160,128]{1,0:T(8,128)(2,1)S(1)} %get-tuple-element.18), channel_id=1, source_target_pairs={{0,4},{4,0},{1,5},{5,1},{2,6},{6,2},{3,7},{7,3},{8,12},{12,8},{9,1... | collective-permute-start | bytes 3194888 | tf_op jit(solution)/shard_map/ppermute | solution.py:47
  34.3 0.1 collective-permute-start.17
  34.4 0.4 collective-permute-start.18
  34.9 0.4 collective-permute-done.11.refs_4_
  35.2 3.2 %collective-permute-start.19 = (bf16[1040,128]{1,0:T(8,128)(2,1)S(1)}, bf16[1040,128]{1,0:T(8,128)(2,1)S(1)}, u32[]{:S(2)}, u32[]{:S(2)}) collective-permute-start(bf16[1040,128]{1,0:T(8,128)(2,1)S(1)} %collective-permute-done.7.refs_2_), channel_id=1, source_target_pairs={{0,4},{4,0},{1,5},{5,1},{2,6},{6,2},{3,7},{7,3},{8,12},{12,8},{9,1... | collective-permute-start | bytes 798728 | tf_op jit(solution)/shard_map/ppermute | solution.py:47
  38.4 1.2 %collective-permute-done.19.refs_15_ = bf16[1040,128]{1,0:T(8,128)(2,1)S(1)} collective-permute-done((bf16[1040,128]{1,0:T(8,128)(2,1)S(1)}, bf16[1040,128]{1,0:T(8,128)(2,1)S(1)}, u32[]{:S(2)}, u32[]{:S(2)}) %collective-permute-start.19) | collective-permute-done | bytes 266272 | tf_op jit(solution)/shard_map/ppermute | solution.py:47
  39.6 0.4 collective-permute-start.15
  39.9 0.0 collective-permute-done.20.refs_16_
  40.0 0.4 collective-permute-start.16
  40.3 0.1 collective-permute-start.21
  40.5 0.4 collective-permute-start.22
  40.8 1.8 %collective-permute-done.21.refs_17_ = bf16[1040,128]{1,0:T(8,128)(2,1)S(1)} collective-permute-done((bf16[1040,128]{1,0:T(8,128)(2,1)S(1)}, bf16[1040,128]{1,0:T(8,128)(2,1)S(1)}, u32[]{:S(2)}, u32[]{:S(2)}) %collective-permute-start.21) | collective-permute-done | bytes 266272 | tf_op jit(solution)/shard_map/ppermute | solution.py:47
  42.6 0.4 collective-permute-done.22.refs_18_
  43.0 0.0 copy-start
  43.0 3.0 %shard_map.48 = (f32[264,128]{1,0:T(8,128)S(1)}, f32[264,128]{1,0:T(8,128)S(1)}, f32[264,128]{1,0:T(8,128)S(1)}, f32[264,128]{1,0:T(8,128)S(1)}) custom-call(s32[2,1,4]{2,1,0:T(1,128)S(1)} %copy-done.1, bf16[2,16,128,128]{3,2,1,0:T(8,128)(2,1)S(1)} %get-tuple-element.16.tiles_ref, s32[4,128]{1,0:T(4,128)S(1)} %get-tuple-element.17.right_ids_ref, ...), custom_call_target="tpu_custom_call" | custom-call | flops 536870912 | bytes 10485760 | tf_op jit(solution)/shard_map/pallas_call | solution.py:199
  46.0 1.4 %collective-permute-start.23 = (f32[264,128]{1,0:T(8,128)S(1)}, f32[264,128]{1,0:T(8,128)S(1)}, u32[]{:S(2)}, u32[]{:S(2)}) collective-permute-start(f32[264,128]{1,0:T(8,128)S(1)} %get-tuple-element.20), channel_id=1, source_target_pairs={{0,1},{1,2},{2,3},{3,0},{4,5},{5,6},{6,7},{7,4},{8,9},{9,10},{10,1... | collective-permute-start | bytes 405512 | tf_op jit(solution)/shard_map/ppermute | solution.py:216
  47.4 2.6 %collective-permute-start.24 = (f32[264,128]{1,0:T(8,128)S(1)}, f32[264,128]{1,0:T(8,128)S(1)}, u32[]{:S(2)}, u32[]{:S(2)}) collective-permute-start(f32[264,128]{1,0:T(8,128)S(1)} %get-tuple-element.21), channel_id=1, source_target_pairs={{0,2},{1,3},{2,0},{3,1},{4,6},{5,7},{6,4},{7,5},{8,10},{9,11},{10,... | collective-permute-start | bytes 405512 | tf_op jit(solution)/shard_map/ppermute | solution.py:216
  50.0 1.1 %collective-permute-start.25 = (f32[264,128]{1,0:T(8,128)S(1)}, f32[264,128]{1,0:T(8,128)S(1)}, u32[]{:S(2)}, u32[]{:S(2)}) collective-permute-start(f32[264,128]{1,0:T(8,128)S(1)} %get-tuple-element.22), channel_id=1, source_target_pairs={{0,3},{1,0},{2,1},{3,2},{4,7},{5,4},{6,5},{7,6},{8,11},{9,8},{10,9... | collective-permute-start | bytes 405512 | tf_op jit(solution)/shard_map/ppermute | solution.py:216
  51.1 1.2 %collective-permute-done.23.refs_1_ = f32[264,128]{1,0:T(8,128)S(1)} collective-permute-done((f32[264,128]{1,0:T(8,128)S(1)}, f32[264,128]{1,0:T(8,128)S(1)}, u32[]{:S(2)}, u32[]{:S(2)}) %collective-permute-start.23) | collective-permute-done | bytes 135200 | tf_op jit(solution)/shard_map/ppermute | solution.py:216
  52.3 4.0 %collective-permute-done.24.refs_2_ = f32[264,128]{1,0:T(8,128)S(1)} collective-permute-done((f32[264,128]{1,0:T(8,128)S(1)}, f32[264,128]{1,0:T(8,128)S(1)}, u32[]{:S(2)}, u32[]{:S(2)}) %collective-permute-start.24) | collective-permute-done | bytes 135200 | tf_op jit(solution)/shard_map/ppermute | solution.py:216
  56.3 0.8 %shard_map.49 = bf16[2,4,1,128,128]{4,3,2,1,0:T(8,128)(2,1)} custom-call(s32[2,4,128]{2,1,0:T(4,128)S(1)} %copy-done, f32[264,128]{1,0:T(8,128)S(1)} %get-tuple-element.19.refs_0_, f32[264,128]{1,0:T(8,128)S(1)} %collective-permute-done.23.refs_1_, f32[264,128]{1,0:T(8,128)S(1)} %collective-permute-done.24.refs_2_, ...), custom_call_target="tpu_custom_call" | custom-call | tf_op jit(solution)/shard_map/pallas_call | solution.py:217
  (27 shorter events, 0.2 us)
Async XLA Ops:
  2.0 8.7 %collective-permute-start.3 = (bf16[1040,128]{1,0:T(8,128)(2,1)S(1)}, bf16[1040,128]{1,0:T(8,128)(2,1)S(1)}, u32[]{:S(2)}, u32[]{:S(2)}) collective-permute-start(bf16[1040,128]{1,0:T(8,128)(2,1)S(1)} %pad_maximum_fusion.refs_0_.refs_2_), channel_id=1, source_target_pairs={{0,32},{4,12},{8,40},{12,20},{16,48},{20,28},{24,56},{28,4},{32,64... | collective-permute-start | bytes 798728 | tf_op jit(solution)/shard_map/ppermute | solution.py:43
  4.5 8.4 %collective-permute-start.4 = (bf16[1040,128]{1,0:T(8,128)(2,1)S(1)}, bf16[1040,128]{1,0:T(8,128)(2,1)S(1)}, u32[]{:S(2)}, u32[]{:S(2)}) collective-permute-start(bf16[1040,128]{1,0:T(8,128)(2,1)S(1)} %pad_maximum_fusion.refs_0_.refs_2_), channel_id=1, source_target_pairs={{0,96},{4,28},{8,104},{12,4},{16,112},{20,12},{24,120},{28,20},{32... | collective-permute-start | bytes 798728 | tf_op jit(solution)/shard_map/ppermute | solution.py:43
  6.7 9.0 %collective-permute-start = (bf16[1040,128]{1,0:T(8,128)(2,1)S(1)}, bf16[1040,128]{1,0:T(8,128)(2,1)S(1)}, u32[]{:S(2)}, u32[]{:S(2)}) collective-permute-start(bf16[1040,128]{1,0:T(8,128)(2,1)S(1)} %pad_maximum_fusion.refs_0_.refs_2_), channel_id=1, source_target_pairs={{0,64},{4,20},{8,72},{12,28},{16,80},{20,4},{24,88},{28,12},{32,96... | collective-permute-start | bytes 798728 | tf_op jit(solution)/shard_map/ppermute | solution.py:43
  7.9 8.6 %collective-permute-start.1 = (bf16[1040,128]{1,0:T(8,128)(2,1)S(1)}, bf16[1040,128]{1,0:T(8,128)(2,1)S(1)}, u32[]{:S(2)}, u32[]{:S(2)}) collective-permute-start(bf16[1040,128]{1,0:T(8,128)(2,1)S(1)} %pad_maximum_fusion.refs_0_.refs_2_), channel_id=1, source_target_pairs={{0,1},{1,2},{2,3},{3,0},{4,5},{5,6},{6,7},{7,4},{8,9},{9,10},{10,1... | collective-permute-start | bytes 798728 | tf_op jit(solution)/shard_map/ppermute | solution.py:152
  9.2 7.3 %collective-permute-start.2 = (bf16[1040,128]{1,0:T(8,128)(2,1)S(1)}, bf16[1040,128]{1,0:T(8,128)(2,1)S(1)}, u32[]{:S(2)}, u32[]{:S(2)}) collective-permute-start(bf16[1040,128]{1,0:T(8,128)(2,1)S(1)} %pad_maximum_fusion.refs_0_.refs_2_), channel_id=1, source_target_pairs={{0,3},{1,0},{2,1},{3,2},{4,7},{5,4},{6,5},{7,6},{8,11},{9,8},{10,9... | collective-permute-start | bytes 798728 | tf_op jit(solution)/shard_map/ppermute | solution.py:152
  12.9 9.7 %collective-permute-start.6 = (bf16[2080,128]{1,0:T(8,128)(2,1)S(1)}, bf16[2080,128]{1,0:T(8,128)(2,1)S(1)}, u32[]{:S(2)}, u32[]{:S(2)}) collective-permute-start(bf16[2080,128]{1,0:T(8,128)(2,1)S(1)} %constant_dynamic-update-slice_fusion.refs_1_), channel_id=1, source_target_pairs={{0,8},{4,36},{8,16},{12,44},{16,24},{20,52},{24,0},{28,60},{32,40}... | collective-permute-start | bytes 1597448 | tf_op jit(solution)/shard_map/ppermute | solution.py:43
  14.2 8.6 %collective-permute-start.8 = (bf16[2080,128]{1,0:T(8,128)(2,1)S(1)}, bf16[2080,128]{1,0:T(8,128)(2,1)S(1)}, u32[]{:S(2)}, u32[]{:S(2)}) collective-permute-start(bf16[2080,128]{1,0:T(8,128)(2,1)S(1)} %constant_dynamic-update-slice_fusion.refs_1_), channel_id=1, source_target_pairs={{0,24},{4,100},{8,0},{12,108},{16,8},{20,116},{24,16},{28,124},{32... | collective-permute-start | bytes 1597448 | tf_op jit(solution)/shard_map/ppermute | solution.py:43
  16.6 11.8 %collective-permute-start.10 = (bf16[2080,128]{1,0:T(8,128)(2,1)S(1)}, bf16[2080,128]{1,0:T(8,128)(2,1)S(1)}, u32[]{:S(2)}, u32[]{:S(2)}) collective-permute-start(bf16[2080,128]{1,0:T(8,128)(2,1)S(1)} %get-tuple-element.14.refs_0_), channel_id=1, source_target_pairs={{0,8},{4,36},{8,16},{12,44},{16,24},{20,52},{24,0},{28,60},{32,40}... | collective-permute-start | bytes 1597448 | tf_op jit(solution)/shard_map/ppermute | solution.py:43
  18.8 9.7 %collective-permute-start.12 = (bf16[2080,128]{1,0:T(8,128)(2,1)S(1)}, bf16[2080,128]{1,0:T(8,128)(2,1)S(1)}, u32[]{:S(2)}, u32[]{:S(2)}) collective-permute-start(bf16[2080,128]{1,0:T(8,128)(2,1)S(1)} %get-tuple-element.14.refs_0_), channel_id=1, source_target_pairs={{0,24},{4,100},{8,0},{12,108},{16,8},{20,116},{24,16},{28,124},{32... | collective-permute-start | bytes 1597448 | tf_op jit(solution)/shard_map/ppermute | solution.py:43
  19.9 11.3 %collective-permute-start.5 = (bf16[1040,128]{1,0:T(8,128)(2,1)S(1)}, bf16[1040,128]{1,0:T(8,128)(2,1)S(1)}, u32[]{:S(2)}, u32[]{:S(2)}) collective-permute-start(bf16[1040,128]{1,0:T(8,128)(2,1)S(1)} %get-tuple-element.15), channel_id=1, source_target_pairs={{0,2},{1,3},{2,0},{3,1},{4,6},{5,7},{6,4},{7,5},{8,10},{9,11},{10,... | collective-permute-start | bytes 798728 | tf_op jit(solution)/shard_map/ppermute | solution.py:162
  22.7 11.7 %collective-permute-start.7 = (bf16[1040,128]{1,0:T(8,128)(2,1)S(1)}, bf16[1040,128]{1,0:T(8,128)(2,1)S(1)}, u32[]{:S(2)}, u32[]{:S(2)}) collective-permute-start(bf16[1040,128]{1,0:T(8,128)(2,1)S(1)} %slice.16), channel_id=1, source_target_pairs={{0,8},{4,36},{8,16},{12,44},{16,24},{20,52},{24,0},{28,60},{32,40}... | collective-permute-start | bytes 798728 | tf_op jit(solution)/shard_map/ppermute | solution.py:43
  22.8 11.6 %collective-permute-start.9 = (bf16[1040,128]{1,0:T(8,128)(2,1)S(1)}, bf16[1040,128]{1,0:T(8,128)(2,1)S(1)}, u32[]{:S(2)}, u32[]{:S(2)}) collective-permute-start(bf16[1040,128]{1,0:T(8,128)(2,1)S(1)} %slice.17), channel_id=1, source_target_pairs={{0,24},{4,100},{8,0},{12,108},{16,8},{20,116},{24,16},{28,124},{32... | collective-permute-start | bytes 798728 | tf_op jit(solution)/shard_map/ppermute | solution.py:43
  28.4 6.8 %collective-permute-start.11 = (bf16[1040,128]{1,0:T(8,128)(2,1)S(1)}, bf16[1040,128]{1,0:T(8,128)(2,1)S(1)}, u32[]{:S(2)}, u32[]{:S(2)}) collective-permute-start(bf16[1040,128]{1,0:T(8,128)(2,1)S(1)} %slice.18), channel_id=1, source_target_pairs={{0,8},{4,36},{8,16},{12,44},{16,24},{20,52},{24,0},{28,60},{32,40}... | collective-permute-start | bytes 798728 | tf_op jit(solution)/shard_map/ppermute | solution.py:43
  28.5 14.5 %copy-start.1 = (s32[2,1,4]{2,1,0:T(1,128)S(1)}, s32[2,1,4]{2,1,0:T(1,128)}, u32[]{:S(2)}) copy-start(s32[2,1,4]{2,1,0:T(1,128)} %kept_ref.1) | copy-start | bytes 100
  28.5 9.9 %collective-permute-start.13 = (bf16[1040,128]{1,0:T(8,128)(2,1)S(1)}, bf16[1040,128]{1,0:T(8,128)(2,1)S(1)}, u32[]{:S(2)}, u32[]{:S(2)}) collective-permute-start(bf16[1040,128]{1,0:T(8,128)(2,1)S(1)} %slice.19), channel_id=1, source_target_pairs={{0,24},{4,100},{8,0},{12,108},{16,8},{20,116},{24,16},{28,124},{32... | collective-permute-start | bytes 798728 | tf_op jit(solution)/shard_map/ppermute | solution.py:43
  31.4 11.7 %collective-permute-start.14 = (bf16[4160,128]{1,0:T(8,128)(2,1)S(1)}, bf16[4160,128]{1,0:T(8,128)(2,1)S(1)}, u32[]{:S(2)}, u32[]{:S(2)}) collective-permute-start(bf16[4160,128]{1,0:T(8,128)(2,1)S(1)} %get-tuple-element.18), channel_id=1, source_target_pairs={{0,4},{4,0},{1,5},{5,1},{2,6},{6,2},{3,7},{7,3},{8,12},{12,8},{9,1... | collective-permute-start | bytes 3194888 | tf_op jit(solution)/shard_map/ppermute | solution.py:47
  34.3 6.0 %collective-permute-start.17 = (bf16[2080,128]{1,0:T(8,128)(2,1)S(1)}, bf16[2080,128]{1,0:T(8,128)(2,1)S(1)}, u32[]{:S(2)}, u32[]{:S(2)}) collective-permute-start(bf16[2080,128]{1,0:T(8,128)(2,1)S(1)} %collective-permute-done.6.refs_6_), channel_id=1, source_target_pairs={{0,4},{4,0},{1,5},{5,1},{2,6},{6,2},{3,7},{7,3},{8,12},{12,8},{9,1... | collective-permute-start | bytes 1597448 | tf_op jit(solution)/shard_map/ppermute | solution.py:47
  34.4 6.0 %collective-permute-start.18 = (bf16[2080,128]{1,0:T(8,128)(2,1)S(1)}, bf16[2080,128]{1,0:T(8,128)(2,1)S(1)}, u32[]{:S(2)}, u32[]{:S(2)}) collective-permute-start(bf16[2080,128]{1,0:T(8,128)(2,1)S(1)} %collective-permute-done.8.refs_7_), channel_id=1, source_target_pairs={{0,4},{4,0},{1,5},{5,1},{2,6},{6,2},{3,7},{7,3},{8,12},{12,8},{9,1... | collective-permute-start | bytes 1597448 | tf_op jit(solution)/shard_map/ppermute | solution.py:47
  35.2 4.4 %collective-permute-start.19 = (bf16[1040,128]{1,0:T(8,128)(2,1)S(1)}, bf16[1040,128]{1,0:T(8,128)(2,1)S(1)}, u32[]{:S(2)}, u32[]{:S(2)}) collective-permute-start(bf16[1040,128]{1,0:T(8,128)(2,1)S(1)} %collective-permute-done.7.refs_2_), channel_id=1, source_target_pairs={{0,4},{4,0},{1,5},{5,1},{2,6},{6,2},{3,7},{7,3},{8,12},{12,8},{9,1... | collective-permute-start | bytes 798728 | tf_op jit(solution)/shard_map/ppermute | solution.py:47
  38.4 1.5 %collective-permute-start.20 = (bf16[1040,128]{1,0:T(8,128)(2,1)S(1)}, bf16[1040,128]{1,0:T(8,128)(2,1)S(1)}, u32[]{:S(2)}, u32[]{:S(2)}) collective-permute-start(bf16[1040,128]{1,0:T(8,128)(2,1)S(1)} %collective-permute-done.9.refs_3_), channel_id=1, source_target_pairs={{0,4},{4,0},{1,5},{5,1},{2,6},{6,2},{3,7},{7,3},{8,12},{12,8},{9,1... | collective-permute-start | bytes 798728 | tf_op jit(solution)/shard_map/ppermute | solution.py:47
  39.6 3.4 %collective-permute-start.15 = (bf16[2080,128]{1,0:T(8,128)(2,1)S(1)}, bf16[2080,128]{1,0:T(8,128)(2,1)S(1)}, u32[]{:S(2)}, u32[]{:S(2)}) collective-permute-start(bf16[2080,128]{1,0:T(8,128)(2,1)S(1)} %collective-permute-done.10.refs_8_), channel_id=1, source_target_pairs={{0,4},{4,0},{1,5},{5,1},{2,6},{6,2},{3,7},{7,3},{8,12},{12,8},{9,1... | collective-permute-start | bytes 1597448 | tf_op jit(solution)/shard_map/ppermute | solution.py:47
  40.0 3.1 %collective-permute-start.16 = (bf16[2080,128]{1,0:T(8,128)(2,1)S(1)}, bf16[2080,128]{1,0:T(8,128)(2,1)S(1)}, u32[]{:S(2)}, u32[]{:S(2)}) collective-permute-start(bf16[2080,128]{1,0:T(8,128)(2,1)S(1)} %collective-permute-done.12.refs_9_), channel_id=1, source_target_pairs={{0,4},{4,0},{1,5},{5,1},{2,6},{6,2},{3,7},{7,3},{8,12},{12,8},{9,1... | collective-permute-start | bytes 1597448 | tf_op jit(solution)/shard_map/ppermute | solution.py:47
  40.3 2.3 %collective-permute-start.21 = (bf16[1040,128]{1,0:T(8,128)(2,1)S(1)}, bf16[1040,128]{1,0:T(8,128)(2,1)S(1)}, u32[]{:S(2)}, u32[]{:S(2)}) collective-permute-start(bf16[1040,128]{1,0:T(8,128)(2,1)S(1)} %collective-permute-done.11.refs_4_), channel_id=1, source_target_pairs={{0,4},{4,0},{1,5},{5,1},{2,6},{6,2},{3,7},{7,3},{8,12},{12,8},{9,1... | collective-permute-start | bytes 798728 | tf_op jit(solution)/shard_map/ppermute | solution.py:47
  40.5 2.5 %collective-permute-start.22 = (bf16[1040,128]{1,0:T(8,128)(2,1)S(1)}, bf16[1040,128]{1,0:T(8,128)(2,1)S(1)}, u32[]{:S(2)}, u32[]{:S(2)}) collective-permute-start(bf16[1040,128]{1,0:T(8,128)(2,1)S(1)} %collective-permute-done.13.refs_5_), channel_id=1, source_target_pairs={{0,4},{4,0},{1,5},{5,1},{2,6},{6,2},{3,7},{7,3},{8,12},{12,8},{9,1... | collective-permute-start | bytes 798728 | tf_op jit(solution)/shard_map/ppermute | solution.py:47
  43.0 13.2 %copy-start = (s32[2,4,128]{2,1,0:T(4,128)S(1)}, s32[2,4,128]{2,1,0:T(4,128)}, u32[]{:S(2)}) copy-start(s32[2,4,128]{2,1,0:T(4,128)} %mask_ref.1) | copy-start | bytes 12292
  46.0 6.2 %collective-permute-start.23 = (f32[264,128]{1,0:T(8,128)S(1)}, f32[264,128]{1,0:T(8,128)S(1)}, u32[]{:S(2)}, u32[]{:S(2)}) collective-permute-start(f32[264,128]{1,0:T(8,128)S(1)} %get-tuple-element.20), channel_id=1, source_target_pairs={{0,1},{1,2},{2,3},{3,0},{4,5},{5,6},{6,7},{7,4},{8,9},{9,10},{10,1... | collective-permute-start | bytes 405512 | tf_op jit(solution)/shard_map/ppermute | solution.py:216
  47.4 8.9 %collective-permute-start.24 = (f32[264,128]{1,0:T(8,128)S(1)}, f32[264,128]{1,0:T(8,128)S(1)}, u32[]{:S(2)}, u32[]{:S(2)}) collective-permute-start(f32[264,128]{1,0:T(8,128)S(1)} %get-tuple-element.21), channel_id=1, source_target_pairs={{0,2},{1,3},{2,0},{3,1},{4,6},{5,7},{6,4},{7,5},{8,10},{9,11},{10,... | collective-permute-start | bytes 405512 | tf_op jit(solution)/shard_map/ppermute | solution.py:216
  50.0 6.2 %collective-permute-start.25 = (f32[264,128]{1,0:T(8,128)S(1)}, f32[264,128]{1,0:T(8,128)S(1)}, u32[]{:S(2)}, u32[]{:S(2)}) collective-permute-start(f32[264,128]{1,0:T(8,128)S(1)} %get-tuple-element.22), channel_id=1, source_target_pairs={{0,3},{1,0},{2,1},{3,2},{4,7},{5,4},{6,5},{7,6},{8,11},{9,8},{10,9... | collective-permute-start | bytes 405512 | tf_op jit(solution)/shard_map/ppermute | solution.py:216

commit v6 on v5

--- a/solution.py
+++ b/solution.py
@@ -20,7 +20,6 @@
 LANES = TILE // GROUP
 CELL = ("x", "z", "core")
 VMEM = pl.BlockSpec(memory_space=pltpu.VMEM)
-SMEM = pl.BlockSpec(memory_space=pltpu.SMEM)
 LIMIT = pltpu.CompilerParams(vmem_limit_bytes=40 * 1024 * 1024)
 
 
@@ -51,9 +50,9 @@
     return (x * SIDE + z) * 2 + core
 
 
-def id_rows(band_rows):
+def id_rows(band_rows, kept_rows):
     cell = cell_number(*(lax.axis_index(name) for name in CELL))
-    rows = jnp.pad(band_rows[:, 0], ((0, 0), (0, GROUP - SLOTS))).reshape(1, LANES)
+    rows = jnp.concatenate([band_rows[:, 0], kept_rows[:, 0]], axis=1).reshape(1, LANES)
     row = lax.broadcasted_iota(jnp.int32, (16, TILE), 0)
     group = lax.broadcasted_iota(jnp.int32, (16, TILE), 1) // LANES
     here = ((row == cell // GROUP) & (group == cell % GROUP)) | ((row == GROUP) & (group == 0))
@@ -82,7 +81,7 @@
             )
 
 
-def expand_kernel(origins, right_shifts, chunk_shifts, kept_ref, tiles_ref, right_ids_ref, *refs):
+def expand_kernel(origins, right_shifts, chunk_shifts, tiles_ref, right_ids_ref, *refs):
     left_refs, chunk_refs = refs[: len(origins)], refs[len(origins) : len(origins) + BANDS]
     all_ref, acc, table, ids, place, sem = refs[len(origins) + BANDS :]
     band, x, z, core = (lax.axis_index(name) for name in ("layer",) + CELL)
@@ -128,7 +127,8 @@
         total = lax.fori_loop(0, BLOCKS, add, jnp.zeros((8, TILE), jnp.float32), unroll=4)
         total = jnp.sum(total, axis=0, keepdims=True)
         for s, shift in enumerate(chunk_shifts):
-            value = acc[p, kept_ref[p, 0, (band + shift) & (BANDS - 1)]]
+            slot = (band + shift) & (BANDS - 1)
+            value = acc[p, ids[BANDS, GROUP * p + SLOTS + slot]]
             chunk_refs[s][p * TILE : (p + 1) * TILE] = value * value
             chunk_refs[s][PANELS * TILE + 4 * p : PANELS * TILE + 4 * p + 4] = jnp.broadcast_to(total, (4, TILE))
 
@@ -148,7 +148,7 @@
 
 
 def per_device(tile_values, band_rows, kept_rows, prune_mask):
-    unit = jnp.concatenate([tile_values.reshape(BODY, TILE), id_rows(band_rows)], axis=0)
+    unit = jnp.concatenate([tile_values.reshape(BODY, TILE), id_rows(band_rows, kept_rows)], axis=0)
     rights = [lax.ppermute(unit, "layer", ring(s)) for s in (1, 3)]
     near, back, away = [along(unit, 0, shift) for shift in (2, 1, 3)]
     second = jnp.concatenate([back, away], axis=0)
@@ -195,11 +195,11 @@
     origins += [[(a, 0, True) for a in one + two]] + [[(a, b, True) for a, b in where] for _, where in swapped]
     counts = [len(where) for where in origins]
     units = sum(counts)
-    chunk_shifts = (0, 1, 2, 3)
+    chunk_shifts = (0, 2, 1, 3)
     chunks = pl.pallas_call(
         functools.partial(expand_kernel, origins, right_shifts, chunk_shifts),
         out_shape=[jax.ShapeDtypeStruct((CHUNK, TILE), jnp.float32)] * BANDS,
-        in_specs=[SMEM] + [VMEM] * (len(lefts) + 2),
+        in_specs=[VMEM] * (len(lefts) + 2),
         out_specs=[VMEM] * BANDS,
         scratch_shapes=[
             pltpu.VMEM((units * UNIT, TILE), jnp.bfloat16),
@@ -211,7 +211,7 @@
         ],
         compiler_params=LIMIT,
         cost_estimate=pl.CostEstimate(flops=2**29, bytes_accessed=10 * 2**20, transcendentals=0),
-    )(kept_rows, tiles, right_ids, *lefts)
+    )(tiles, right_ids, *lefts)
 
     chunks = [chunks[0]] + [lax.ppermute(chunks[s], "layer", ring(chunk_shifts[s])) for s in (1, 2, 3)]
     return pl.pallas_call(

time: 57.8 us -> 56.7 us (0.981)
  waiting for transfers between devices: 15 us -> 13.9 us
  other arithmetic: 1.07 us -> 1.84 us
  starting transfers between devices: 35.9 us -> 36.6 us
  local copies, waits for them, and re-layouts: 1 us -> 0.3 us
    ppermute x3, waiting for transfers between devices: 5.18 us -> 4.1 us  [per_device(): lax.ppermute(chunks[s], 'layer', ring(chunk_shifts[s]))]
    concatenate x1 -> x2, other arithmetic: 0.97 us -> 1.74 us  [the longest x1 0.97 us: per_device(): jnp.concatenate([tile_values.reshape(BODY, TILE), id_rows(band_rows, kept...]
    pad x1 -> x0, local copies, waits for them, and re-layouts: 0.69 us -> none  [id_rows(): jnp.pad(band_rows[:, 0], ((0, 0), (0, GROUP - SLOTS))).reshape(1, LANES)]
    ppermute x3, starting transfers between devices: 5.05 us -> 5.68 us  [per_device(): lax.ppermute(chunks[s], 'layer', ring(chunk_shifts[s]))]
where the time goes in v6:
time: 56.7 us; the launch traced here: 56.1 us
  starting transfers between devices  36.6 us (65%)
  waiting for transfers between devices  13.9 us (25%)
  Pallas kernels  3.36 us (6%)
  other arithmetic  1.84 us (3%)
    ppermute x11, starting transfers between devices, along(): return lax.ppermute(value, CELL, cells(steps[axis], steps[1 - axis]))  17.6 us
    ppermute x9, starting transfers between devices, swap(): return lax.ppermute(value, 'core', [(0, 1), (1, 0)])  7.93 us
    ppermute x3, starting transfers between devices, per_device(): lax.ppermute(chunks[s], 'layer', ring(chunk_shifts[s]))  5.68 us
    ppermute x11, waiting for transfers between devices, along(): return lax.ppermute(value, CELL, cells(steps[axis], steps[1 - axis]))  5.59 us
    ppermute x3, waiting for transfers between devices, per_device(): lax.ppermute(chunks[s], 'layer', ring(chunk_shifts[s]))  4.1 us
    ppermute x9, waiting for transfers between devices, swap(): return lax.ppermute(value, 'core', [(0, 1), (1, 0)])  3.35 us
    ppermute x2, starting transfers between devices, per_device(): rights = [lax.ppermute(unit, 'layer', ring(s)) for s in (1, 3)]  2.74 us
    ppermute x1, starting transfers between devices, per_device(): rights = [unit, *rights, lax.ppermute(unit_again, 'layer', ring(2))]  2.62 us
  transfers between devices with their start and end apart: 26, of which 10 were waited for; matrix products, arithmetic and copies ran while one was open for 0% of the time, Pallas kernels for 0%

profile of v6, /device:TPU:1, one launch (start us, length us, event | category | flops | bytes accessed | tf_op | source)
XLA Modules:
  0.0 56.1 jit_solution(14824394568277119640)
XLA Ops:
  0.0 0.8 %pad_add_fusion = s32[2,8]{1,0:T(2,128)S(1)} fusion(s32[2,4]{1,0:T(2,128)} %bitcast.4, s32[2,4]{1,0:T(2,128)} %bitcast.5), kind=kLoop, calls=%fused_computation.10 | loop fusion | flops 16 | bytes 128 | tf_op jit(solution)/shard_map/concatenate | solution.py:55
  0.8 0.1 tile.10
  0.9 0.1 tile.12
  1.0 0.1 select_convert_fusion
  1.1 1.0 %pad_maximum_fusion.refs_0_.refs_2_ = bf16[1040,128]{1,0:T(8,128)(2,1)S(1)} fusion(bf16[16,128]{1,0:T(8,128)(2,1)S(1)} %select_convert_fusion, bf16[1024,128]{1,0:T(8,128)(2,1)} %bitcast.3), kind=kLoop, calls=%fused_computation | loop fusion | flops 532480 | bytes 532480 | tf_op jit(solution)/shard_map/concatenate | solution.py:151
  2.0 2.5 %collective-permute-start.3 = (bf16[1040,128]{1,0:T(8,128)(2,1)S(1)}, bf16[1040,128]{1,0:T(8,128)(2,1)S(1)}, u32[]{:S(2)}, u32[]{:S(2)}) collective-permute-start(bf16[1040,128]{1,0:T(8,128)(2,1)S(1)} %pad_maximum_fusion.refs_0_.refs_2_), channel_id=1, source_target_pairs={{0,32},{4,12},{8,40},{12,20},{16,48},{20,28},{24,56},{28,4},{32,64... | collective-permute-start | bytes 798728 | tf_op jit(solution)/shard_map/ppermute | solution.py:42
  4.6 2.2 %collective-permute-start.4 = (bf16[1040,128]{1,0:T(8,128)(2,1)S(1)}, bf16[1040,128]{1,0:T(8,128)(2,1)S(1)}, u32[]{:S(2)}, u32[]{:S(2)}) collective-permute-start(bf16[1040,128]{1,0:T(8,128)(2,1)S(1)} %pad_maximum_fusion.refs_0_.refs_2_), channel_id=1, source_target_pairs={{0,96},{4,28},{8,104},{12,4},{16,112},{20,12},{24,120},{28,20},{32... | collective-permute-start | bytes 798728 | tf_op jit(solution)/shard_map/ppermute | solution.py:42
  6.8 1.2 %collective-permute-start = (bf16[1040,128]{1,0:T(8,128)(2,1)S(1)}, bf16[1040,128]{1,0:T(8,128)(2,1)S(1)}, u32[]{:S(2)}, u32[]{:S(2)}) collective-permute-start(bf16[1040,128]{1,0:T(8,128)(2,1)S(1)} %pad_maximum_fusion.refs_0_.refs_2_), channel_id=1, source_target_pairs={{0,64},{4,20},{8,72},{12,28},{16,80},{20,4},{24,88},{28,12},{32,96... | collective-permute-start | bytes 798728 | tf_op jit(solution)/shard_map/ppermute | solution.py:42
  8.0 1.3 %collective-permute-start.1 = (bf16[1040,128]{1,0:T(8,128)(2,1)S(1)}, bf16[1040,128]{1,0:T(8,128)(2,1)S(1)}, u32[]{:S(2)}, u32[]{:S(2)}) collective-permute-start(bf16[1040,128]{1,0:T(8,128)(2,1)S(1)} %pad_maximum_fusion.refs_0_.refs_2_), channel_id=1, source_target_pairs={{0,1},{1,2},{2,3},{3,0},{4,5},{5,6},{6,7},{7,4},{8,9},{9,10},{10,1... | collective-permute-start | bytes 798728 | tf_op jit(solution)/shard_map/ppermute | solution.py:152
  9.3 1.4 %collective-permute-start.2 = (bf16[1040,128]{1,0:T(8,128)(2,1)S(1)}, bf16[1040,128]{1,0:T(8,128)(2,1)S(1)}, u32[]{:S(2)}, u32[]{:S(2)}) collective-permute-start(bf16[1040,128]{1,0:T(8,128)(2,1)S(1)} %pad_maximum_fusion.refs_0_.refs_2_), channel_id=1, source_target_pairs={{0,3},{1,0},{2,1},{3,2},{4,7},{5,4},{6,5},{7,6},{8,11},{9,8},{10,9... | collective-permute-start | bytes 798728 | tf_op jit(solution)/shard_map/ppermute | solution.py:152
  10.7 0.0 collective-permute-done.3
  10.8 2.2 %collective-permute-done.4 = bf16[1040,128]{1,0:T(8,128)(2,1)S(1)} collective-permute-done((bf16[1040,128]{1,0:T(8,128)(2,1)S(1)}, bf16[1040,128]{1,0:T(8,128)(2,1)S(1)}, u32[]{:S(2)}, u32[]{:S(2)}) %collective-permute-start.4) | collective-permute-done | bytes 266272 | tf_op jit(solution)/shard_map/ppermute | solution.py:42
  13.0 1.3 %collective-permute-start.6 = (bf16[2080,128]{1,0:T(8,128)(2,1)S(1)}, bf16[2080,128]{1,0:T(8,128)(2,1)S(1)}, u32[]{:S(2)}, u32[]{:S(2)}) collective-permute-start(bf16[2080,128]{1,0:T(8,128)(2,1)S(1)} %constant_dynamic-update-slice_fusion.refs_1_), channel_id=1, source_target_pairs={{0,8},{4,36},{8,16},{12,44},{16,24},{20,52},{24,0},{28,60},{32,40}... | collective-permute-start | bytes 1597448 | tf_op jit(solution)/shard_map/ppermute | solution.py:42
  14.3 1.5 %collective-permute-start.8 = (bf16[2080,128]{1,0:T(8,128)(2,1)S(1)}, bf16[2080,128]{1,0:T(8,128)(2,1)S(1)}, u32[]{:S(2)}, u32[]{:S(2)}) collective-permute-start(bf16[2080,128]{1,0:T(8,128)(2,1)S(1)} %constant_dynamic-update-slice_fusion.refs_1_), channel_id=1, source_target_pairs={{0,24},{4,100},{8,0},{12,108},{16,8},{20,116},{24,16},{28,124},{32... | collective-permute-start | bytes 1597448 | tf_op jit(solution)/shard_map/ppermute | solution.py:42
  15.8 0.8 %collective-permute-done.1.refs_2_.refs_3_ = bf16[1040,128]{1,0:T(8,128)(2,1)S(1)} collective-permute-done((bf16[1040,128]{1,0:T(8,128)(2,1)S(1)}, bf16[1040,128]{1,0:T(8,128)(2,1)S(1)}, u32[]{:S(2)}, u32[]{:S(2)}) %collective-permute-start.1) | collective-permute-done | bytes 266272 | tf_op jit(solution)/shard_map/ppermute | solution.py:152
  16.6 0.1 shard_map.46
  16.7 2.2 %collective-permute-start.10 = (bf16[2080,128]{1,0:T(8,128)(2,1)S(1)}, bf16[2080,128]{1,0:T(8,128)(2,1)S(1)}, u32[]{:S(2)}, u32[]{:S(2)}) collective-permute-start(bf16[2080,128]{1,0:T(8,128)(2,1)S(1)} %get-tuple-element.14.refs_0_), channel_id=1, source_target_pairs={{0,8},{4,36},{8,16},{12,44},{16,24},{20,52},{24,0},{28,60},{32,40}... | collective-permute-start | bytes 1597448 | tf_op jit(solution)/shard_map/ppermute | solution.py:42
  18.9 1.1 %collective-permute-start.12 = (bf16[2080,128]{1,0:T(8,128)(2,1)S(1)}, bf16[2080,128]{1,0:T(8,128)(2,1)S(1)}, u32[]{:S(2)}, u32[]{:S(2)}) collective-permute-start(bf16[2080,128]{1,0:T(8,128)(2,1)S(1)} %get-tuple-element.14.refs_0_), channel_id=1, source_target_pairs={{0,24},{4,100},{8,0},{12,108},{16,8},{20,116},{24,16},{28,124},{32... | collective-permute-start | bytes 1597448 | tf_op jit(solution)/shard_map/ppermute | solution.py:42
  20.0 2.6 %collective-permute-start.5 = (bf16[1040,128]{1,0:T(8,128)(2,1)S(1)}, bf16[1040,128]{1,0:T(8,128)(2,1)S(1)}, u32[]{:S(2)}, u32[]{:S(2)}) collective-permute-start(bf16[1040,128]{1,0:T(8,128)(2,1)S(1)} %get-tuple-element.15), channel_id=1, source_target_pairs={{0,2},{1,3},{2,0},{3,1},{4,6},{5,7},{6,4},{7,5},{8,10},{9,11},{10,... | collective-permute-start | bytes 798728 | tf_op jit(solution)/shard_map/ppermute | solution.py:162
  22.6 0.1 collective-permute-done.6.refs_6_
  22.8 0.1 collective-permute-start.7
  22.9 2.7 %collective-permute-start.9 = (bf16[1040,128]{1,0:T(8,128)(2,1)S(1)}, bf16[1040,128]{1,0:T(8,128)(2,1)S(1)}, u32[]{:S(2)}, u32[]{:S(2)}) collective-permute-start(bf16[1040,128]{1,0:T(8,128)(2,1)S(1)} %slice.17), channel_id=1, source_target_pairs={{0,24},{4,100},{8,0},{12,108},{16,8},{20,116},{24,16},{28,124},{32... | collective-permute-start | bytes 798728 | tf_op jit(solution)/shard_map/ppermute | solution.py:42
  25.6 2.8 %collective-permute-done.10.refs_8_ = bf16[2080,128]{1,0:T(8,128)(2,1)S(1)} collective-permute-done((bf16[2080,128]{1,0:T(8,128)(2,1)S(1)}, bf16[2080,128]{1,0:T(8,128)(2,1)S(1)}, u32[]{:S(2)}, u32[]{:S(2)}) %collective-permute-start.10) | collective-permute-done | bytes 532512 | tf_op jit(solution)/shard_map/ppermute | solution.py:42
  28.5 0.1 collective-permute-start.11
  28.6 2.7 %collective-permute-start.13 = (bf16[1040,128]{1,0:T(8,128)(2,1)S(1)}, bf16[1040,128]{1,0:T(8,128)(2,1)S(1)}, u32[]{:S(2)}, u32[]{:S(2)}) collective-permute-start(bf16[1040,128]{1,0:T(8,128)(2,1)S(1)} %slice.19), channel_id=1, source_target_pairs={{0,24},{4,100},{8,0},{12,108},{16,8},{20,116},{24,16},{28,124},{32... | collective-permute-start | bytes 798728 | tf_op jit(solution)/shard_map/ppermute | solution.py:42
  31.3 0.1 shard_map.47
  31.4 3.0 %collective-permute-start.14 = (bf16[4160,128]{1,0:T(8,128)(2,1)S(1)}, bf16[4160,128]{1,0:T(8,128)(2,1)S(1)}, u32[]{:S(2)}, u32[]{:S(2)}) collective-permute-start(bf16[4160,128]{1,0:T(8,128)(2,1)S(1)} %get-tuple-element.18), channel_id=1, source_target_pairs={{0,4},{4,0},{1,5},{5,1},{2,6},{6,2},{3,7},{7,3},{8,12},{12,8},{9,1... | collective-permute-start | bytes 3194888 | tf_op jit(solution)/shard_map/ppermute | solution.py:46
  34.4 0.1 collective-permute-start.17
  34.5 0.4 collective-permute-start.18
  34.9 0.4 collective-permute-done.11.refs_4_
  35.3 3.2 %collective-permute-start.19 = (bf16[1040,128]{1,0:T(8,128)(2,1)S(1)}, bf16[1040,128]{1,0:T(8,128)(2,1)S(1)}, u32[]{:S(2)}, u32[]{:S(2)}) collective-permute-start(bf16[1040,128]{1,0:T(8,128)(2,1)S(1)} %collective-permute-done.7.refs_2_), channel_id=1, source_target_pairs={{0,4},{4,0},{1,5},{5,1},{2,6},{6,2},{3,7},{7,3},{8,12},{12,8},{9,1... | collective-permute-start | bytes 798728 | tf_op jit(solution)/shard_map/ppermute | solution.py:46
  38.5 0.0 collective-permute-start.20
  38.5 1.2 %collective-permute-done.19.refs_15_ = bf16[1040,128]{1,0:T(8,128)(2,1)S(1)} collective-permute-done((bf16[1040,128]{1,0:T(8,128)(2,1)S(1)}, bf16[1040,128]{1,0:T(8,128)(2,1)S(1)}, u32[]{:S(2)}, u32[]{:S(2)}) %collective-permute-start.19) | collective-permute-done | bytes 266272 | tf_op jit(solution)/shard_map/ppermute | solution.py:46
  39.7 0.4 collective-permute-start.15
  40.0 0.0 collective-permute-done.20.refs_16_
  40.0 0.4 collective-permute-start.16
  40.4 0.1 collective-permute-start.21
  40.6 0.4 collective-permute-start.22
  40.9 1.8 %collective-permute-done.21.refs_17_ = bf16[1040,128]{1,0:T(8,128)(2,1)S(1)} collective-permute-done((bf16[1040,128]{1,0:T(8,128)(2,1)S(1)}, bf16[1040,128]{1,0:T(8,128)(2,1)S(1)}, u32[]{:S(2)}, u32[]{:S(2)}) %collective-permute-start.21) | collective-permute-done | bytes 266272 | tf_op jit(solution)/shard_map/ppermute | solution.py:46
  42.7 0.4 collective-permute-done.22.refs_18_
  43.1 0.0 copy-start
  43.1 2.4 %shard_map.48 = (f32[264,128]{1,0:T(8,128)S(1)}, f32[264,128]{1,0:T(8,128)S(1)}, f32[264,128]{1,0:T(8,128)S(1)}, f32[264,128]{1,0:T(8,128)S(1)}) custom-call(bf16[2,16,128,128]{3,2,1,0:T(8,128)(2,1)S(1)} %get-tuple-element.16.tiles_ref, s32[4,128]{1,0:T(4,128)S(1)} %get-tuple-element.17.right_ids_ref, bf16[2080,128]{1,0:T(8,128)(2,1)S(1)} %get-tuple-element.14.refs_0_, ...), custom_call_target="tpu_custom_call" | custom-call | flops 536870912 | bytes 10485760 | tf_op jit(solution)/shard_map/pallas_call | solution.py:199
  45.5 3.0 %collective-permute-start.23 = (f32[264,128]{1,0:T(8,128)S(1)}, f32[264,128]{1,0:T(8,128)S(1)}, u32[]{:S(2)}, u32[]{:S(2)}) collective-permute-start(f32[264,128]{1,0:T(8,128)S(1)} %get-tuple-element.20), channel_id=1, source_target_pairs={{0,2},{1,3},{2,0},{3,1},{4,6},{5,7},{6,4},{7,5},{8,10},{9,11},{10,... | collective-permute-start | bytes 405512 | tf_op jit(solution)/shard_map/ppermute | solution.py:216
  48.5 0.4 collective-permute-start.24
  48.9 2.3 %collective-permute-start.25 = (f32[264,128]{1,0:T(8,128)S(1)}, f32[264,128]{1,0:T(8,128)S(1)}, u32[]{:S(2)}, u32[]{:S(2)}) collective-permute-start(f32[264,128]{1,0:T(8,128)S(1)} %get-tuple-element.22), channel_id=1, source_target_pairs={{0,3},{1,0},{2,1},{3,2},{4,7},{5,4},{6,5},{7,6},{8,11},{9,8},{10,9... | collective-permute-start | bytes 405512 | tf_op jit(solution)/shard_map/ppermute | solution.py:216
  51.2 0.7 %collective-permute-done.23.refs_1_ = f32[264,128]{1,0:T(8,128)S(1)} collective-permute-done((f32[264,128]{1,0:T(8,128)S(1)}, f32[264,128]{1,0:T(8,128)S(1)}, u32[]{:S(2)}, u32[]{:S(2)}) %collective-permute-start.23) | collective-permute-done | bytes 135200 | tf_op jit(solution)/shard_map/ppermute | solution.py:216
  51.9 3.4 %collective-permute-done.24.refs_2_ = f32[264,128]{1,0:T(8,128)S(1)} collective-permute-done((f32[264,128]{1,0:T(8,128)S(1)}, f32[264,128]{1,0:T(8,128)S(1)}, u32[]{:S(2)}, u32[]{:S(2)}) %collective-permute-start.24) | collective-permute-done | bytes 135200 | tf_op jit(solution)/shard_map/ppermute | solution.py:216
  55.3 0.8 %shard_map.49 = bf16[2,4,1,128,128]{4,3,2,1,0:T(8,128)(2,1)} custom-call(s32[2,4,128]{2,1,0:T(4,128)S(1)} %copy-done, f32[264,128]{1,0:T(8,128)S(1)} %get-tuple-element.19.refs_0_, f32[264,128]{1,0:T(8,128)S(1)} %collective-permute-done.23.refs_1_, f32[264,128]{1,0:T(8,128)S(1)} %collective-permute-done.24.refs_2_, ...), custom_call_target="tpu_custom_call" | custom-call | tf_op jit(solution)/shard_map/pallas_call | solution.py:217
  (25 shorter events, 0.2 us)
Async XLA Ops:
  2.0 8.7 %collective-permute-start.3 = (bf16[1040,128]{1,0:T(8,128)(2,1)S(1)}, bf16[1040,128]{1,0:T(8,128)(2,1)S(1)}, u32[]{:S(2)}, u32[]{:S(2)}) collective-permute-start(bf16[1040,128]{1,0:T(8,128)(2,1)S(1)} %pad_maximum_fusion.refs_0_.refs_2_), channel_id=1, source_target_pairs={{0,32},{4,12},{8,40},{12,20},{16,48},{20,28},{24,56},{28,4},{32,64... | collective-permute-start | bytes 798728 | tf_op jit(solution)/shard_map/ppermute | solution.py:42
  4.6 8.4 %collective-permute-start.4 = (bf16[1040,128]{1,0:T(8,128)(2,1)S(1)}, bf16[1040,128]{1,0:T(8,128)(2,1)S(1)}, u32[]{:S(2)}, u32[]{:S(2)}) collective-permute-start(bf16[1040,128]{1,0:T(8,128)(2,1)S(1)} %pad_maximum_fusion.refs_0_.refs_2_), channel_id=1, source_target_pairs={{0,96},{4,28},{8,104},{12,4},{16,112},{20,12},{24,120},{28,20},{32... | collective-permute-start | bytes 798728 | tf_op jit(solution)/shard_map/ppermute | solution.py:42
  6.8 9.0 %collective-permute-start = (bf16[1040,128]{1,0:T(8,128)(2,1)S(1)}, bf16[1040,128]{1,0:T(8,128)(2,1)S(1)}, u32[]{:S(2)}, u32[]{:S(2)}) collective-permute-start(bf16[1040,128]{1,0:T(8,128)(2,1)S(1)} %pad_maximum_fusion.refs_0_.refs_2_), channel_id=1, source_target_pairs={{0,64},{4,20},{8,72},{12,28},{16,80},{20,4},{24,88},{28,12},{32,96... | collective-permute-start | bytes 798728 | tf_op jit(solution)/shard_map/ppermute | solution.py:42
  8.0 8.6 %collective-permute-start.1 = (bf16[1040,128]{1,0:T(8,128)(2,1)S(1)}, bf16[1040,128]{1,0:T(8,128)(2,1)S(1)}, u32[]{:S(2)}, u32[]{:S(2)}) collective-permute-start(bf16[1040,128]{1,0:T(8,128)(2,1)S(1)} %pad_maximum_fusion.refs_0_.refs_2_), channel_id=1, source_target_pairs={{0,1},{1,2},{2,3},{3,0},{4,5},{5,6},{6,7},{7,4},{8,9},{9,10},{10,1... | collective-permute-start | bytes 798728 | tf_op jit(solution)/shard_map/ppermute | solution.py:152
  9.3 7.3 %collective-permute-start.2 = (bf16[1040,128]{1,0:T(8,128)(2,1)S(1)}, bf16[1040,128]{1,0:T(8,128)(2,1)S(1)}, u32[]{:S(2)}, u32[]{:S(2)}) collective-permute-start(bf16[1040,128]{1,0:T(8,128)(2,1)S(1)} %pad_maximum_fusion.refs_0_.refs_2_), channel_id=1, source_target_pairs={{0,3},{1,0},{2,1},{3,2},{4,7},{5,4},{6,5},{7,6},{8,11},{9,8},{10,9... | collective-permute-start | bytes 798728 | tf_op jit(solution)/shard_map/ppermute | solution.py:152
  13.0 9.7 %collective-permute-start.6 = (bf16[2080,128]{1,0:T(8,128)(2,1)S(1)}, bf16[2080,128]{1,0:T(8,128)(2,1)S(1)}, u32[]{:S(2)}, u32[]{:S(2)}) collective-permute-start(bf16[2080,128]{1,0:T(8,128)(2,1)S(1)} %constant_dynamic-update-slice_fusion.refs_1_), channel_id=1, source_target_pairs={{0,8},{4,36},{8,16},{12,44},{16,24},{20,52},{24,0},{28,60},{32,40}... | collective-permute-start | bytes 1597448 | tf_op jit(solution)/shard_map/ppermute | solution.py:42
  14.3 8.6 %collective-permute-start.8 = (bf16[2080,128]{1,0:T(8,128)(2,1)S(1)}, bf16[2080,128]{1,0:T(8,128)(2,1)S(1)}, u32[]{:S(2)}, u32[]{:S(2)}) collective-permute-start(bf16[2080,128]{1,0:T(8,128)(2,1)S(1)} %constant_dynamic-update-slice_fusion.refs_1_), channel_id=1, source_target_pairs={{0,24},{4,100},{8,0},{12,108},{16,8},{20,116},{24,16},{28,124},{32... | collective-permute-start | bytes 1597448 | tf_op jit(solution)/shard_map/ppermute | solution.py:42
  16.7 11.8 %collective-permute-start.10 = (bf16[2080,128]{1,0:T(8,128)(2,1)S(1)}, bf16[2080,128]{1,0:T(8,128)(2,1)S(1)}, u32[]{:S(2)}, u32[]{:S(2)}) collective-permute-start(bf16[2080,128]{1,0:T(8,128)(2,1)S(1)} %get-tuple-element.14.refs_0_), channel_id=1, source_target_pairs={{0,8},{4,36},{8,16},{12,44},{16,24},{20,52},{24,0},{28,60},{32,40}... | collective-permute-start | bytes 1597448 | tf_op jit(solution)/shard_map/ppermute | solution.py:42
  18.9 9.7 %collective-permute-start.12 = (bf16[2080,128]{1,0:T(8,128)(2,1)S(1)}, bf16[2080,128]{1,0:T(8,128)(2,1)S(1)}, u32[]{:S(2)}, u32[]{:S(2)}) collective-permute-start(bf16[2080,128]{1,0:T(8,128)(2,1)S(1)} %get-tuple-element.14.refs_0_), channel_id=1, source_target_pairs={{0,24},{4,100},{8,0},{12,108},{16,8},{20,116},{24,16},{28,124},{32... | collective-permute-start | bytes 1597448 | tf_op jit(solution)/shard_map/ppermute | solution.py:42
  20.0 11.3 %collective-permute-start.5 = (bf16[1040,128]{1,0:T(8,128)(2,1)S(1)}, bf16[1040,128]{1,0:T(8,128)(2,1)S(1)}, u32[]{:S(2)}, u32[]{:S(2)}) collective-permute-start(bf16[1040,128]{1,0:T(8,128)(2,1)S(1)} %get-tuple-element.15), channel_id=1, source_target_pairs={{0,2},{1,3},{2,0},{3,1},{4,6},{5,7},{6,4},{7,5},{8,10},{9,11},{10,... | collective-permute-start | bytes 798728 | tf_op jit(solution)/shard_map/ppermute | solution.py:162
  22.8 11.7 %collective-permute-start.7 = (bf16[1040,128]{1,0:T(8,128)(2,1)S(1)}, bf16[1040,128]{1,0:T(8,128)(2,1)S(1)}, u32[]{:S(2)}, u32[]{:S(2)}) collective-permute-start(bf16[1040,128]{1,0:T(8,128)(2,1)S(1)} %slice.16), channel_id=1, source_target_pairs={{0,8},{4,36},{8,16},{12,44},{16,24},{20,52},{24,0},{28,60},{32,40}... | collective-permute-start | bytes 798728 | tf_op jit(solution)/shard_map/ppermute | solution.py:42
  22.9 11.6 %collective-permute-start.9 = (bf16[1040,128]{1,0:T(8,128)(2,1)S(1)}, bf16[1040,128]{1,0:T(8,128)(2,1)S(1)}, u32[]{:S(2)}, u32[]{:S(2)}) collective-permute-start(bf16[1040,128]{1,0:T(8,128)(2,1)S(1)} %slice.17), channel_id=1, source_target_pairs={{0,24},{4,100},{8,0},{12,108},{16,8},{20,116},{24,16},{28,124},{32... | collective-permute-start | bytes 798728 | tf_op jit(solution)/shard_map/ppermute | solution.py:42
  28.5 6.8 %collective-permute-start.11 = (bf16[1040,128]{1,0:T(8,128)(2,1)S(1)}, bf16[1040,128]{1,0:T(8,128)(2,1)S(1)}, u32[]{:S(2)}, u32[]{:S(2)}) collective-permute-start(bf16[1040,128]{1,0:T(8,128)(2,1)S(1)} %slice.18), channel_id=1, source_target_pairs={{0,8},{4,36},{8,16},{12,44},{16,24},{20,52},{24,0},{28,60},{32,40}... | collective-permute-start | bytes 798728 | tf_op jit(solution)/shard_map/ppermute | solution.py:42
  28.6 9.9 %collective-permute-start.13 = (bf16[1040,128]{1,0:T(8,128)(2,1)S(1)}, bf16[1040,128]{1,0:T(8,128)(2,1)S(1)}, u32[]{:S(2)}, u32[]{:S(2)}) collective-permute-start(bf16[1040,128]{1,0:T(8,128)(2,1)S(1)} %slice.19), channel_id=1, source_target_pairs={{0,24},{4,100},{8,0},{12,108},{16,8},{20,116},{24,16},{28,124},{32... | collective-permute-start | bytes 798728 | tf_op jit(solution)/shard_map/ppermute | solution.py:42
  31.4 11.7 %collective-permute-start.14 = (bf16[4160,128]{1,0:T(8,128)(2,1)S(1)}, bf16[4160,128]{1,0:T(8,128)(2,1)S(1)}, u32[]{:S(2)}, u32[]{:S(2)}) collective-permute-start(bf16[4160,128]{1,0:T(8,128)(2,1)S(1)} %get-tuple-element.18), channel_id=1, source_target_pairs={{0,4},{4,0},{1,5},{5,1},{2,6},{6,2},{3,7},{7,3},{8,12},{12,8},{9,1... | collective-permute-start | bytes 3194888 | tf_op jit(solution)/shard_map/ppermute | solution.py:46
  34.4 6.0 %collective-permute-start.17 = (bf16[2080,128]{1,0:T(8,128)(2,1)S(1)}, bf16[2080,128]{1,0:T(8,128)(2,1)S(1)}, u32[]{:S(2)}, u32[]{:S(2)}) collective-permute-start(bf16[2080,128]{1,0:T(8,128)(2,1)S(1)} %collective-permute-done.6.refs_6_), channel_id=1, source_target_pairs={{0,4},{4,0},{1,5},{5,1},{2,6},{6,2},{3,7},{7,3},{8,12},{12,8},{9,1... | collective-permute-start | bytes 1597448 | tf_op jit(solution)/shard_map/ppermute | solution.py:46
  34.5 6.0 %collective-permute-start.18 = (bf16[2080,128]{1,0:T(8,128)(2,1)S(1)}, bf16[2080,128]{1,0:T(8,128)(2,1)S(1)}, u32[]{:S(2)}, u32[]{:S(2)}) collective-permute-start(bf16[2080,128]{1,0:T(8,128)(2,1)S(1)} %collective-permute-done.8.refs_7_), channel_id=1, source_target_pairs={{0,4},{4,0},{1,5},{5,1},{2,6},{6,2},{3,7},{7,3},{8,12},{12,8},{9,1... | collective-permute-start | bytes 1597448 | tf_op jit(solution)/shard_map/ppermute | solution.py:46
  35.3 4.4 %collective-permute-start.19 = (bf16[1040,128]{1,0:T(8,128)(2,1)S(1)}, bf16[1040,128]{1,0:T(8,128)(2,1)S(1)}, u32[]{:S(2)}, u32[]{:S(2)}) collective-permute-start(bf16[1040,128]{1,0:T(8,128)(2,1)S(1)} %collective-permute-done.7.refs_2_), channel_id=1, source_target_pairs={{0,4},{4,0},{1,5},{5,1},{2,6},{6,2},{3,7},{7,3},{8,12},{12,8},{9,1... | collective-permute-start | bytes 798728 | tf_op jit(solution)/shard_map/ppermute | solution.py:46
  38.5 1.5 %collective-permute-start.20 = (bf16[1040,128]{1,0:T(8,128)(2,1)S(1)}, bf16[1040,128]{1,0:T(8,128)(2,1)S(1)}, u32[]{:S(2)}, u32[]{:S(2)}) collective-permute-start(bf16[1040,128]{1,0:T(8,128)(2,1)S(1)} %collective-permute-done.9.refs_3_), channel_id=1, source_target_pairs={{0,4},{4,0},{1,5},{5,1},{2,6},{6,2},{3,7},{7,3},{8,12},{12,8},{9,1... | collective-permute-start | bytes 798728 | tf_op jit(solution)/shard_map/ppermute | solution.py:46
  39.7 3.4 %collective-permute-start.15 = (bf16[2080,128]{1,0:T(8,128)(2,1)S(1)}, bf16[2080,128]{1,0:T(8,128)(2,1)S(1)}, u32[]{:S(2)}, u32[]{:S(2)}) collective-permute-start(bf16[2080,128]{1,0:T(8,128)(2,1)S(1)} %collective-permute-done.10.refs_8_), channel_id=1, source_target_pairs={{0,4},{4,0},{1,5},{5,1},{2,6},{6,2},{3,7},{7,3},{8,12},{12,8},{9,1... | collective-permute-start | bytes 1597448 | tf_op jit(solution)/shard_map/ppermute | solution.py:46
  40.0 3.1 %collective-permute-start.16 = (bf16[2080,128]{1,0:T(8,128)(2,1)S(1)}, bf16[2080,128]{1,0:T(8,128)(2,1)S(1)}, u32[]{:S(2)}, u32[]{:S(2)}) collective-permute-start(bf16[2080,128]{1,0:T(8,128)(2,1)S(1)} %collective-permute-done.12.refs_9_), channel_id=1, source_target_pairs={{0,4},{4,0},{1,5},{5,1},{2,6},{6,2},{3,7},{7,3},{8,12},{12,8},{9,1... | collective-permute-start | bytes 1597448 | tf_op jit(solution)/shard_map/ppermute | solution.py:46
  40.4 2.3 %collective-permute-start.21 = (bf16[1040,128]{1,0:T(8,128)(2,1)S(1)}, bf16[1040,128]{1,0:T(8,128)(2,1)S(1)}, u32[]{:S(2)}, u32[]{:S(2)}) collective-permute-start(bf16[1040,128]{1,0:T(8,128)(2,1)S(1)} %collective-permute-done.11.refs_4_), channel_id=1, source_target_pairs={{0,4},{4,0},{1,5},{5,1},{2,6},{6,2},{3,7},{7,3},{8,12},{12,8},{9,1... | collective-permute-start | bytes 798728 | tf_op jit(solution)/shard_map/ppermute | solution.py:46
  40.6 2.5 %collective-permute-start.22 = (bf16[1040,128]{1,0:T(8,128)(2,1)S(1)}, bf16[1040,128]{1,0:T(8,128)(2,1)S(1)}, u32[]{:S(2)}, u32[]{:S(2)}) collective-permute-start(bf16[1040,128]{1,0:T(8,128)(2,1)S(1)} %collective-permute-done.13.refs_5_), channel_id=1, source_target_pairs={{0,4},{4,0},{1,5},{5,1},{2,6},{6,2},{3,7},{7,3},{8,12},{12,8},{9,1... | collective-permute-start | bytes 798728 | tf_op jit(solution)/shard_map/ppermute | solution.py:46
  43.1 12.2 %copy-start = (s32[2,4,128]{2,1,0:T(4,128)S(1)}, s32[2,4,128]{2,1,0:T(4,128)}, u32[]{:S(2)}) copy-start(s32[2,4,128]{2,1,0:T(4,128)} %mask_ref.1) | copy-start | bytes 12292
  45.5 6.4 %collective-permute-start.23 = (f32[264,128]{1,0:T(8,128)S(1)}, f32[264,128]{1,0:T(8,128)S(1)}, u32[]{:S(2)}, u32[]{:S(2)}) collective-permute-start(f32[264,128]{1,0:T(8,128)S(1)} %get-tuple-element.20), channel_id=1, source_target_pairs={{0,2},{1,3},{2,0},{3,1},{4,6},{5,7},{6,4},{7,5},{8,10},{9,11},{10,... | collective-permute-start | bytes 405512 | tf_op jit(solution)/shard_map/ppermute | solution.py:216
  48.5 6.8 %collective-permute-start.24 = (f32[264,128]{1,0:T(8,128)S(1)}, f32[264,128]{1,0:T(8,128)S(1)}, u32[]{:S(2)}, u32[]{:S(2)}) collective-permute-start(f32[264,128]{1,0:T(8,128)S(1)} %get-tuple-element.21), channel_id=1, source_target_pairs={{0,1},{1,2},{2,3},{3,0},{4,5},{5,6},{6,7},{7,4},{8,9},{9,10},{10,1... | collective-permute-start | bytes 405512 | tf_op jit(solution)/shard_map/ppermute | solution.py:216
  48.9 6.4 %collective-permute-start.25 = (f32[264,128]{1,0:T(8,128)S(1)}, f32[264,128]{1,0:T(8,128)S(1)}, u32[]{:S(2)}, u32[]{:S(2)}) collective-permute-start(f32[264,128]{1,0:T(8,128)S(1)} %get-tuple-element.22), channel_id=1, source_target_pairs={{0,3},{1,0},{2,1},{3,2},{4,7},{5,4},{6,5},{7,6},{8,11},{9,8},{10,9... | collective-permute-start | bytes 405512 | tf_op jit(solution)/shard_map/ppermute | solution.py:216

commit v7 on v6

--- a/solution.py
+++ b/solution.py
@@ -52,11 +52,15 @@
 
 def id_rows(band_rows, kept_rows):
     cell = cell_number(*(lax.axis_index(name) for name in CELL))
-    rows = jnp.concatenate([band_rows[:, 0], kept_rows[:, 0]], axis=1).reshape(1, LANES)
     row = lax.broadcasted_iota(jnp.int32, (16, TILE), 0)
-    group = lax.broadcasted_iota(jnp.int32, (16, TILE), 1) // LANES
+    lane = lax.broadcasted_iota(jnp.int32, (16, TILE), 1)
+    group = lane // LANES
     here = ((row == cell // GROUP) & (group == cell % GROUP)) | ((row == GROUP) & (group == 0))
-    return jnp.where(here, jnp.tile(rows, (1, GROUP)), 0).astype(jnp.bfloat16)
+    shape = (16, TILE, PANELS, SLOTS)
+    spot = lax.broadcasted_iota(jnp.int32, shape, 2) * GROUP + lax.broadcasted_iota(jnp.int32, shape, 3)
+    place = (lane % LANES)[:, :, None, None]
+    ids = jnp.where(place == spot, band_rows[:, 0], 0) + jnp.where(place == spot + SLOTS, kept_rows[:, 0], 0)
+    return jnp.where(here, jnp.sum(ids, axis=(2, 3)), 0).astype(jnp.bfloat16)
 
 
 def buffer_kernel(count, *refs):

time: 56.7 us -> 56.6 us (level)
    reduce_sum x0 -> x1, other arithmetic: none -> 0.78 us  [id_rows(): return jnp.where(here, jnp.sum(ids, axis=(2, 3)), 0).astype(jnp.bfloat16)]
    concatenate x1 -> x0, other arithmetic: 0.77 us -> none  [id_rows(): jnp.concatenate([band_rows[:, 0], kept_rows[:, 0]], axis=1)]
where the time goes in v7:
time: 56.6 us; the launch traced here: 56 us
  starting transfers between devices  36.6 us (65%)
  waiting for transfers between devices  13.9 us (25%)
  Pallas kernels  3.37 us (6%)
  other arithmetic  1.87 us (3%)
    ppermute x11, starting transfers between devices, along(): return lax.ppermute(value, CELL, cells(steps[axis], steps[1 - axis]))  17.6 us
    ppermute x9, starting transfers between devices, swap(): return lax.ppermute(value, 'core', [(0, 1), (1, 0)])  7.93 us
    ppermute x3, starting transfers between devices, per_device(): lax.ppermute(chunks[s], 'layer', ring(chunk_shifts[s]))  5.66 us
    ppermute x11, waiting for transfers between devices, along(): return lax.ppermute(value, CELL, cells(steps[axis], steps[1 - axis]))  5.59 us
    ppermute x3, waiting for transfers between devices, per_device(): lax.ppermute(chunks[s], 'layer', ring(chunk_shifts[s]))  4.09 us
    ppermute x9, waiting for transfers between devices, swap(): return lax.ppermute(value, 'core', [(0, 1), (1, 0)])  3.35 us
    ppermute x2, starting transfers between devices, per_device(): rights = [lax.ppermute(unit, 'layer', ring(s)) for s in (1, 3)]  2.74 us
    ppermute x1, starting transfers between devices, per_device(): rights = [unit, *rights, lax.ppermute(unit_again, 'layer', ring(2))]  2.62 us
  transfers between devices with their start and end apart: 26, of which 10 were waited for; matrix products, arithmetic and copies ran while one was open for 0% of the time, Pallas kernels for 0%

profile of v7, /device:TPU:1, one launch (start us, length us, event | category | flops | bytes accessed | tf_op | source)
XLA Modules:
  0.0 56.0 jit_solution(5775415875103830388)
XLA Ops:
  0.1 0.8 %add_reduce_fusion = s32[16,128]{1,0:T(8,128)S(1)} fusion(s32[2,4]{1,0:T(2,128)} %bitcast.4, s32[2,4]{1,0:T(2,128)} %bitcast.5, s32[2]{0:T(128)S(1)} %iota_multiply_fusion, s32[16,128]{1,0:T(8,128)S(1)} %broadcast_select_fusion), kind=kLoop, calls=%fused_computation.1 | loop fusion | flops 129024 | bytes 16456 | tf_op jit(solution)/shard_map/reduce_sum | solution.py:63
  0.9 0.1 select_convert_fusion
  1.0 1.0 %pad_maximum_fusion.refs_0_.refs_2_ = bf16[1040,128]{1,0:T(8,128)(2,1)S(1)} fusion(bf16[16,128]{1,0:T(8,128)(2,1)S(1)} %select_convert_fusion, bf16[1024,128]{1,0:T(8,128)(2,1)} %bitcast.3), kind=kLoop, calls=%fused_computation | loop fusion | flops 532480 | bytes 532480 | tf_op jit(solution)/shard_map/concatenate | solution.py:155
  1.9 2.5 %collective-permute-start.3 = (bf16[1040,128]{1,0:T(8,128)(2,1)S(1)}, bf16[1040,128]{1,0:T(8,128)(2,1)S(1)}, u32[]{:S(2)}, u32[]{:S(2)}) collective-permute-start(bf16[1040,128]{1,0:T(8,128)(2,1)S(1)} %pad_maximum_fusion.refs_0_.refs_2_), channel_id=1, source_target_pairs={{0,32},{4,12},{8,40},{12,20},{16,48},{20,28},{24,56},{28,4},{32,64... | collective-permute-start | bytes 798728 | tf_op jit(solution)/shard_map/ppermute | solution.py:42
  4.5 2.2 %collective-permute-start.4 = (bf16[1040,128]{1,0:T(8,128)(2,1)S(1)}, bf16[1040,128]{1,0:T(8,128)(2,1)S(1)}, u32[]{:S(2)}, u32[]{:S(2)}) collective-permute-start(bf16[1040,128]{1,0:T(8,128)(2,1)S(1)} %pad_maximum_fusion.refs_0_.refs_2_), channel_id=1, source_target_pairs={{0,96},{4,28},{8,104},{12,4},{16,112},{20,12},{24,120},{28,20},{32... | collective-permute-start | bytes 798728 | tf_op jit(solution)/shard_map/ppermute | solution.py:42
  6.7 1.2 %collective-permute-start = (bf16[1040,128]{1,0:T(8,128)(2,1)S(1)}, bf16[1040,128]{1,0:T(8,128)(2,1)S(1)}, u32[]{:S(2)}, u32[]{:S(2)}) collective-permute-start(bf16[1040,128]{1,0:T(8,128)(2,1)S(1)} %pad_maximum_fusion.refs_0_.refs_2_), channel_id=1, source_target_pairs={{0,64},{4,20},{8,72},{12,28},{16,80},{20,4},{24,88},{28,12},{32,96... | collective-permute-start | bytes 798728 | tf_op jit(solution)/shard_map/ppermute | solution.py:42
  7.9 1.3 %collective-permute-start.1 = (bf16[1040,128]{1,0:T(8,128)(2,1)S(1)}, bf16[1040,128]{1,0:T(8,128)(2,1)S(1)}, u32[]{:S(2)}, u32[]{:S(2)}) collective-permute-start(bf16[1040,128]{1,0:T(8,128)(2,1)S(1)} %pad_maximum_fusion.refs_0_.refs_2_), channel_id=1, source_target_pairs={{0,1},{1,2},{2,3},{3,0},{4,5},{5,6},{6,7},{7,4},{8,9},{9,10},{10,1... | collective-permute-start | bytes 798728 | tf_op jit(solution)/shard_map/ppermute | solution.py:156
  9.2 1.4 %collective-permute-start.2 = (bf16[1040,128]{1,0:T(8,128)(2,1)S(1)}, bf16[1040,128]{1,0:T(8,128)(2,1)S(1)}, u32[]{:S(2)}, u32[]{:S(2)}) collective-permute-start(bf16[1040,128]{1,0:T(8,128)(2,1)S(1)} %pad_maximum_fusion.refs_0_.refs_2_), channel_id=1, source_target_pairs={{0,3},{1,0},{2,1},{3,2},{4,7},{5,4},{6,5},{7,6},{8,11},{9,8},{10,9... | collective-permute-start | bytes 798728 | tf_op jit(solution)/shard_map/ppermute | solution.py:156
  10.6 0.0 collective-permute-done.3
  10.7 2.2 %collective-permute-done.4 = bf16[1040,128]{1,0:T(8,128)(2,1)S(1)} collective-permute-done((bf16[1040,128]{1,0:T(8,128)(2,1)S(1)}, bf16[1040,128]{1,0:T(8,128)(2,1)S(1)}, u32[]{:S(2)}, u32[]{:S(2)}) %collective-permute-start.4) | collective-permute-done | bytes 266272 | tf_op jit(solution)/shard_map/ppermute | solution.py:42
  12.9 1.3 %collective-permute-start.6 = (bf16[2080,128]{1,0:T(8,128)(2,1)S(1)}, bf16[2080,128]{1,0:T(8,128)(2,1)S(1)}, u32[]{:S(2)}, u32[]{:S(2)}) collective-permute-start(bf16[2080,128]{1,0:T(8,128)(2,1)S(1)} %constant_dynamic-update-slice_fusion.refs_1_), channel_id=1, source_target_pairs={{0,8},{4,36},{8,16},{12,44},{16,24},{20,52},{24,0},{28,60},{32,40}... | collective-permute-start | bytes 1597448 | tf_op jit(solution)/shard_map/ppermute | solution.py:42
  14.2 1.5 %collective-permute-start.8 = (bf16[2080,128]{1,0:T(8,128)(2,1)S(1)}, bf16[2080,128]{1,0:T(8,128)(2,1)S(1)}, u32[]{:S(2)}, u32[]{:S(2)}) collective-permute-start(bf16[2080,128]{1,0:T(8,128)(2,1)S(1)} %constant_dynamic-update-slice_fusion.refs_1_), channel_id=1, source_target_pairs={{0,24},{4,100},{8,0},{12,108},{16,8},{20,116},{24,16},{28,124},{32... | collective-permute-start | bytes 1597448 | tf_op jit(solution)/shard_map/ppermute | solution.py:42
  15.7 0.0 collective-permute-done.refs_1_
  15.7 0.8 %collective-permute-done.1.refs_2_.refs_3_ = bf16[1040,128]{1,0:T(8,128)(2,1)S(1)} collective-permute-done((bf16[1040,128]{1,0:T(8,128)(2,1)S(1)}, bf16[1040,128]{1,0:T(8,128)(2,1)S(1)}, u32[]{:S(2)}, u32[]{:S(2)}) %collective-permute-start.1) | collective-permute-done | bytes 266272 | tf_op jit(solution)/shard_map/ppermute | solution.py:156
  16.5 0.1 shard_map.46
  16.6 2.2 %collective-permute-start.10 = (bf16[2080,128]{1,0:T(8,128)(2,1)S(1)}, bf16[2080,128]{1,0:T(8,128)(2,1)S(1)}, u32[]{:S(2)}, u32[]{:S(2)}) collective-permute-start(bf16[2080,128]{1,0:T(8,128)(2,1)S(1)} %get-tuple-element.14.refs_0_), channel_id=1, source_target_pairs={{0,8},{4,36},{8,16},{12,44},{16,24},{20,52},{24,0},{28,60},{32,40}... | collective-permute-start | bytes 1597448 | tf_op jit(solution)/shard_map/ppermute | solution.py:42
  18.8 1.1 %collective-permute-start.12 = (bf16[2080,128]{1,0:T(8,128)(2,1)S(1)}, bf16[2080,128]{1,0:T(8,128)(2,1)S(1)}, u32[]{:S(2)}, u32[]{:S(2)}) collective-permute-start(bf16[2080,128]{1,0:T(8,128)(2,1)S(1)} %get-tuple-element.14.refs_0_), channel_id=1, source_target_pairs={{0,24},{4,100},{8,0},{12,108},{16,8},{20,116},{24,16},{28,124},{32... | collective-permute-start | bytes 1597448 | tf_op jit(solution)/shard_map/ppermute | solution.py:42
  19.9 2.6 %collective-permute-start.5 = (bf16[1040,128]{1,0:T(8,128)(2,1)S(1)}, bf16[1040,128]{1,0:T(8,128)(2,1)S(1)}, u32[]{:S(2)}, u32[]{:S(2)}) collective-permute-start(bf16[1040,128]{1,0:T(8,128)(2,1)S(1)} %get-tuple-element.15), channel_id=1, source_target_pairs={{0,2},{1,3},{2,0},{3,1},{4,6},{5,7},{6,4},{7,5},{8,10},{9,11},{10,... | collective-permute-start | bytes 798728 | tf_op jit(solution)/shard_map/ppermute | solution.py:166
  22.5 0.1 collective-permute-done.6.refs_6_
  22.6 0.1 collective-permute-start.7
  22.8 2.7 %collective-permute-start.9 = (bf16[1040,128]{1,0:T(8,128)(2,1)S(1)}, bf16[1040,128]{1,0:T(8,128)(2,1)S(1)}, u32[]{:S(2)}, u32[]{:S(2)}) collective-permute-start(bf16[1040,128]{1,0:T(8,128)(2,1)S(1)} %slice.17), channel_id=1, source_target_pairs={{0,24},{4,100},{8,0},{12,108},{16,8},{20,116},{24,16},{28,124},{32... | collective-permute-start | bytes 798728 | tf_op jit(solution)/shard_map/ppermute | solution.py:42
  25.5 2.8 %collective-permute-done.10.refs_8_ = bf16[2080,128]{1,0:T(8,128)(2,1)S(1)} collective-permute-done((bf16[2080,128]{1,0:T(8,128)(2,1)S(1)}, bf16[2080,128]{1,0:T(8,128)(2,1)S(1)}, u32[]{:S(2)}, u32[]{:S(2)}) %collective-permute-start.10) | collective-permute-done | bytes 532512 | tf_op jit(solution)/shard_map/ppermute | solution.py:42
  28.4 0.1 collective-permute-start.11
  28.4 0.0 collective-permute-done.12.refs_9_
  28.5 2.7 %collective-permute-start.13 = (bf16[1040,128]{1,0:T(8,128)(2,1)S(1)}, bf16[1040,128]{1,0:T(8,128)(2,1)S(1)}, u32[]{:S(2)}, u32[]{:S(2)}) collective-permute-start(bf16[1040,128]{1,0:T(8,128)(2,1)S(1)} %slice.19), channel_id=1, source_target_pairs={{0,24},{4,100},{8,0},{12,108},{16,8},{20,116},{24,16},{28,124},{32... | collective-permute-start | bytes 798728 | tf_op jit(solution)/shard_map/ppermute | solution.py:42
  31.2 0.1 shard_map.47
  31.3 3.0 %collective-permute-start.14 = (bf16[4160,128]{1,0:T(8,128)(2,1)S(1)}, bf16[4160,128]{1,0:T(8,128)(2,1)S(1)}, u32[]{:S(2)}, u32[]{:S(2)}) collective-permute-start(bf16[4160,128]{1,0:T(8,128)(2,1)S(1)} %get-tuple-element.18), channel_id=1, source_target_pairs={{0,4},{4,0},{1,5},{5,1},{2,6},{6,2},{3,7},{7,3},{8,12},{12,8},{9,1... | collective-permute-start | bytes 3194888 | tf_op jit(solution)/shard_map/ppermute | solution.py:46
  34.3 0.1 collective-permute-start.17
  34.4 0.4 collective-permute-start.18
  34.8 0.4 collective-permute-done.11.refs_4_
  35.2 3.2 %collective-permute-start.19 = (bf16[1040,128]{1,0:T(8,128)(2,1)S(1)}, bf16[1040,128]{1,0:T(8,128)(2,1)S(1)}, u32[]{:S(2)}, u32[]{:S(2)}) collective-permute-start(bf16[1040,128]{1,0:T(8,128)(2,1)S(1)} %collective-permute-done.7.refs_2_), channel_id=1, source_target_pairs={{0,4},{4,0},{1,5},{5,1},{2,6},{6,2},{3,7},{7,3},{8,12},{12,8},{9,1... | collective-permute-start | bytes 798728 | tf_op jit(solution)/shard_map/ppermute | solution.py:46
  38.4 0.0 collective-permute-start.20
  38.4 1.2 %collective-permute-done.19.refs_15_ = bf16[1040,128]{1,0:T(8,128)(2,1)S(1)} collective-permute-done((bf16[1040,128]{1,0:T(8,128)(2,1)S(1)}, bf16[1040,128]{1,0:T(8,128)(2,1)S(1)}, u32[]{:S(2)}, u32[]{:S(2)}) %collective-permute-start.19) | collective-permute-done | bytes 266272 | tf_op jit(solution)/shard_map/ppermute | solution.py:46
  39.5 0.4 collective-permute-start.15
  39.9 0.0 collective-permute-done.20.refs_16_
  39.9 0.4 collective-permute-start.16
  40.3 0.1 collective-permute-start.21
  40.4 0.4 collective-permute-start.22
  40.8 1.8 %collective-permute-done.21.refs_17_ = bf16[1040,128]{1,0:T(8,128)(2,1)S(1)} collective-permute-done((bf16[1040,128]{1,0:T(8,128)(2,1)S(1)}, bf16[1040,128]{1,0:T(8,128)(2,1)S(1)}, u32[]{:S(2)}, u32[]{:S(2)}) %collective-permute-start.21) | collective-permute-done | bytes 266272 | tf_op jit(solution)/shard_map/ppermute | solution.py:46
  42.6 0.4 collective-permute-done.22.refs_18_
  43.0 0.0 copy-start
  43.0 2.4 %shard_map.48 = (f32[264,128]{1,0:T(8,128)S(1)}, f32[264,128]{1,0:T(8,128)S(1)}, f32[264,128]{1,0:T(8,128)S(1)}, f32[264,128]{1,0:T(8,128)S(1)}) custom-call(bf16[2,16,128,128]{3,2,1,0:T(8,128)(2,1)S(1)} %get-tuple-element.16.tiles_ref, s32[4,128]{1,0:T(4,128)S(1)} %get-tuple-element.17.right_ids_ref, bf16[2080,128]{1,0:T(8,128)(2,1)S(1)} %get-tuple-element.14.refs_0_, ...), custom_call_target="tpu_custom_call" | custom-call | flops 536870912 | bytes 10485760 | tf_op jit(solution)/shard_map/pallas_call | solution.py:203
  45.4 3.0 %collective-permute-start.23 = (f32[264,128]{1,0:T(8,128)S(1)}, f32[264,128]{1,0:T(8,128)S(1)}, u32[]{:S(2)}, u32[]{:S(2)}) collective-permute-start(f32[264,128]{1,0:T(8,128)S(1)} %get-tuple-element.20), channel_id=1, source_target_pairs={{0,2},{1,3},{2,0},{3,1},{4,6},{5,7},{6,4},{7,5},{8,10},{9,11},{10,... | collective-permute-start | bytes 405512 | tf_op jit(solution)/shard_map/ppermute | solution.py:220
  48.4 0.4 collective-permute-start.24
  48.8 2.3 %collective-permute-start.25 = (f32[264,128]{1,0:T(8,128)S(1)}, f32[264,128]{1,0:T(8,128)S(1)}, u32[]{:S(2)}, u32[]{:S(2)}) collective-permute-start(f32[264,128]{1,0:T(8,128)S(1)} %get-tuple-element.22), channel_id=1, source_target_pairs={{0,3},{1,0},{2,1},{3,2},{4,7},{5,4},{6,5},{7,6},{8,11},{9,8},{10,9... | collective-permute-start | bytes 405512 | tf_op jit(solution)/shard_map/ppermute | solution.py:220
  51.1 0.7 %collective-permute-done.23.refs_1_ = f32[264,128]{1,0:T(8,128)S(1)} collective-permute-done((f32[264,128]{1,0:T(8,128)S(1)}, f32[264,128]{1,0:T(8,128)S(1)}, u32[]{:S(2)}, u32[]{:S(2)}) %collective-permute-start.23) | collective-permute-done | bytes 135200 | tf_op jit(solution)/shard_map/ppermute | solution.py:220
  51.8 3.4 %collective-permute-done.24.refs_2_ = f32[264,128]{1,0:T(8,128)S(1)} collective-permute-done((f32[264,128]{1,0:T(8,128)S(1)}, f32[264,128]{1,0:T(8,128)S(1)}, u32[]{:S(2)}, u32[]{:S(2)}) %collective-permute-start.24) | collective-permute-done | bytes 135200 | tf_op jit(solution)/shard_map/ppermute | solution.py:220
  55.2 0.8 %shard_map.49 = bf16[2,4,1,128,128]{4,3,2,1,0:T(8,128)(2,1)} custom-call(s32[2,4,128]{2,1,0:T(4,128)S(1)} %copy-done, f32[264,128]{1,0:T(8,128)S(1)} %get-tuple-element.19.refs_0_, f32[264,128]{1,0:T(8,128)S(1)} %collective-permute-done.23.refs_1_, f32[264,128]{1,0:T(8,128)S(1)} %collective-permute-done.24.refs_2_, ...), custom_call_target="tpu_custom_call" | custom-call | tf_op jit(solution)/shard_map/pallas_call | solution.py:221
  (26 shorter events, 0.2 us)
Async XLA Ops:
  1.9 8.7 %collective-permute-start.3 = (bf16[1040,128]{1,0:T(8,128)(2,1)S(1)}, bf16[1040,128]{1,0:T(8,128)(2,1)S(1)}, u32[]{:S(2)}, u32[]{:S(2)}) collective-permute-start(bf16[1040,128]{1,0:T(8,128)(2,1)S(1)} %pad_maximum_fusion.refs_0_.refs_2_), channel_id=1, source_target_pairs={{0,32},{4,12},{8,40},{12,20},{16,48},{20,28},{24,56},{28,4},{32,64... | collective-permute-start | bytes 798728 | tf_op jit(solution)/shard_map/ppermute | solution.py:42
  4.5 8.4 %collective-permute-start.4 = (bf16[1040,128]{1,0:T(8,128)(2,1)S(1)}, bf16[1040,128]{1,0:T(8,128)(2,1)S(1)}, u32[]{:S(2)}, u32[]{:S(2)}) collective-permute-start(bf16[1040,128]{1,0:T(8,128)(2,1)S(1)} %pad_maximum_fusion.refs_0_.refs_2_), channel_id=1, source_target_pairs={{0,96},{4,28},{8,104},{12,4},{16,112},{20,12},{24,120},{28,20},{32... | collective-permute-start | bytes 798728 | tf_op jit(solution)/shard_map/ppermute | solution.py:42
  6.7 9.0 %collective-permute-start = (bf16[1040,128]{1,0:T(8,128)(2,1)S(1)}, bf16[1040,128]{1,0:T(8,128)(2,1)S(1)}, u32[]{:S(2)}, u32[]{:S(2)}) collective-permute-start(bf16[1040,128]{1,0:T(8,128)(2,1)S(1)} %pad_maximum_fusion.refs_0_.refs_2_), channel_id=1, source_target_pairs={{0,64},{4,20},{8,72},{12,28},{16,80},{20,4},{24,88},{28,12},{32,96... | collective-permute-start | bytes 798728 | tf_op jit(solution)/shard_map/ppermute | solution.py:42
  7.9 8.6 %collective-permute-start.1 = (bf16[1040,128]{1,0:T(8,128)(2,1)S(1)}, bf16[1040,128]{1,0:T(8,128)(2,1)S(1)}, u32[]{:S(2)}, u32[]{:S(2)}) collective-permute-start(bf16[1040,128]{1,0:T(8,128)(2,1)S(1)} %pad_maximum_fusion.refs_0_.refs_2_), channel_id=1, source_target_pairs={{0,1},{1,2},{2,3},{3,0},{4,5},{5,6},{6,7},{7,4},{8,9},{9,10},{10,1... | collective-permute-start | bytes 798728 | tf_op jit(solution)/shard_map/ppermute | solution.py:156
  9.2 7.3 %collective-permute-start.2 = (bf16[1040,128]{1,0:T(8,128)(2,1)S(1)}, bf16[1040,128]{1,0:T(8,128)(2,1)S(1)}, u32[]{:S(2)}, u32[]{:S(2)}) collective-permute-start(bf16[1040,128]{1,0:T(8,128)(2,1)S(1)} %pad_maximum_fusion.refs_0_.refs_2_), channel_id=1, source_target_pairs={{0,3},{1,0},{2,1},{3,2},{4,7},{5,4},{6,5},{7,6},{8,11},{9,8},{10,9... | collective-permute-start | bytes 798728 | tf_op jit(solution)/shard_map/ppermute | solution.py:156
  12.9 9.7 %collective-permute-start.6 = (bf16[2080,128]{1,0:T(8,128)(2,1)S(1)}, bf16[2080,128]{1,0:T(8,128)(2,1)S(1)}, u32[]{:S(2)}, u32[]{:S(2)}) collective-permute-start(bf16[2080,128]{1,0:T(8,128)(2,1)S(1)} %constant_dynamic-update-slice_fusion.refs_1_), channel_id=1, source_target_pairs={{0,8},{4,36},{8,16},{12,44},{16,24},{20,52},{24,0},{28,60},{32,40}... | collective-permute-start | bytes 1597448 | tf_op jit(solution)/shard_map/ppermute | solution.py:42
  14.2 8.6 %collective-permute-start.8 = (bf16[2080,128]{1,0:T(8,128)(2,1)S(1)}, bf16[2080,128]{1,0:T(8,128)(2,1)S(1)}, u32[]{:S(2)}, u32[]{:S(2)}) collective-permute-start(bf16[2080,128]{1,0:T(8,128)(2,1)S(1)} %constant_dynamic-update-slice_fusion.refs_1_), channel_id=1, source_target_pairs={{0,24},{4,100},{8,0},{12,108},{16,8},{20,116},{24,16},{28,124},{32... | collective-permute-start | bytes 1597448 | tf_op jit(solution)/shard_map/ppermute | solution.py:42
  16.6 11.8 %collective-permute-start.10 = (bf16[2080,128]{1,0:T(8,128)(2,1)S(1)}, bf16[2080,128]{1,0:T(8,128)(2,1)S(1)}, u32[]{:S(2)}, u32[]{:S(2)}) collective-permute-start(bf16[2080,128]{1,0:T(8,128)(2,1)S(1)} %get-tuple-element.14.refs_0_), channel_id=1, source_target_pairs={{0,8},{4,36},{8,16},{12,44},{16,24},{20,52},{24,0},{28,60},{32,40}... | collective-permute-start | bytes 1597448 | tf_op jit(solution)/shard_map/ppermute | solution.py:42
  18.8 9.7 %collective-permute-start.12 = (bf16[2080,128]{1,0:T(8,128)(2,1)S(1)}, bf16[2080,128]{1,0:T(8,128)(2,1)S(1)}, u32[]{:S(2)}, u32[]{:S(2)}) collective-permute-start(bf16[2080,128]{1,0:T(8,128)(2,1)S(1)} %get-tuple-element.14.refs_0_), channel_id=1, source_target_pairs={{0,24},{4,100},{8,0},{12,108},{16,8},{20,116},{24,16},{28,124},{32... | collective-permute-start | bytes 1597448 | tf_op jit(solution)/shard_map/ppermute | solution.py:42
  19.9 11.3 %collective-permute-start.5 = (bf16[1040,128]{1,0:T(8,128)(2,1)S(1)}, bf16[1040,128]{1,0:T(8,128)(2,1)S(1)}, u32[]{:S(2)}, u32[]{:S(2)}) collective-permute-start(bf16[1040,128]{1,0:T(8,128)(2,1)S(1)} %get-tuple-element.15), channel_id=1, source_target_pairs={{0,2},{1,3},{2,0},{3,1},{4,6},{5,7},{6,4},{7,5},{8,10},{9,11},{10,... | collective-permute-start | bytes 798728 | tf_op jit(solution)/shard_map/ppermute | solution.py:166
  22.6 11.7 %collective-permute-start.7 = (bf16[1040,128]{1,0:T(8,128)(2,1)S(1)}, bf16[1040,128]{1,0:T(8,128)(2,1)S(1)}, u32[]{:S(2)}, u32[]{:S(2)}) collective-permute-start(bf16[1040,128]{1,0:T(8,128)(2,1)S(1)} %slice.16), channel_id=1, source_target_pairs={{0,8},{4,36},{8,16},{12,44},{16,24},{20,52},{24,0},{28,60},{32,40}... | collective-permute-start | bytes 798728 | tf_op jit(solution)/shard_map/ppermute | solution.py:42
  22.8 11.6 %collective-permute-start.9 = (bf16[1040,128]{1,0:T(8,128)(2,1)S(1)}, bf16[1040,128]{1,0:T(8,128)(2,1)S(1)}, u32[]{:S(2)}, u32[]{:S(2)}) collective-permute-start(bf16[1040,128]{1,0:T(8,128)(2,1)S(1)} %slice.17), channel_id=1, source_target_pairs={{0,24},{4,100},{8,0},{12,108},{16,8},{20,116},{24,16},{28,124},{32... | collective-permute-start | bytes 798728 | tf_op jit(solution)/shard_map/ppermute | solution.py:42
  28.4 6.8 %collective-permute-start.11 = (bf16[1040,128]{1,0:T(8,128)(2,1)S(1)}, bf16[1040,128]{1,0:T(8,128)(2,1)S(1)}, u32[]{:S(2)}, u32[]{:S(2)}) collective-permute-start(bf16[1040,128]{1,0:T(8,128)(2,1)S(1)} %slice.18), channel_id=1, source_target_pairs={{0,8},{4,36},{8,16},{12,44},{16,24},{20,52},{24,0},{28,60},{32,40}... | collective-permute-start | bytes 798728 | tf_op jit(solution)/shard_map/ppermute | solution.py:42
  28.5 9.9 %collective-permute-start.13 = (bf16[1040,128]{1,0:T(8,128)(2,1)S(1)}, bf16[1040,128]{1,0:T(8,128)(2,1)S(1)}, u32[]{:S(2)}, u32[]{:S(2)}) collective-permute-start(bf16[1040,128]{1,0:T(8,128)(2,1)S(1)} %slice.19), channel_id=1, source_target_pairs={{0,24},{4,100},{8,0},{12,108},{16,8},{20,116},{24,16},{28,124},{32... | collective-permute-start | bytes 798728 | tf_op jit(solution)/shard_map/ppermute | solution.py:42
  31.3 11.7 %collective-permute-start.14 = (bf16[4160,128]{1,0:T(8,128)(2,1)S(1)}, bf16[4160,128]{1,0:T(8,128)(2,1)S(1)}, u32[]{:S(2)}, u32[]{:S(2)}) collective-permute-start(bf16[4160,128]{1,0:T(8,128)(2,1)S(1)} %get-tuple-element.18), channel_id=1, source_target_pairs={{0,4},{4,0},{1,5},{5,1},{2,6},{6,2},{3,7},{7,3},{8,12},{12,8},{9,1... | collective-permute-start | bytes 3194888 | tf_op jit(solution)/shard_map/ppermute | solution.py:46
  34.3 6.0 %collective-permute-start.17 = (bf16[2080,128]{1,0:T(8,128)(2,1)S(1)}, bf16[2080,128]{1,0:T(8,128)(2,1)S(1)}, u32[]{:S(2)}, u32[]{:S(2)}) collective-permute-start(bf16[2080,128]{1,0:T(8,128)(2,1)S(1)} %collective-permute-done.6.refs_6_), channel_id=1, source_target_pairs={{0,4},{4,0},{1,5},{5,1},{2,6},{6,2},{3,7},{7,3},{8,12},{12,8},{9,1... | collective-permute-start | bytes 1597448 | tf_op jit(solution)/shard_map/ppermute | solution.py:46
  34.4 6.0 %collective-permute-start.18 = (bf16[2080,128]{1,0:T(8,128)(2,1)S(1)}, bf16[2080,128]{1,0:T(8,128)(2,1)S(1)}, u32[]{:S(2)}, u32[]{:S(2)}) collective-permute-start(bf16[2080,128]{1,0:T(8,128)(2,1)S(1)} %collective-permute-done.8.refs_7_), channel_id=1, source_target_pairs={{0,4},{4,0},{1,5},{5,1},{2,6},{6,2},{3,7},{7,3},{8,12},{12,8},{9,1... | collective-permute-start | bytes 1597448 | tf_op jit(solution)/shard_map/ppermute | solution.py:46
  35.2 4.4 %collective-permute-start.19 = (bf16[1040,128]{1,0:T(8,128)(2,1)S(1)}, bf16[1040,128]{1,0:T(8,128)(2,1)S(1)}, u32[]{:S(2)}, u32[]{:S(2)}) collective-permute-start(bf16[1040,128]{1,0:T(8,128)(2,1)S(1)} %collective-permute-done.7.refs_2_), channel_id=1, source_target_pairs={{0,4},{4,0},{1,5},{5,1},{2,6},{6,2},{3,7},{7,3},{8,12},{12,8},{9,1... | collective-permute-start | bytes 798728 | tf_op jit(solution)/shard_map/ppermute | solution.py:46
  38.4 1.5 %collective-permute-start.20 = (bf16[1040,128]{1,0:T(8,128)(2,1)S(1)}, bf16[1040,128]{1,0:T(8,128)(2,1)S(1)}, u32[]{:S(2)}, u32[]{:S(2)}) collective-permute-start(bf16[1040,128]{1,0:T(8,128)(2,1)S(1)} %collective-permute-done.9.refs_3_), channel_id=1, source_target_pairs={{0,4},{4,0},{1,5},{5,1},{2,6},{6,2},{3,7},{7,3},{8,12},{12,8},{9,1... | collective-permute-start | bytes 798728 | tf_op jit(solution)/shard_map/ppermute | solution.py:46
  39.5 3.4 %collective-permute-start.15 = (bf16[2080,128]{1,0:T(8,128)(2,1)S(1)}, bf16[2080,128]{1,0:T(8,128)(2,1)S(1)}, u32[]{:S(2)}, u32[]{:S(2)}) collective-permute-start(bf16[2080,128]{1,0:T(8,128)(2,1)S(1)} %collective-permute-done.10.refs_8_), channel_id=1, source_target_pairs={{0,4},{4,0},{1,5},{5,1},{2,6},{6,2},{3,7},{7,3},{8,12},{12,8},{9,1... | collective-permute-start | bytes 1597448 | tf_op jit(solution)/shard_map/ppermute | solution.py:46
  39.9 3.1 %collective-permute-start.16 = (bf16[2080,128]{1,0:T(8,128)(2,1)S(1)}, bf16[2080,128]{1,0:T(8,128)(2,1)S(1)}, u32[]{:S(2)}, u32[]{:S(2)}) collective-permute-start(bf16[2080,128]{1,0:T(8,128)(2,1)S(1)} %collective-permute-done.12.refs_9_), channel_id=1, source_target_pairs={{0,4},{4,0},{1,5},{5,1},{2,6},{6,2},{3,7},{7,3},{8,12},{12,8},{9,1... | collective-permute-start | bytes 1597448 | tf_op jit(solution)/shard_map/ppermute | solution.py:46
  40.3 2.3 %collective-permute-start.21 = (bf16[1040,128]{1,0:T(8,128)(2,1)S(1)}, bf16[1040,128]{1,0:T(8,128)(2,1)S(1)}, u32[]{:S(2)}, u32[]{:S(2)}) collective-permute-start(bf16[1040,128]{1,0:T(8,128)(2,1)S(1)} %collective-permute-done.11.refs_4_), channel_id=1, source_target_pairs={{0,4},{4,0},{1,5},{5,1},{2,6},{6,2},{3,7},{7,3},{8,12},{12,8},{9,1... | collective-permute-start | bytes 798728 | tf_op jit(solution)/shard_map/ppermute | solution.py:46
  40.4 2.5 %collective-permute-start.22 = (bf16[1040,128]{1,0:T(8,128)(2,1)S(1)}, bf16[1040,128]{1,0:T(8,128)(2,1)S(1)}, u32[]{:S(2)}, u32[]{:S(2)}) collective-permute-start(bf16[1040,128]{1,0:T(8,128)(2,1)S(1)} %collective-permute-done.13.refs_5_), channel_id=1, source_target_pairs={{0,4},{4,0},{1,5},{5,1},{2,6},{6,2},{3,7},{7,3},{8,12},{12,8},{9,1... | collective-permute-start | bytes 798728 | tf_op jit(solution)/shard_map/ppermute | solution.py:46
  43.0 12.2 %copy-start = (s32[2,4,128]{2,1,0:T(4,128)S(1)}, s32[2,4,128]{2,1,0:T(4,128)}, u32[]{:S(2)}) copy-start(s32[2,4,128]{2,1,0:T(4,128)} %mask_ref.1) | copy-start | bytes 12292
  45.4 6.4 %collective-permute-start.23 = (f32[264,128]{1,0:T(8,128)S(1)}, f32[264,128]{1,0:T(8,128)S(1)}, u32[]{:S(2)}, u32[]{:S(2)}) collective-permute-start(f32[264,128]{1,0:T(8,128)S(1)} %get-tuple-element.20), channel_id=1, source_target_pairs={{0,2},{1,3},{2,0},{3,1},{4,6},{5,7},{6,4},{7,5},{8,10},{9,11},{10,... | collective-permute-start | bytes 405512 | tf_op jit(solution)/shard_map/ppermute | solution.py:220
  48.4 6.8 %collective-permute-start.24 = (f32[264,128]{1,0:T(8,128)S(1)}, f32[264,128]{1,0:T(8,128)S(1)}, u32[]{:S(2)}, u32[]{:S(2)}) collective-permute-start(f32[264,128]{1,0:T(8,128)S(1)} %get-tuple-element.21), channel_id=1, source_target_pairs={{0,1},{1,2},{2,3},{3,0},{4,5},{5,6},{6,7},{7,4},{8,9},{9,10},{10,1... | collective-permute-start | bytes 405512 | tf_op jit(solution)/shard_map/ppermute | solution.py:220
  48.8 6.4 %collective-permute-start.25 = (f32[264,128]{1,0:T(8,128)S(1)}, f32[264,128]{1,0:T(8,128)S(1)}, u32[]{:S(2)}, u32[]{:S(2)}) collective-permute-start(f32[264,128]{1,0:T(8,128)S(1)} %get-tuple-element.22), channel_id=1, source_target_pairs={{0,3},{1,0},{2,1},{3,2},{4,7},{5,4},{6,5},{7,6},{8,11},{9,8},{10,9... | collective-permute-start | bytes 405512 | tf_op jit(solution)/shard_map/ppermute | solution.py:220

commit v8 on v7

--- a/solution.py
+++ b/solution.py
@@ -128,7 +128,7 @@
             value = acc[p, r]
             return total + jnp.sum((value * value).reshape(TILE // 8, 8, TILE), axis=0)
 
-        total = lax.fori_loop(0, BLOCKS, add, jnp.zeros((8, TILE), jnp.float32), unroll=4)
+        total = lax.fori_loop(0, BLOCKS, add, jnp.zeros((8, TILE), jnp.float32), unroll=BLOCKS)
         total = jnp.sum(total, axis=0, keepdims=True)
         for s, shift in enumerate(chunk_shifts):
             slot = (band + shift) & (BANDS - 1)

time: 56.6 us -> 56.5 us (level)
  no operation moved by 1% of the time
where the time goes in v8:
time: 56.5 us; the launch traced here: 55.9 us
  starting transfers between devices  36.5 us (65%)
  waiting for transfers between devices  13.9 us (25%)
  Pallas kernels  3.31 us (6%)
  other arithmetic  1.87 us (3%)
    ppermute x11, starting transfers between devices, along(): return lax.ppermute(value, CELL, cells(steps[axis], steps[1 - axis]))  17.6 us
    ppermute x9, starting transfers between devices, swap(): return lax.ppermute(value, 'core', [(0, 1), (1, 0)])  7.93 us
    ppermute x3, starting transfers between devices, per_device(): lax.ppermute(chunks[s], 'layer', ring(chunk_shifts[s]))  5.66 us
    ppermute x11, waiting for transfers between devices, along(): return lax.ppermute(value, CELL, cells(steps[axis], steps[1 - axis]))  5.59 us
    ppermute x3, waiting for transfers between devices, per_device(): lax.ppermute(chunks[s], 'layer', ring(chunk_shifts[s]))  4.1 us
    ppermute x9, waiting for transfers between devices, swap(): return lax.ppermute(value, 'core', [(0, 1), (1, 0)])  3.35 us
    ppermute x2, starting transfers between devices, per_device(): rights = [lax.ppermute(unit, 'layer', ring(s)) for s in (1, 3)]  2.74 us
    ppermute x1, starting transfers between devices, per_device(): rights = [unit, *rights, lax.ppermute(unit_again, 'layer', ring(2))]  2.62 us
  transfers between devices with their start and end apart: 26, of which 10 were waited for; matrix products, arithmetic and copies ran while one was open for 0% of the time, Pallas kernels for 0%

profile of v8, /device:TPU:1, one launch (start us, length us, event | category | flops | bytes accessed | tf_op | source)
XLA Modules:
  0.0 55.9 jit_solution(13932161686037414873)
XLA Ops:
  0.1 0.8 %add_reduce_fusion = s32[16,128]{1,0:T(8,128)S(1)} fusion(s32[2,4]{1,0:T(2,128)} %bitcast.4, s32[2,4]{1,0:T(2,128)} %bitcast.5, s32[2]{0:T(128)S(1)} %iota_multiply_fusion, s32[16,128]{1,0:T(8,128)S(1)} %broadcast_select_fusion), kind=kLoop, calls=%fused_computation.1 | loop fusion | flops 129024 | bytes 16456 | tf_op jit(solution)/shard_map/reduce_sum | solution.py:63
  0.9 0.1 select_convert_fusion
  1.0 1.0 %pad_maximum_fusion.refs_0_.refs_2_ = bf16[1040,128]{1,0:T(8,128)(2,1)S(1)} fusion(bf16[16,128]{1,0:T(8,128)(2,1)S(1)} %select_convert_fusion, bf16[1024,128]{1,0:T(8,128)(2,1)} %bitcast.3), kind=kLoop, calls=%fused_computation | loop fusion | flops 532480 | bytes 532480 | tf_op jit(solution)/shard_map/concatenate | solution.py:155
  1.9 2.5 %collective-permute-start.3 = (bf16[1040,128]{1,0:T(8,128)(2,1)S(1)}, bf16[1040,128]{1,0:T(8,128)(2,1)S(1)}, u32[]{:S(2)}, u32[]{:S(2)}) collective-permute-start(bf16[1040,128]{1,0:T(8,128)(2,1)S(1)} %pad_maximum_fusion.refs_0_.refs_2_), channel_id=1, source_target_pairs={{0,32},{4,12},{8,40},{12,20},{16,48},{20,28},{24,56},{28,4},{32,64... | collective-permute-start | bytes 798728 | tf_op jit(solution)/shard_map/ppermute | solution.py:42
  4.5 2.2 %collective-permute-start.4 = (bf16[1040,128]{1,0:T(8,128)(2,1)S(1)}, bf16[1040,128]{1,0:T(8,128)(2,1)S(1)}, u32[]{:S(2)}, u32[]{:S(2)}) collective-permute-start(bf16[1040,128]{1,0:T(8,128)(2,1)S(1)} %pad_maximum_fusion.refs_0_.refs_2_), channel_id=1, source_target_pairs={{0,96},{4,28},{8,104},{12,4},{16,112},{20,12},{24,120},{28,20},{32... | collective-permute-start | bytes 798728 | tf_op jit(solution)/shard_map/ppermute | solution.py:42
  6.7 1.2 %collective-permute-start = (bf16[1040,128]{1,0:T(8,128)(2,1)S(1)}, bf16[1040,128]{1,0:T(8,128)(2,1)S(1)}, u32[]{:S(2)}, u32[]{:S(2)}) collective-permute-start(bf16[1040,128]{1,0:T(8,128)(2,1)S(1)} %pad_maximum_fusion.refs_0_.refs_2_), channel_id=1, source_target_pairs={{0,64},{4,20},{8,72},{12,28},{16,80},{20,4},{24,88},{28,12},{32,96... | collective-permute-start | bytes 798728 | tf_op jit(solution)/shard_map/ppermute | solution.py:42
  7.9 1.3 %collective-permute-start.1 = (bf16[1040,128]{1,0:T(8,128)(2,1)S(1)}, bf16[1040,128]{1,0:T(8,128)(2,1)S(1)}, u32[]{:S(2)}, u32[]{:S(2)}) collective-permute-start(bf16[1040,128]{1,0:T(8,128)(2,1)S(1)} %pad_maximum_fusion.refs_0_.refs_2_), channel_id=1, source_target_pairs={{0,1},{1,2},{2,3},{3,0},{4,5},{5,6},{6,7},{7,4},{8,9},{9,10},{10,1... | collective-permute-start | bytes 798728 | tf_op jit(solution)/shard_map/ppermute | solution.py:156
  9.2 1.4 %collective-permute-start.2 = (bf16[1040,128]{1,0:T(8,128)(2,1)S(1)}, bf16[1040,128]{1,0:T(8,128)(2,1)S(1)}, u32[]{:S(2)}, u32[]{:S(2)}) collective-permute-start(bf16[1040,128]{1,0:T(8,128)(2,1)S(1)} %pad_maximum_fusion.refs_0_.refs_2_), channel_id=1, source_target_pairs={{0,3},{1,0},{2,1},{3,2},{4,7},{5,4},{6,5},{7,6},{8,11},{9,8},{10,9... | collective-permute-start | bytes 798728 | tf_op jit(solution)/shard_map/ppermute | solution.py:156
  10.6 0.0 collective-permute-done.3
  10.7 2.2 %collective-permute-done.4 = bf16[1040,128]{1,0:T(8,128)(2,1)S(1)} collective-permute-done((bf16[1040,128]{1,0:T(8,128)(2,1)S(1)}, bf16[1040,128]{1,0:T(8,128)(2,1)S(1)}, u32[]{:S(2)}, u32[]{:S(2)}) %collective-permute-start.4) | collective-permute-done | bytes 266272 | tf_op jit(solution)/shard_map/ppermute | solution.py:42
  12.9 1.3 %collective-permute-start.6 = (bf16[2080,128]{1,0:T(8,128)(2,1)S(1)}, bf16[2080,128]{1,0:T(8,128)(2,1)S(1)}, u32[]{:S(2)}, u32[]{:S(2)}) collective-permute-start(bf16[2080,128]{1,0:T(8,128)(2,1)S(1)} %constant_dynamic-update-slice_fusion.refs_1_), channel_id=1, source_target_pairs={{0,8},{4,36},{8,16},{12,44},{16,24},{20,52},{24,0},{28,60},{32,40}... | collective-permute-start | bytes 1597448 | tf_op jit(solution)/shard_map/ppermute | solution.py:42
  14.2 1.5 %collective-permute-start.8 = (bf16[2080,128]{1,0:T(8,128)(2,1)S(1)}, bf16[2080,128]{1,0:T(8,128)(2,1)S(1)}, u32[]{:S(2)}, u32[]{:S(2)}) collective-permute-start(bf16[2080,128]{1,0:T(8,128)(2,1)S(1)} %constant_dynamic-update-slice_fusion.refs_1_), channel_id=1, source_target_pairs={{0,24},{4,100},{8,0},{12,108},{16,8},{20,116},{24,16},{28,124},{32... | collective-permute-start | bytes 1597448 | tf_op jit(solution)/shard_map/ppermute | solution.py:42
  15.7 0.8 %collective-permute-done.1.refs_2_.refs_3_ = bf16[1040,128]{1,0:T(8,128)(2,1)S(1)} collective-permute-done((bf16[1040,128]{1,0:T(8,128)(2,1)S(1)}, bf16[1040,128]{1,0:T(8,128)(2,1)S(1)}, u32[]{:S(2)}, u32[]{:S(2)}) %collective-permute-start.1) | collective-permute-done | bytes 266272 | tf_op jit(solution)/shard_map/ppermute | solution.py:156
  16.5 0.0 collective-permute-done.2.refs_3_.refs_4_
  16.5 0.1 shard_map.46
  16.6 2.2 %collective-permute-start.10 = (bf16[2080,128]{1,0:T(8,128)(2,1)S(1)}, bf16[2080,128]{1,0:T(8,128)(2,1)S(1)}, u32[]{:S(2)}, u32[]{:S(2)}) collective-permute-start(bf16[2080,128]{1,0:T(8,128)(2,1)S(1)} %get-tuple-element.14.refs_0_), channel_id=1, source_target_pairs={{0,8},{4,36},{8,16},{12,44},{16,24},{20,52},{24,0},{28,60},{32,40}... | collective-permute-start | bytes 1597448 | tf_op jit(solution)/shard_map/ppermute | solution.py:42
  18.8 1.1 %collective-permute-start.12 = (bf16[2080,128]{1,0:T(8,128)(2,1)S(1)}, bf16[2080,128]{1,0:T(8,128)(2,1)S(1)}, u32[]{:S(2)}, u32[]{:S(2)}) collective-permute-start(bf16[2080,128]{1,0:T(8,128)(2,1)S(1)} %get-tuple-element.14.refs_0_), channel_id=1, source_target_pairs={{0,24},{4,100},{8,0},{12,108},{16,8},{20,116},{24,16},{28,124},{32... | collective-permute-start | bytes 1597448 | tf_op jit(solution)/shard_map/ppermute | solution.py:42
  19.9 2.6 %collective-permute-start.5 = (bf16[1040,128]{1,0:T(8,128)(2,1)S(1)}, bf16[1040,128]{1,0:T(8,128)(2,1)S(1)}, u32[]{:S(2)}, u32[]{:S(2)}) collective-permute-start(bf16[1040,128]{1,0:T(8,128)(2,1)S(1)} %get-tuple-element.15), channel_id=1, source_target_pairs={{0,2},{1,3},{2,0},{3,1},{4,6},{5,7},{6,4},{7,5},{8,10},{9,11},{10,... | collective-permute-start | bytes 798728 | tf_op jit(solution)/shard_map/ppermute | solution.py:166
  22.5 0.1 collective-permute-done.6.refs_6_
  22.6 0.1 collective-permute-start.7
  22.8 0.0 collective-permute-done.8.refs_7_
  22.8 2.7 %collective-permute-start.9 = (bf16[1040,128]{1,0:T(8,128)(2,1)S(1)}, bf16[1040,128]{1,0:T(8,128)(2,1)S(1)}, u32[]{:S(2)}, u32[]{:S(2)}) collective-permute-start(bf16[1040,128]{1,0:T(8,128)(2,1)S(1)} %slice.17), channel_id=1, source_target_pairs={{0,24},{4,100},{8,0},{12,108},{16,8},{20,116},{24,16},{28,124},{32... | collective-permute-start | bytes 798728 | tf_op jit(solution)/shard_map/ppermute | solution.py:42
  25.5 2.8 %collective-permute-done.10.refs_8_ = bf16[2080,128]{1,0:T(8,128)(2,1)S(1)} collective-permute-done((bf16[2080,128]{1,0:T(8,128)(2,1)S(1)}, bf16[2080,128]{1,0:T(8,128)(2,1)S(1)}, u32[]{:S(2)}, u32[]{:S(2)}) %collective-permute-start.10) | collective-permute-done | bytes 532512 | tf_op jit(solution)/shard_map/ppermute | solution.py:42
  28.4 0.1 collective-permute-start.11
  28.5 2.7 %collective-permute-start.13 = (bf16[1040,128]{1,0:T(8,128)(2,1)S(1)}, bf16[1040,128]{1,0:T(8,128)(2,1)S(1)}, u32[]{:S(2)}, u32[]{:S(2)}) collective-permute-start(bf16[1040,128]{1,0:T(8,128)(2,1)S(1)} %slice.19), channel_id=1, source_target_pairs={{0,24},{4,100},{8,0},{12,108},{16,8},{20,116},{24,16},{28,124},{32... | collective-permute-start | bytes 798728 | tf_op jit(solution)/shard_map/ppermute | solution.py:42
  31.2 0.1 shard_map.47
  31.3 3.0 %collective-permute-start.14 = (bf16[4160,128]{1,0:T(8,128)(2,1)S(1)}, bf16[4160,128]{1,0:T(8,128)(2,1)S(1)}, u32[]{:S(2)}, u32[]{:S(2)}) collective-permute-start(bf16[4160,128]{1,0:T(8,128)(2,1)S(1)} %get-tuple-element.18), channel_id=1, source_target_pairs={{0,4},{4,0},{1,5},{5,1},{2,6},{6,2},{3,7},{7,3},{8,12},{12,8},{9,1... | collective-permute-start | bytes 3194888 | tf_op jit(solution)/shard_map/ppermute | solution.py:46
  34.3 0.1 collective-permute-start.17
  34.4 0.4 collective-permute-start.18
  34.8 0.4 collective-permute-done.11.refs_4_
  35.2 3.2 %collective-permute-start.19 = (bf16[1040,128]{1,0:T(8,128)(2,1)S(1)}, bf16[1040,128]{1,0:T(8,128)(2,1)S(1)}, u32[]{:S(2)}, u32[]{:S(2)}) collective-permute-start(bf16[1040,128]{1,0:T(8,128)(2,1)S(1)} %collective-permute-done.7.refs_2_), channel_id=1, source_target_pairs={{0,4},{4,0},{1,5},{5,1},{2,6},{6,2},{3,7},{7,3},{8,12},{12,8},{9,1... | collective-permute-start | bytes 798728 | tf_op jit(solution)/shard_map/ppermute | solution.py:46
  38.4 0.0 collective-permute-start.20
  38.4 1.2 %collective-permute-done.19.refs_15_ = bf16[1040,128]{1,0:T(8,128)(2,1)S(1)} collective-permute-done((bf16[1040,128]{1,0:T(8,128)(2,1)S(1)}, bf16[1040,128]{1,0:T(8,128)(2,1)S(1)}, u32[]{:S(2)}, u32[]{:S(2)}) %collective-permute-start.19) | collective-permute-done | bytes 266272 | tf_op jit(solution)/shard_map/ppermute | solution.py:46
  39.5 0.4 collective-permute-start.15
  39.9 0.0 collective-permute-done.20.refs_16_
  39.9 0.4 collective-permute-start.16
  40.3 0.1 collective-permute-start.21
  40.4 0.4 collective-permute-start.22
  40.8 1.8 %collective-permute-done.21.refs_17_ = bf16[1040,128]{1,0:T(8,128)(2,1)S(1)} collective-permute-done((bf16[1040,128]{1,0:T(8,128)(2,1)S(1)}, bf16[1040,128]{1,0:T(8,128)(2,1)S(1)}, u32[]{:S(2)}, u32[]{:S(2)}) %collective-permute-start.21) | collective-permute-done | bytes 266272 | tf_op jit(solution)/shard_map/ppermute | solution.py:46
  42.6 0.4 collective-permute-done.22.refs_18_
  43.0 0.0 copy-start
  43.0 2.3 %shard_map.48 = (f32[264,128]{1,0:T(8,128)S(1)}, f32[264,128]{1,0:T(8,128)S(1)}, f32[264,128]{1,0:T(8,128)S(1)}, f32[264,128]{1,0:T(8,128)S(1)}) custom-call(bf16[2,16,128,128]{3,2,1,0:T(8,128)(2,1)S(1)} %get-tuple-element.16.tiles_ref, s32[4,128]{1,0:T(4,128)S(1)} %get-tuple-element.17.right_ids_ref, bf16[2080,128]{1,0:T(8,128)(2,1)S(1)} %get-tuple-element.14.refs_0_, ...), custom_call_target="tpu_custom_call" | custom-call | flops 536870912 | bytes 10485760 | tf_op jit(solution)/shard_map/pallas_call | solution.py:203
  45.4 3.0 %collective-permute-start.23 = (f32[264,128]{1,0:T(8,128)S(1)}, f32[264,128]{1,0:T(8,128)S(1)}, u32[]{:S(2)}, u32[]{:S(2)}) collective-permute-start(f32[264,128]{1,0:T(8,128)S(1)} %get-tuple-element.20), channel_id=1, source_target_pairs={{0,2},{1,3},{2,0},{3,1},{4,6},{5,7},{6,4},{7,5},{8,10},{9,11},{10,... | collective-permute-start | bytes 405512 | tf_op jit(solution)/shard_map/ppermute | solution.py:220
  48.3 0.4 collective-permute-start.24
  48.8 2.3 %collective-permute-start.25 = (f32[264,128]{1,0:T(8,128)S(1)}, f32[264,128]{1,0:T(8,128)S(1)}, u32[]{:S(2)}, u32[]{:S(2)}) collective-permute-start(f32[264,128]{1,0:T(8,128)S(1)} %get-tuple-element.22), channel_id=1, source_target_pairs={{0,3},{1,0},{2,1},{3,2},{4,7},{5,4},{6,5},{7,6},{8,11},{9,8},{10,9... | collective-permute-start | bytes 405512 | tf_op jit(solution)/shard_map/ppermute | solution.py:220
  51.0 0.7 %collective-permute-done.23.refs_1_ = f32[264,128]{1,0:T(8,128)S(1)} collective-permute-done((f32[264,128]{1,0:T(8,128)S(1)}, f32[264,128]{1,0:T(8,128)S(1)}, u32[]{:S(2)}, u32[]{:S(2)}) %collective-permute-start.23) | collective-permute-done | bytes 135200 | tf_op jit(solution)/shard_map/ppermute | solution.py:220
  51.8 3.4 %collective-permute-done.24.refs_2_ = f32[264,128]{1,0:T(8,128)S(1)} collective-permute-done((f32[264,128]{1,0:T(8,128)S(1)}, f32[264,128]{1,0:T(8,128)S(1)}, u32[]{:S(2)}, u32[]{:S(2)}) %collective-permute-start.24) | collective-permute-done | bytes 135200 | tf_op jit(solution)/shard_map/ppermute | solution.py:220
  55.1 0.8 %shard_map.49 = bf16[2,4,1,128,128]{4,3,2,1,0:T(8,128)(2,1)} custom-call(s32[2,4,128]{2,1,0:T(4,128)S(1)} %copy-done, f32[264,128]{1,0:T(8,128)S(1)} %get-tuple-element.19.refs_0_, f32[264,128]{1,0:T(8,128)S(1)} %collective-permute-done.23.refs_1_, f32[264,128]{1,0:T(8,128)S(1)} %collective-permute-done.24.refs_2_, ...), custom_call_target="tpu_custom_call" | custom-call | tf_op jit(solution)/shard_map/pallas_call | solution.py:221
  (26 shorter events, 0.2 us)
Async XLA Ops:
  1.9 8.7 %collective-permute-start.3 = (bf16[1040,128]{1,0:T(8,128)(2,1)S(1)}, bf16[1040,128]{1,0:T(8,128)(2,1)S(1)}, u32[]{:S(2)}, u32[]{:S(2)}) collective-permute-start(bf16[1040,128]{1,0:T(8,128)(2,1)S(1)} %pad_maximum_fusion.refs_0_.refs_2_), channel_id=1, source_target_pairs={{0,32},{4,12},{8,40},{12,20},{16,48},{20,28},{24,56},{28,4},{32,64... | collective-permute-start | bytes 798728 | tf_op jit(solution)/shard_map/ppermute | solution.py:42
  4.5 8.4 %collective-permute-start.4 = (bf16[1040,128]{1,0:T(8,128)(2,1)S(1)}, bf16[1040,128]{1,0:T(8,128)(2,1)S(1)}, u32[]{:S(2)}, u32[]{:S(2)}) collective-permute-start(bf16[1040,128]{1,0:T(8,128)(2,1)S(1)} %pad_maximum_fusion.refs_0_.refs_2_), channel_id=1, source_target_pairs={{0,96},{4,28},{8,104},{12,4},{16,112},{20,12},{24,120},{28,20},{32... | collective-permute-start | bytes 798728 | tf_op jit(solution)/shard_map/ppermute | solution.py:42
  6.7 9.0 %collective-permute-start = (bf16[1040,128]{1,0:T(8,128)(2,1)S(1)}, bf16[1040,128]{1,0:T(8,128)(2,1)S(1)}, u32[]{:S(2)}, u32[]{:S(2)}) collective-permute-start(bf16[1040,128]{1,0:T(8,128)(2,1)S(1)} %pad_maximum_fusion.refs_0_.refs_2_), channel_id=1, source_target_pairs={{0,64},{4,20},{8,72},{12,28},{16,80},{20,4},{24,88},{28,12},{32,96... | collective-permute-start | bytes 798728 | tf_op jit(solution)/shard_map/ppermute | solution.py:42
  7.9 8.6 %collective-permute-start.1 = (bf16[1040,128]{1,0:T(8,128)(2,1)S(1)}, bf16[1040,128]{1,0:T(8,128)(2,1)S(1)}, u32[]{:S(2)}, u32[]{:S(2)}) collective-permute-start(bf16[1040,128]{1,0:T(8,128)(2,1)S(1)} %pad_maximum_fusion.refs_0_.refs_2_), channel_id=1, source_target_pairs={{0,1},{1,2},{2,3},{3,0},{4,5},{5,6},{6,7},{7,4},{8,9},{9,10},{10,1... | collective-permute-start | bytes 798728 | tf_op jit(solution)/shard_map/ppermute | solution.py:156
  9.2 7.3 %collective-permute-start.2 = (bf16[1040,128]{1,0:T(8,128)(2,1)S(1)}, bf16[1040,128]{1,0:T(8,128)(2,1)S(1)}, u32[]{:S(2)}, u32[]{:S(2)}) collective-permute-start(bf16[1040,128]{1,0:T(8,128)(2,1)S(1)} %pad_maximum_fusion.refs_0_.refs_2_), channel_id=1, source_target_pairs={{0,3},{1,0},{2,1},{3,2},{4,7},{5,4},{6,5},{7,6},{8,11},{9,8},{10,9... | collective-permute-start | bytes 798728 | tf_op jit(solution)/shard_map/ppermute | solution.py:156
  12.9 9.7 %collective-permute-start.6 = (bf16[2080,128]{1,0:T(8,128)(2,1)S(1)}, bf16[2080,128]{1,0:T(8,128)(2,1)S(1)}, u32[]{:S(2)}, u32[]{:S(2)}) collective-permute-start(bf16[2080,128]{1,0:T(8,128)(2,1)S(1)} %constant_dynamic-update-slice_fusion.refs_1_), channel_id=1, source_target_pairs={{0,8},{4,36},{8,16},{12,44},{16,24},{20,52},{24,0},{28,60},{32,40}... | collective-permute-start | bytes 1597448 | tf_op jit(solution)/shard_map/ppermute | solution.py:42
  14.2 8.6 %collective-permute-start.8 = (bf16[2080,128]{1,0:T(8,128)(2,1)S(1)}, bf16[2080,128]{1,0:T(8,128)(2,1)S(1)}, u32[]{:S(2)}, u32[]{:S(2)}) collective-permute-start(bf16[2080,128]{1,0:T(8,128)(2,1)S(1)} %constant_dynamic-update-slice_fusion.refs_1_), channel_id=1, source_target_pairs={{0,24},{4,100},{8,0},{12,108},{16,8},{20,116},{24,16},{28,124},{32... | collective-permute-start | bytes 1597448 | tf_op jit(solution)/shard_map/ppermute | solution.py:42
  16.6 11.8 %collective-permute-start.10 = (bf16[2080,128]{1,0:T(8,128)(2,1)S(1)}, bf16[2080,128]{1,0:T(8,128)(2,1)S(1)}, u32[]{:S(2)}, u32[]{:S(2)}) collective-permute-start(bf16[2080,128]{1,0:T(8,128)(2,1)S(1)} %get-tuple-element.14.refs_0_), channel_id=1, source_target_pairs={{0,8},{4,36},{8,16},{12,44},{16,24},{20,52},{24,0},{28,60},{32,40}... | collective-permute-start | bytes 1597448 | tf_op jit(solution)/shard_map/ppermute | solution.py:42
  18.8 9.7 %collective-permute-start.12 = (bf16[2080,128]{1,0:T(8,128)(2,1)S(1)}, bf16[2080,128]{1,0:T(8,128)(2,1)S(1)}, u32[]{:S(2)}, u32[]{:S(2)}) collective-permute-start(bf16[2080,128]{1,0:T(8,128)(2,1)S(1)} %get-tuple-element.14.refs_0_), channel_id=1, source_target_pairs={{0,24},{4,100},{8,0},{12,108},{16,8},{20,116},{24,16},{28,124},{32... | collective-permute-start | bytes 1597448 | tf_op jit(solution)/shard_map/ppermute | solution.py:42
  19.9 11.3 %collective-permute-start.5 = (bf16[1040,128]{1,0:T(8,128)(2,1)S(1)}, bf16[1040,128]{1,0:T(8,128)(2,1)S(1)}, u32[]{:S(2)}, u32[]{:S(2)}) collective-permute-start(bf16[1040,128]{1,0:T(8,128)(2,1)S(1)} %get-tuple-element.15), channel_id=1, source_target_pairs={{0,2},{1,3},{2,0},{3,1},{4,6},{5,7},{6,4},{7,5},{8,10},{9,11},{10,... | collective-permute-start | bytes 798728 | tf_op jit(solution)/shard_map/ppermute | solution.py:166
  22.6 11.7 %collective-permute-start.7 = (bf16[1040,128]{1,0:T(8,128)(2,1)S(1)}, bf16[1040,128]{1,0:T(8,128)(2,1)S(1)}, u32[]{:S(2)}, u32[]{:S(2)}) collective-permute-start(bf16[1040,128]{1,0:T(8,128)(2,1)S(1)} %slice.16), channel_id=1, source_target_pairs={{0,8},{4,36},{8,16},{12,44},{16,24},{20,52},{24,0},{28,60},{32,40}... | collective-permute-start | bytes 798728 | tf_op jit(solution)/shard_map/ppermute | solution.py:42
  22.8 11.6 %collective-permute-start.9 = (bf16[1040,128]{1,0:T(8,128)(2,1)S(1)}, bf16[1040,128]{1,0:T(8,128)(2,1)S(1)}, u32[]{:S(2)}, u32[]{:S(2)}) collective-permute-start(bf16[1040,128]{1,0:T(8,128)(2,1)S(1)} %slice.17), channel_id=1, source_target_pairs={{0,24},{4,100},{8,0},{12,108},{16,8},{20,116},{24,16},{28,124},{32... | collective-permute-start | bytes 798728 | tf_op jit(solution)/shard_map/ppermute | solution.py:42
  28.4 6.8 %collective-permute-start.11 = (bf16[1040,128]{1,0:T(8,128)(2,1)S(1)}, bf16[1040,128]{1,0:T(8,128)(2,1)S(1)}, u32[]{:S(2)}, u32[]{:S(2)}) collective-permute-start(bf16[1040,128]{1,0:T(8,128)(2,1)S(1)} %slice.18), channel_id=1, source_target_pairs={{0,8},{4,36},{8,16},{12,44},{16,24},{20,52},{24,0},{28,60},{32,40}... | collective-permute-start | bytes 798728 | tf_op jit(solution)/shard_map/ppermute | solution.py:42
  28.5 9.9 %collective-permute-start.13 = (bf16[1040,128]{1,0:T(8,128)(2,1)S(1)}, bf16[1040,128]{1,0:T(8,128)(2,1)S(1)}, u32[]{:S(2)}, u32[]{:S(2)}) collective-permute-start(bf16[1040,128]{1,0:T(8,128)(2,1)S(1)} %slice.19), channel_id=1, source_target_pairs={{0,24},{4,100},{8,0},{12,108},{16,8},{20,116},{24,16},{28,124},{32... | collective-permute-start | bytes 798728 | tf_op jit(solution)/shard_map/ppermute | solution.py:42
  31.3 11.7 %collective-permute-start.14 = (bf16[4160,128]{1,0:T(8,128)(2,1)S(1)}, bf16[4160,128]{1,0:T(8,128)(2,1)S(1)}, u32[]{:S(2)}, u32[]{:S(2)}) collective-permute-start(bf16[4160,128]{1,0:T(8,128)(2,1)S(1)} %get-tuple-element.18), channel_id=1, source_target_pairs={{0,4},{4,0},{1,5},{5,1},{2,6},{6,2},{3,7},{7,3},{8,12},{12,8},{9,1... | collective-permute-start | bytes 3194888 | tf_op jit(solution)/shard_map/ppermute | solution.py:46
  34.3 6.0 %collective-permute-start.17 = (bf16[2080,128]{1,0:T(8,128)(2,1)S(1)}, bf16[2080,128]{1,0:T(8,128)(2,1)S(1)}, u32[]{:S(2)}, u32[]{:S(2)}) collective-permute-start(bf16[2080,128]{1,0:T(8,128)(2,1)S(1)} %collective-permute-done.6.refs_6_), channel_id=1, source_target_pairs={{0,4},{4,0},{1,5},{5,1},{2,6},{6,2},{3,7},{7,3},{8,12},{12,8},{9,1... | collective-permute-start | bytes 1597448 | tf_op jit(solution)/shard_map/ppermute | solution.py:46
  34.4 6.0 %collective-permute-start.18 = (bf16[2080,128]{1,0:T(8,128)(2,1)S(1)}, bf16[2080,128]{1,0:T(8,128)(2,1)S(1)}, u32[]{:S(2)}, u32[]{:S(2)}) collective-permute-start(bf16[2080,128]{1,0:T(8,128)(2,1)S(1)} %collective-permute-done.8.refs_7_), channel_id=1, source_target_pairs={{0,4},{4,0},{1,5},{5,1},{2,6},{6,2},{3,7},{7,3},{8,12},{12,8},{9,1... | collective-permute-start | bytes 1597448 | tf_op jit(solution)/shard_map/ppermute | solution.py:46
  35.2 4.4 %collective-permute-start.19 = (bf16[1040,128]{1,0:T(8,128)(2,1)S(1)}, bf16[1040,128]{1,0:T(8,128)(2,1)S(1)}, u32[]{:S(2)}, u32[]{:S(2)}) collective-permute-start(bf16[1040,128]{1,0:T(8,128)(2,1)S(1)} %collective-permute-done.7.refs_2_), channel_id=1, source_target_pairs={{0,4},{4,0},{1,5},{5,1},{2,6},{6,2},{3,7},{7,3},{8,12},{12,8},{9,1... | collective-permute-start | bytes 798728 | tf_op jit(solution)/shard_map/ppermute | solution.py:46
  38.4 1.5 %collective-permute-start.20 = (bf16[1040,128]{1,0:T(8,128)(2,1)S(1)}, bf16[1040,128]{1,0:T(8,128)(2,1)S(1)}, u32[]{:S(2)}, u32[]{:S(2)}) collective-permute-start(bf16[1040,128]{1,0:T(8,128)(2,1)S(1)} %collective-permute-done.9.refs_3_), channel_id=1, source_target_pairs={{0,4},{4,0},{1,5},{5,1},{2,6},{6,2},{3,7},{7,3},{8,12},{12,8},{9,1... | collective-permute-start | bytes 798728 | tf_op jit(solution)/shard_map/ppermute | solution.py:46
  39.5 3.4 %collective-permute-start.15 = (bf16[2080,128]{1,0:T(8,128)(2,1)S(1)}, bf16[2080,128]{1,0:T(8,128)(2,1)S(1)}, u32[]{:S(2)}, u32[]{:S(2)}) collective-permute-start(bf16[2080,128]{1,0:T(8,128)(2,1)S(1)} %collective-permute-done.10.refs_8_), channel_id=1, source_target_pairs={{0,4},{4,0},{1,5},{5,1},{2,6},{6,2},{3,7},{7,3},{8,12},{12,8},{9,1... | collective-permute-start | bytes 1597448 | tf_op jit(solution)/shard_map/ppermute | solution.py:46
  39.9 3.1 %collective-permute-start.16 = (bf16[2080,128]{1,0:T(8,128)(2,1)S(1)}, bf16[2080,128]{1,0:T(8,128)(2,1)S(1)}, u32[]{:S(2)}, u32[]{:S(2)}) collective-permute-start(bf16[2080,128]{1,0:T(8,128)(2,1)S(1)} %collective-permute-done.12.refs_9_), channel_id=1, source_target_pairs={{0,4},{4,0},{1,5},{5,1},{2,6},{6,2},{3,7},{7,3},{8,12},{12,8},{9,1... | collective-permute-start | bytes 1597448 | tf_op jit(solution)/shard_map/ppermute | solution.py:46
  40.3 2.3 %collective-permute-start.21 = (bf16[1040,128]{1,0:T(8,128)(2,1)S(1)}, bf16[1040,128]{1,0:T(8,128)(2,1)S(1)}, u32[]{:S(2)}, u32[]{:S(2)}) collective-permute-start(bf16[1040,128]{1,0:T(8,128)(2,1)S(1)} %collective-permute-done.11.refs_4_), channel_id=1, source_target_pairs={{0,4},{4,0},{1,5},{5,1},{2,6},{6,2},{3,7},{7,3},{8,12},{12,8},{9,1... | collective-permute-start | bytes 798728 | tf_op jit(solution)/shard_map/ppermute | solution.py:46
  40.4 2.5 %collective-permute-start.22 = (bf16[1040,128]{1,0:T(8,128)(2,1)S(1)}, bf16[1040,128]{1,0:T(8,128)(2,1)S(1)}, u32[]{:S(2)}, u32[]{:S(2)}) collective-permute-start(bf16[1040,128]{1,0:T(8,128)(2,1)S(1)} %collective-permute-done.13.refs_5_), channel_id=1, source_target_pairs={{0,4},{4,0},{1,5},{5,1},{2,6},{6,2},{3,7},{7,3},{8,12},{12,8},{9,1... | collective-permute-start | bytes 798728 | tf_op jit(solution)/shard_map/ppermute | solution.py:46
  43.0 12.1 %copy-start = (s32[2,4,128]{2,1,0:T(4,128)S(1)}, s32[2,4,128]{2,1,0:T(4,128)}, u32[]{:S(2)}) copy-start(s32[2,4,128]{2,1,0:T(4,128)} %mask_ref.1) | copy-start | bytes 12292
  45.4 6.4 %collective-permute-start.23 = (f32[264,128]{1,0:T(8,128)S(1)}, f32[264,128]{1,0:T(8,128)S(1)}, u32[]{:S(2)}, u32[]{:S(2)}) collective-permute-start(f32[264,128]{1,0:T(8,128)S(1)} %get-tuple-element.20), channel_id=1, source_target_pairs={{0,2},{1,3},{2,0},{3,1},{4,6},{5,7},{6,4},{7,5},{8,10},{9,11},{10,... | collective-permute-start | bytes 405512 | tf_op jit(solution)/shard_map/ppermute | solution.py:220
  48.3 6.8 %collective-permute-start.24 = (f32[264,128]{1,0:T(8,128)S(1)}, f32[264,128]{1,0:T(8,128)S(1)}, u32[]{:S(2)}, u32[]{:S(2)}) collective-permute-start(f32[264,128]{1,0:T(8,128)S(1)} %get-tuple-element.21), channel_id=1, source_target_pairs={{0,1},{1,2},{2,3},{3,0},{4,5},{5,6},{6,7},{7,4},{8,9},{9,10},{10,1... | collective-permute-start | bytes 405512 | tf_op jit(solution)/shard_map/ppermute | solution.py:220
  48.8 6.4 %collective-permute-start.25 = (f32[264,128]{1,0:T(8,128)S(1)}, f32[264,128]{1,0:T(8,128)S(1)}, u32[]{:S(2)}, u32[]{:S(2)}) collective-permute-start(f32[264,128]{1,0:T(8,128)S(1)} %get-tuple-element.22), channel_id=1, source_target_pairs={{0,3},{1,0},{2,1},{3,2},{4,7},{5,4},{6,5},{7,6},{8,11},{9,8},{10,9... | collective-permute-start | bytes 405512 | tf_op jit(solution)/shard_map/ppermute | solution.py:220
